TPU v7x, 512 devices: a whole 4x8x8 slice. The times are simulated.
512 devices in a mesh: sample: 8 (over y_lo, core), row: 8 (over y_hi, x), col: 8 (over z).
Axes of the slice: x: 4, y: 8 (y_hi: 2, y_lo: 4; y = y_hi * 4 + y_lo), z: 8, core: 2. Of those that a mesh axis runs over, the one named last changes fastest.
Arguments:
- images: bfloat16 [8, 192, 192, 256], P('sample', 'row', 'col'), may hold values from -6 to 6
- w_expand: bfloat16 [256, 1024], replicated, may hold values from -0.375 to 0.375
- w_depth: bfloat16 [3, 3, 1024], replicated, may hold values from -2 to 2
- w_short: bfloat16 [256, 512], replicated, may hold values from -0.375 to 0.375
- w_proj: bfloat16 [1024, 512], P('sample'), may hold values from -0.1875 to 0.1875
- w_qkv: bfloat16 [512, 768], P('sample'), may hold values from -0.25 to 0.25
- w_out: bfloat16 [256, 512], P('sample'), may hold values from -0.375 to 0.375
- cotangent: bfloat16 [8, 96, 96, 512], P('sample', 'row', 'col'), may hold values from -6 to 6
Outputs:
- grad_image: bfloat16 [8, 192, 192, 256], P('sample', 'row', 'col')
- grad_expand: float32 [256, 1024], replicated
- grad_depth: float32 [3, 3, 1024], replicated
- grad_short: float32 [256, 512], replicated
- grad_proj: float32 [1024, 512], P('sample')
- grad_qkv: float32 [512, 768], P('sample')
- grad_out: float32 [256, 512], P('sample')
All inputs are finite; a program needn't handle non-finite values.
Results may differ from a plain program's by a relative error of at most 0.02.
Values may be sent and summed in bfloat16 or wider, within the bound.
No kernel may reach another device: no remote copies, remote signals or barrier semaphores. Data moves between devices by JAX's collectives and lax.ppermute only.
A program may use at most 64 MiB of HBM per device.

v0:
```python
import math

import jax
import jax.numpy as jnp
from jax import lax
from jax.sharding import PartitionSpec as P

HEADS = 8


norm_epsilon = 1e-05
tanh_coeff = 0.7978845608028654
cubic_coeff = 0.044715


def shifted(block, axis, distance):
    devices = range(lax.axis_size(axis))
    route = [(i - distance, i) for i in devices if i - distance in devices]
    return lax.ppermute(block, axis, route)


def gelu_tanh(values):
    return (
        0.5
        * values
        * (1.0 + jnp.tanh(tanh_coeff * (values + cubic_coeff * values * values * values)))
    )


def gelu_slope(values):
    inner = jnp.tanh(tanh_coeff * (values + cubic_coeff * values * values * values))
    return 0.5 * (1.0 + inner) + 0.5 * values * (1.0 - inner * inner) * tanh_coeff * (
        1.0 + 3.0 * cubic_coeff * values * values
    )


def apply_matrix(activations, matrix):
    return lax.dot_general(
        activations,
        matrix,
        (((activations.ndim - 1,), (0,)), ((), ())),
        preferred_element_type=jnp.float32,
    )


def apply_transpose(activations, matrix):
    return lax.dot_general(
        activations,
        matrix,
        (((activations.ndim - 1,), (1,)), ((), ())),
        preferred_element_type=jnp.float32,
    )


def outer_sum(left_side, right_side):
    left_flat = left_side.reshape(-1, left_side.shape[-1])
    right_flat = right_side.reshape(-1, right_side.shape[-1])
    return lax.dot_general(
        left_flat, right_flat, (((0,), (0,)), ((), ())), preferred_element_type=jnp.float32
    )


def batched(form, left_side, right_side):
    return jnp.einsum(form, left_side, right_side, preferred_element_type=jnp.float32)


def depthwise(extended, filters, out_rows, out_cols):
    running = jnp.zeros((extended.shape[0], out_rows, out_cols, extended.shape[3]), jnp.float32)
    for row_tap in range(3):
        for col_tap in range(3):
            window = extended[
                :,
                row_tap : row_tap + 2 * out_rows - 1 : 2,
                col_tap : col_tap + 2 * out_cols - 1 : 2,
                :,
            ]
            running = running + window.astype(jnp.float32) * filters[row_tap, col_tap].astype(
                jnp.float32
            )
    return running


def depthwise_filter_grad(extended, d_conv):
    out_rows = d_conv.shape[1]
    out_cols = d_conv.shape[2]
    tap_rows = []
    for row_tap in range(3):
        taps = []
        for col_tap in range(3):
            window = extended[
                :,
                row_tap : row_tap + 2 * out_rows - 1 : 2,
                col_tap : col_tap + 2 * out_cols - 1 : 2,
                :,
            ]
            taps.append(
                jnp.sum(window.astype(jnp.float32) * d_conv.astype(jnp.float32), axis=(0, 1, 2))
            )
        tap_rows.append(jnp.stack(taps))
    return jnp.stack(tap_rows)


def weave(first, second, axis):
    extra = [(0, 0)] * second.ndim
    extra[axis] = (0, first.shape[axis] - second.shape[axis])
    second = jnp.pad(second, extra)
    stacked = jnp.stack([first, second], axis=axis + 1)
    shape = list(first.shape)
    shape[axis] = 2 * first.shape[axis]
    merged = stacked.reshape(shape)
    return lax.slice_in_dim(
        merged, 0, first.shape[axis] + second.shape[axis] - extra[axis][1], axis=axis
    )


def depthwise_back(d_conv, filters):
    out_rows = d_conv.shape[1]
    out_cols = d_conv.shape[2]
    padded = jnp.pad(d_conv.astype(jnp.float32), ((0, 0), (1, 1), (1, 1), (0, 0)))
    row_taps = (((0, 1, out_rows + 2), (2, 0, out_rows + 1)), ((1, 1, out_rows + 1),))
    col_taps = (((0, 1, out_cols + 2), (2, 0, out_cols + 1)), ((1, 1, out_cols + 1),))
    parity_rows = []
    for row_group in row_taps:
        blocks = []
        for col_group in col_taps:
            running = None
            for row_tap, row_lo, row_hi in row_group:
                for col_tap, col_lo, col_hi in col_group:
                    term = padded[:, row_lo:row_hi, col_lo:col_hi] * filters[
                        row_tap, col_tap
                    ].astype(jnp.float32)
                    running = term if running is None else running + term
            blocks.append(running)
        parity_rows.append(weave(blocks[0], blocks[1], 2))
    return weave(parity_rows[0], parity_rows[1], 1)


def pool_cells(images):
    shaped = images.astype(jnp.float32).reshape(
        images.shape[0], images.shape[1] // 2, 2, images.shape[2] // 2, 2, images.shape[3]
    )
    return jnp.mean(shaped, axis=(2, 4)).astype(jnp.bfloat16)


def unpool_cells(d_pooled):
    return jnp.repeat(jnp.repeat(d_pooled, 2, axis=1), 2, axis=2) * 0.25


def layer_norm(section_out):
    widened = section_out.astype(jnp.float32)
    centred = widened - jnp.mean(widened, axis=-1, keepdims=True)
    inv_std = lax.rsqrt(jnp.mean(centred * centred, axis=-1, keepdims=True) + norm_epsilon)
    return (centred * inv_std, inv_std)


def layer_norm_back(d_normed, normalized, inv_std):
    return inv_std * (
        d_normed
        - jnp.mean(d_normed, axis=-1, keepdims=True)
        - normalized * jnp.mean(d_normed * normalized, axis=-1, keepdims=True)
    )


def split_heads(grouped, head_count):
    batch, slots, width = grouped.shape
    head_size = width // 3 // head_count
    pieces = grouped.reshape(batch, slots, 3, head_count, head_size)
    return (pieces[:, :, 0], pieces[:, :, 1], pieces[:, :, 2], head_size)


def attend(grouped, key_mask, head_count):
    query_part, key_part, value_part, head_size = split_heads(grouped, head_count)
    scores = batched("bqhd,bkhd->bhqk", query_part, key_part) / math.sqrt(head_size)
    raised = jnp.exp(scores) * key_mask
    weights32 = raised / jnp.sum(raised, axis=-1, keepdims=True)
    weights = weights32.astype(jnp.bfloat16)
    mixture = batched("bhqk,bkhd->bqhd", weights, value_part).astype(jnp.bfloat16)
    return (mixture.reshape(grouped.shape[0], grouped.shape[1], -1), weights32, weights)


def attend_back(grouped, weights32, weights, d_mixture, head_count):
    query_part, key_part, value_part, head_size = split_heads(grouped, head_count)
    d_heads = d_mixture.reshape(grouped.shape[0], grouped.shape[1], head_count, head_size)
    d_weights = batched("bqhd,bkhd->bhqk", d_heads, value_part)
    d_values = batched("bhqk,bqhd->bkhd", weights, d_heads)
    d_scores = (
        weights32 * (d_weights - jnp.sum(weights32 * d_weights, axis=-1, keepdims=True))
    ).astype(jnp.bfloat16)
    d_queries = batched("bhqk,bkhd->bqhd", d_scores, key_part) / math.sqrt(head_size)
    d_keys = batched("bhqk,bqhd->bkhd", d_scores, query_part) / math.sqrt(head_size)
    stacked = jnp.stack([d_queries, d_keys, d_values], axis=2).astype(jnp.bfloat16)
    return stacked.reshape(grouped.shape)


def slot_rows(out_count, part_count, my_index):
    slot_depth = (out_count + part_count - 1) // part_count
    depth_ids = jnp.arange(slot_depth, dtype=jnp.int32)[:, None]
    part_ids = jnp.arange(part_count, dtype=jnp.int32)[None, :]
    local_rows = (part_ids - out_count * my_index) % part_count + part_count * depth_ids
    return local_rows.reshape(-1)


def slot_valid(out_count, part_count, my_index):
    slot_depth = (out_count + part_count - 1) // part_count
    source_ids = jnp.arange(part_count, dtype=jnp.int32)[:, None]
    depth_ids = jnp.arange(slot_depth, dtype=jnp.int32)[None, :]
    local_rows = (my_index - out_count * source_ids) % part_count + part_count * depth_ids
    return (local_rows < out_count).astype(jnp.float32).reshape(-1)


def home_rows(out_count, part_count, my_index):
    rows_here = jnp.arange(out_count, dtype=jnp.int32)
    return rows_here // part_count * part_count + (rows_here + out_count * my_index) % part_count


def regroup(tokens):
    out_count = tokens.shape[1]
    part_rows = lax.axis_size("row")
    part_cols = lax.axis_size("col")
    depth_rows = (out_count + part_rows - 1) // part_rows
    depth_cols = (out_count + part_cols - 1) // part_cols
    padded = jnp.pad(
        tokens,
        (
            (0, 0),
            (0, depth_rows * part_rows - out_count),
            (0, depth_cols * part_cols - out_count),
            (0, 0),
        ),
    )
    picked = jnp.take(padded, slot_rows(out_count, part_rows, lax.axis_index("row")), axis=1)
    picked = jnp.take(picked, slot_rows(out_count, part_cols, lax.axis_index("col")), axis=2)
    picked = picked.reshape(
        tokens.shape[0], depth_rows, part_rows, depth_cols, part_cols, tokens.shape[3]
    )
    moved = lax.all_to_all(
        lax.all_to_all(picked, "row", split_axis=2, concat_axis=1, tiled=True),
        "col",
        split_axis=4,
        concat_axis=3,
        tiled=True,
    )
    return moved.reshape(
        tokens.shape[0], depth_rows * part_rows * depth_cols * part_cols, tokens.shape[3]
    )


def ungroup(slotted, out_count):
    part_rows = lax.axis_size("row")
    part_cols = lax.axis_size("col")
    depth_rows = (out_count + part_rows - 1) // part_rows
    depth_cols = (out_count + part_cols - 1) // part_cols
    shaped = slotted.reshape(
        slotted.shape[0], depth_rows * part_rows, 1, depth_cols * part_cols, 1, slotted.shape[2]
    )
    moved = lax.all_to_all(
        lax.all_to_all(shaped, "row", split_axis=1, concat_axis=2, tiled=True),
        "col",
        split_axis=3,
        concat_axis=4,
        tiled=True,
    )
    moved = moved.reshape(
        slotted.shape[0], depth_rows * part_rows, depth_cols * part_cols, slotted.shape[2]
    )
    placed = jnp.take(moved, home_rows(out_count, part_rows, lax.axis_index("row")), axis=1)
    return jnp.take(placed, home_rows(out_count, part_cols, lax.axis_index("col")), axis=2)


def on_device(images, w_expand, w_depth, w_short, w_proj, w_qkv, w_out, cotangent):
    proj_full, qkv_full, out_full = (
        lax.all_gather(w_proj, "sample", axis=0, tiled=True),
        lax.all_gather(w_qkv, "sample", axis=0, tiled=True),
        lax.all_gather(w_out, "sample", axis=0, tiled=True),
    )
    out_count = images.shape[1] // 2
    pre_act = apply_matrix(images, w_expand)
    expanded = gelu_tanh(pre_act).astype(jnp.bfloat16)
    top_rim = shifted(expanded[:, -1:], "row", 1)
    taller = jnp.concatenate([top_rim, expanded], axis=1)
    left_rim = shifted(taller[:, :, -1:], "col", 1)
    extended = jnp.concatenate([left_rim, taller], axis=2)
    conv_out = depthwise(extended, w_depth, out_count, out_count)
    activated = gelu_tanh(conv_out).astype(jnp.bfloat16)
    pooled = pool_cells(images)
    section_out = (apply_matrix(activated, proj_full) + apply_matrix(pooled, w_short)).astype(
        jnp.bfloat16
    )
    normalized, inv_std = layer_norm(section_out)
    normed = normalized.astype(jnp.bfloat16)
    packed = apply_matrix(normed, qkv_full).astype(jnp.bfloat16)
    grouped = regroup(packed)
    valid_rows = slot_valid(out_count, lax.axis_size("row"), lax.axis_index("row"))
    valid_cols = slot_valid(out_count, lax.axis_size("col"), lax.axis_index("col"))
    key_mask = (valid_rows[:, None] * valid_cols[None, :]).reshape(-1)
    mixed_slots, weights32, weights = attend(grouped, key_mask, HEADS)
    mixture = ungroup(mixed_slots, out_count)
    part_out = outer_sum(mixture, cotangent)
    d_mixture = apply_transpose(cotangent, out_full).astype(jnp.bfloat16)
    d_slots = attend_back(grouped, weights32, weights, regroup(d_mixture), HEADS)
    d_packed = ungroup(d_slots, out_count)
    part_qkv = outer_sum(normed, d_packed)
    d_normed = apply_transpose(d_packed, qkv_full)
    d_section = (
        cotangent.astype(jnp.float32) + layer_norm_back(d_normed, normalized, inv_std)
    ).astype(jnp.bfloat16)
    part_proj = outer_sum(activated, d_section)
    part_short = outer_sum(pooled, d_section)
    d_activated = apply_transpose(d_section, proj_full)
    d_conv = (d_activated * gelu_slope(conv_out)).astype(jnp.bfloat16)
    part_depth = depthwise_filter_grad(extended, d_conv)
    d_extended = depthwise_back(d_conv, w_depth)
    edge_cols = shifted(d_extended[:, :, :1].astype(jnp.bfloat16), "col", -1).astype(jnp.float32)
    d_extended = d_extended.at[:, :, -1:].add(edge_cols)
    edge_rows = shifted(d_extended[:, :1].astype(jnp.bfloat16), "row", -1).astype(jnp.float32)
    d_extended = d_extended.at[:, -1:].add(edge_rows)
    d_expanded = d_extended[:, 1:, 1:]
    d_pre = (d_expanded * gelu_slope(pre_act)).astype(jnp.bfloat16)
    part_expand = outer_sum(images, d_pre)
    d_pooled = apply_transpose(d_section, w_short)
    grad_image = (apply_transpose(d_pre, w_expand) + unpool_cells(d_pooled)).astype(jnp.bfloat16)
    grad_scale = 1.0 / math.sqrt(
        images.shape[0]
        * lax.axis_size("sample")
        * out_count
        * lax.axis_size("row")
        * out_count
        * lax.axis_size("col")
    )
    sum_expand, sum_depth, sum_short = lax.psum(
        (part_expand, part_depth, part_short), ("sample", "row", "col")
    )
    flat_parts = (part_proj.reshape(-1), part_qkv.reshape(-1), part_out.reshape(-1))
    pieces = (
        lax.psum_scatter(
            flat_parts[0].astype(jnp.bfloat16), "sample", scatter_dimension=0, tiled=True
        ).astype(jnp.float32),
        lax.psum_scatter(
            flat_parts[1].astype(jnp.bfloat16), "sample", scatter_dimension=0, tiled=True
        ).astype(jnp.float32),
        lax.psum_scatter(
            flat_parts[2].astype(jnp.bfloat16), "sample", scatter_dimension=0, tiled=True
        ).astype(jnp.float32),
    )
    pieces = lax.psum((pieces[0], pieces[1], pieces[2]), ("row", "col"))
    grad_proj = pieces[0].reshape(-1, part_proj.shape[1]) * grad_scale
    grad_qkv = pieces[1].reshape(-1, part_qkv.shape[1]) * grad_scale
    grad_out = pieces[2].reshape(-1, part_out.shape[1]) * grad_scale
    return (
        grad_image,
        sum_expand * grad_scale,
        sum_depth * grad_scale,
        sum_short * grad_scale,
        grad_proj,
        grad_qkv,
        grad_out,
    )


def solution(mesh):
    placed = (
        P("sample", "row", "col", None),
        P(),
        P(),
        P(),
        P("sample", None),
        P("sample", None),
        P("sample", None),
        P("sample", "row", "col", None),
    )
    return jax.shard_map(
        on_device,
        mesh=mesh,
        in_specs=placed,
        out_specs=(
            P("sample", "row", "col", None),
            P(),
            P(),
            P(),
            P("sample", None),
            P("sample", None),
            P("sample", None),
        ),
        check_vma=False,
    )
```

profile of v0, /device:TPU:8, one launch (start us, length us, event | category | flops | bytes accessed | tf_op | source)
XLA Modules:
  0.0 1594.8 jit_solution(5015605287517613504)
XLA Ops:
  12.5 3.4 collective-permute-start
  16.3 14.4 all_gather.11
  33.1 6.6 all-to-all-start.2
  39.7 19.8 %all_gather.10 = bf16[512,768]{1,0:T(8,128)(2,1)S(1)} all-gather(bf16[64,768]{1,0:T(8,128)(2,1)S(1)} %copy-done.34), channel_id=1, replica_groups=mesh['sample'=8,'row'=8,'col'=8] {'sample'}, dimensions={0}, use_global_device_ids=true | all-gather | bytes 884736 | tf_op jit(solution)/shard_map/all_gather | solution.py:273
  60.8 4.0 slice.207
  64.8 3.9 slice.211
  68.7 3.9 slice.213
  79.9 7.1 slice.199
  87.0 7.1 slice.201
  95.9 5.7 slice.197
  101.6 5.8 slice.203
  107.5 7.1 slice.209
  123.2 10.3 all-to-all-start
  135.2 13.9 all-to-all-done
  149.2 9.6 all-to-all-start.3
  159.8 8.0 all-to-all-done.3
  167.9 4.0 all-to-all-start.1
  174.2 9.5 all-to-all-done.1
  198.5 3.6 all-to-all-start.6
  208.2 4.5 all-to-all-done.6
  212.6 5.3 all-to-all-start.4
  218.6 11.6 all-to-all-done.4
  230.3 3.4 all-to-all-start.7
  234.7 8.0 all-to-all-done.7
  242.7 3.5 all-to-all-start.5
  252.1 5.8 all-to-all-done.5
  274.8 92.2 %psum.43 = f32[3,3,1024]{2,1,0:T(4,128)S(1)} all-reduce(f32[3,3,1024]{2,1,0:T(4,128)S(1)} %pad_maximum_fusion.5), channel_id=1, replica_groups=mesh['sample'=8,'row'=8,'col'=8] {'sample','row','col'}, use_global_device_ids=true, to_apply=%region_17.18 | all-reduce | flops 9216 | bytes 73728 | tf_op jit(solution)/shard_map/psum | solution.py:330
  373.1 3.1 pad_maximum_fusion
  383.7 3.3 scatter-add.6
  402.6 56.2 %all-reduce.20.cloned.1.call-done = (bf16[524288]{0:T(1024)(128)(2,1)}, bf16[393216]{0:T(1024)(128)(2,1)}, bf16[131072]{0:T(1024)(128)(2,1)}) async-done(((bf16[524288]{0:T(1024)(128)(2,1)}, bf16[393216]{0:T(1024)(128)(2,1)}, bf16[131072]{0:T(1024)(128)(2,1)}), (bf16[524288]{0:T(1024)(128)(2,1)}, bf16[393216]{0:T(1024)(128)(2,1)}, bf16[131072]{0:T(1024)(128)(2,1)})) %all-reduce.20.cloned.1.call-update) | async-done | bytes 2097168
  463.5 279.9 %all-reduce.16.cloned.1.call-done = (f32[256,1024]{0,1:T(8,128)}, f32[256,512]{1,0:T(8,128)}) async-done(((f32[256,1024]{0,1:T(8,128)}, f32[256,512]{1,0:T(8,128)}), (f32[256,1024]{0,1:T(8,128)}, f32[256,512]{1,0:T(8,128)})) %all-reduce.16.cloned.1.call-update) | async-done | bytes 1572880 | tf_op jit(solution)/shard_map/psum | solution.py:330
  747.0 836.2 %all-reduce.18.cloned.1.call-done = (f32[65536]{0:T(1024)}, f32[49152]{0:T(1024)}, f32[16384]{0:T(1024)}) async-done(((f32[65536]{0:T(1024)}, f32[49152]{0:T(1024)}, f32[16384]{0:T(1024)}), (f32[65536]{0:T(1024)}, f32[49152]{0:T(1024)}, f32[16384]{0:T(1024)})) %all-reduce.18.cloned.1.call-update) | async-done | bytes 524304 | tf_op jit(solution)/shard_map/psum | solution.py:345
  (300 shorter events, 116.8 us)
Async XLA Ops:
  7.2 110.6 %all-gather.2.cloned.1.call-start = ((), (), s32[]{:S(2)}) async-start(), calls=%async_computation.8 | async-start | bytes 1179648 | tf_op jit(solution)/shard_map/all_gather | solution.py:272
  11.8 27.9 %copy-start.34 = (bf16[64,768]{1,0:T(8,128)(2,1)S(1)}, bf16[64,768]{1,0:T(8,128)(2,1)}, u32[]{:S(2)}) copy-start(bf16[64,768]{1,0:T(8,128)(2,1)} %param.17) | copy-start | bytes 294916
  11.8 47.7 %copy-start.35 = (bf16[3,3,1024]{2,1,0:T(4,128)(2,1)S(1)}, bf16[3,3,1024]{2,1,0:T(4,128)(2,1)}, u32[]{:S(2)}) copy-start(bf16[3,3,1024]{2,1,0:T(4,128)(2,1)} %param.14) | copy-start | bytes 55300
  12.5 62.5 %collective-permute-start = (bf16[1,1,24,1024]{3,2,1,0:T(8,128)(2,1)}, bf16[1,1,24,1024]{3,2,1,0:T(8,128)(2,1)S(1)}, u32[]{:S(2)}, u32[]{:S(2)}) collective-permute-start(bf16[1,1,24,1024]{3,2,1,0:T(8,128)(2,1)} %slice.250), channel_id=1, source_target_pairs={{0,8},{8,16},{16,24},{24,32},{32,40},{40,48},{48,56},{1,9},{9,17},... | collective-permute-start | bytes 147464 | tf_op jit(solution)/shard_map/ppermute | solution.py:19
  33.1 90.1 %all-to-all-start.2 = ((bf16[1,2,8,2,8,256]{5,4,3,1,0,2:T(8,128)(2,1)}), bf16[1,2,8,2,8,256]{5,4,3,1,0,2:T(8,128)(2,1)}, u32[]{:S(2)}, u32[]{:S(2)}) async-start(bf16[1,2,8,2,8,256]{5,4,3,1,0,2:T(8,128)(2,1)} %copy_select_fusion.1), calls=%async_computation.2 | async-start | bytes 262144 | tf_op jit(solution)/shard_map/all_to_all | solution.py:237
  59.6 60.7 %copy-start.3 = (bf16[512,768]{1,0:T(8,128)(2,1)}, bf16[512,768]{1,0:T(8,128)(2,1)S(1)}, u32[]{:S(2)}) copy-start(bf16[512,768]{1,0:T(8,128)(2,1)S(1)} %all_gather.10) | copy-start | bytes 2359300
  60.2 54.3 %copy-start.36 = (f32[1,1,1024]{2,1,0:T(1,128)}, f32[1,1,1024]{2,1,0:T(1,128)S(1)}, u32[]{:S(2)}) copy-start(f32[1,1,1024]{2,1,0:T(1,128)S(1)} %get-tuple-element.91) | copy-start | bytes 12292
  60.2 54.3 %copy-start.38 = (f32[1,1,1024]{2,1,0:T(1,128)}, f32[1,1,1024]{2,1,0:T(1,128)S(1)}, u32[]{:S(2)}) copy-start(f32[1,1,1024]{2,1,0:T(1,128)S(1)} %get-tuple-element.93) | copy-start | bytes 12292
  60.2 54.3 %copy-start.40 = (f32[1,1,1024]{2,1,0:T(1,128)}, f32[1,1,1024]{2,1,0:T(1,128)S(1)}, u32[]{:S(2)}) copy-start(f32[1,1,1024]{2,1,0:T(1,128)S(1)} %get-tuple-element.89) | copy-start | bytes 12292
  60.2 54.3 %copy-start.42 = (f32[1,1,1024]{2,1,0:T(1,128)}, f32[1,1,1024]{2,1,0:T(1,128)S(1)}, u32[]{:S(2)}) copy-start(f32[1,1,1024]{2,1,0:T(1,128)S(1)} %get-tuple-element.90) | copy-start | bytes 12292
  60.2 54.4 %copy-start.44 = (f32[1,1,1024]{2,1,0:T(1,128)}, f32[1,1,1024]{2,1,0:T(1,128)S(1)}, u32[]{:S(2)}) copy-start(f32[1,1,1024]{2,1,0:T(1,128)S(1)} %get-tuple-element.94) | copy-start | bytes 12292
  60.3 54.4 %copy-start.46 = (f32[1,1,1024]{2,1,0:T(1,128)}, f32[1,1,1024]{2,1,0:T(1,128)S(1)}, u32[]{:S(2)}) copy-start(f32[1,1,1024]{2,1,0:T(1,128)S(1)} %get-tuple-element.96) | copy-start | bytes 12292
  60.3 54.4 %copy-start.48 = (f32[1,1,1024]{2,1,0:T(1,128)}, f32[1,1,1024]{2,1,0:T(1,128)S(1)}, u32[]{:S(2)}) copy-start(f32[1,1,1024]{2,1,0:T(1,128)S(1)} %get-tuple-element.95) | copy-start | bytes 12292
  60.3 54.4 %copy-start.50 = (f32[1,1,1024]{2,1,0:T(1,128)}, f32[1,1,1024]{2,1,0:T(1,128)S(1)}, u32[]{:S(2)}) copy-start(f32[1,1,1024]{2,1,0:T(1,128)S(1)} %get-tuple-element.97) | copy-start | bytes 12292
  60.8 53.8 %copy-start.5 = (bf16[1,12,12,1024]{3,2,1,0:T(8,128)(2,1)}, bf16[1,12,12,1024]{3,2,1,0:T(8,128)(2,1)S(1)}, u32[]{:S(2)}) copy-start(bf16[1,12,12,1024]{3,2,1,0:T(8,128)(2,1)S(1)} %slice.205) | copy-start | bytes 884740
  75.8 18.2 %collective-permute-start.1 = (bf16[1,25,1,1024]{3,2,1,0:T(2,128)(2,1)}, bf16[1,25,1,1024]{3,2,1,0:T(2,128)(2,1)S(1)}, u32[]{:S(2)}, u32[]{:S(2)}) collective-permute-start(bf16[1,25,1,1024]{3,2,1,0:T(2,128)(2,1)} %fusion.105), channel_id=1, source_target_pairs={{0,1},{1,2},{2,3},{3,4},{4,5},{5,6},{6,7},{8,9},{9,10},{10,11},{11... | collective-permute-start | bytes 153608 | tf_op jit(solution)/shard_map/ppermute | solution.py:19
  94.1 20.6 %copy-start.7 = (bf16[1,12,12,1024]{3,2,1,0:T(8,128)(2,1)S(1)}, bf16[1,12,12,1024]{3,2,1,0:T(8,128)(2,1)}, u32[]{:S(2)}) copy-start(bf16[1,12,12,1024]{3,2,1,0:T(8,128)(2,1)} %slice.207) | copy-start | bytes 884740
  94.1 20.6 %copy-start.54 = (f32[1,1,1024]{2,1,0:T(1,128)S(1)}, f32[1,1,1024]{2,1,0:T(1,128)}, u32[]{:S(2)}) copy-start(f32[1,1,1024]{2,1,0:T(1,128)} %get-tuple-element.92) | copy-start | bytes 12292
  121.6 50.3 %copy-start.60 = (s32[2]{0:T(128)S(1)}, s32[2]{0:T(128)}, u32[]{:S(2)}) copy-start(s32[2]{0:T(128)} %copy-done.59) | copy-start | bytes 28
  123.2 25.9 %all-to-all-start = ((bf16[1,2,8,2,8,768]{5,4,3,1,0,2:T(8,128)(2,1)}), bf16[1,2,8,2,8,768]{5,4,3,1,0,2:T(8,128)(2,1)S(1)}, u32[]{:S(2)}, u32[]{:S(2)}) async-start(bf16[1,2,8,2,8,768]{5,4,3,1,0,2:T(8,128)(2,1)} %copy_select_fusion), calls=%async_computation | async-start | bytes 786432 | tf_op jit(solution)/shard_map/all_to_all | solution.py:237
  149.2 18.7 %all-to-all-start.3 = ((bf16[1,16,1,2,8,256]{5,3,1,2,0,4:T(2,128)(2,1)}), bf16[1,16,1,2,8,256]{5,3,1,2,0,4:T(2,128)(2,1)S(1)}, u32[]{:S(2)}, u32[]{:S(2)}) async-start(bf16[1,16,1,2,8,256]{5,3,1,2,0,4:T(2,128)(2,1)} %copy.125), calls=%async_computation.3 | async-start | bytes 262144 | tf_op jit(solution)/shard_map/all_to_all | solution.py:236
  167.9 15.8 all-to-all-start.1
  198.5 14.1 all-to-all-start.6
  212.6 38.3 %copy-start.26 = (bf16[1,12,12,512]{3,2,1,0:T(8,128)(2,1)S(1)}, bf16[1,12,12,512]{3,2,1,0:T(8,128)(2,1)}, u32[]{:S(2)}) copy-start(bf16[1,12,12,512]{3,2,1,0:T(8,128)(2,1)} %param.19) | copy-start | bytes 442372
  212.6 17.6 %all-to-all-start.4 = ((bf16[1,16,1,16,1,768]{5,3,4,2,0,1:T(8,128)(2,1)}), bf16[1,16,1,16,1,768]{5,3,4,2,0,1:T(8,128)(2,1)S(1)}, u32[]{:S(2)}, u32[]{:S(2)}) async-start(bf16[1,16,1,16,1,768]{5,3,4,2,0,1:T(8,128)(2,1)} %bitcast.54), calls=%async_computation.4 | async-start | bytes 786432 | tf_op jit(solution)/shard_map/all_to_all | solution.py:257
  230.3 12.4 all-to-all-start.7
  242.7 15.3 all-to-all-start.5
  246.1 212.8 %all-reduce.20.cloned.1.call-start = ((), (), s32[]{:S(2)}) async-start(), calls=%async_computation.11 | async-start | bytes 4194304
  376.3 6.4 collective-permute-start.2
  377.6 365.8 %all-reduce.16.cloned.1.call-start = ((), (), s32[]{:S(2)}) async-start(), calls=%async_computation.9 | async-start | bytes 3145728 | tf_op jit(solution)/shard_map/psum | solution.py:330
  388.6 6.4 collective-permute-start.3
  402.6 1180.6 %all-reduce.18.cloned.1.call-start = ((), (), s32[]{:S(2)}) async-start(), calls=%async_computation.10 | async-start | bytes 1048576 | tf_op jit(solution)/shard_map/psum | solution.py:345
  (50 other events, 210.5 us)
Sparse Core Ops, SparseCore 0:
  16.0 42.6 all-gather.1
  377.8 81.0 all-reduce.19
  464.5 278.8 all-reduce.15
  747.2 835.8 all-reduce.17
where the time goes:
time: 1600 us; the launch traced here: 1590 us
  waiting for transfers between devices  1240 us (78%)
  blocking collectives  126 us (8%)
  local copies, waits for them, and re-layouts  102 us (6%)
  starting transfers between devices  55.7 us (3%)
  other arithmetic  34.6 us (2%)
  matrix products  23.5 us (1%)
  between operations  17.3 us (1%)
    psum x1, waiting for transfers between devices, on_device(): pieces = lax.psum((pieces[0], pieces[1], pieces[2]), ('row', 'col'))  836 us
    psum x1, waiting for transfers between devices, on_device(): lax.psum((part_expand, part_depth, part_short), ('sample', 'row', 'col'))  280 us
    psum x1, blocking collectives, on_device(): lax.psum((part_expand, part_depth, part_short), ('sample', 'row', 'col'))  92.2 us
    unnamed x5, waiting for transfers between devices  56.3 us
    slice x9, local copies, waits for them, and re-layouts, depthwise(): extended[:, row_tap:row_tap + 2 * out_rows - 1:2, col_tap:col_tap + 2 * o...  45.1 us
  transfers between devices with their start and end apart: 16, of which 11 were waited for; matrix products, arithmetic and copies ran while one was open for 7% of the time, Pallas kernels for 0%

commit v1 on v0

v1 whole, which is shorter than its diff:
```python
import math

import jax
import jax.numpy as jnp
from jax import lax
from jax.sharding import Mesh
from jax.sharding import PartitionSpec as P

HEADS = 8
PARTS = 8

SAMPLE = ("ylo", "core")
ROW = ("yhi", "x")
COL = "z"
GRID_AXES = ("yhi", "x", "z")
CHIPS = ("ylo", "yhi", "x", "z")
RING = ("ylo", "yhi")

norm_epsilon = 1e-05
tanh_coeff = 0.7978845608028654
cubic_coeff = 0.044715

bf16 = jnp.bfloat16
f32 = jnp.float32


def gelu_both(values):
    inner = jnp.tanh(tanh_coeff * (values + cubic_coeff * values * values * values))
    value = 0.5 * values * (1.0 + inner)
    slope = 0.5 * (1.0 + inner) + 0.5 * values * (1.0 - inner * inner) * tanh_coeff * (
        1.0 + 3.0 * cubic_coeff * values * values
    )
    return value, slope


def dot(left, right):
    return lax.dot_general(
        left, right, (((left.ndim - 1,), (0,)), ((), ())), preferred_element_type=f32
    )


def dot_t(left, right):
    return lax.dot_general(
        left, right, (((left.ndim - 1,), (1,)), ((), ())), preferred_element_type=f32
    )


def outer_sum(left, right):
    return lax.dot_general(
        left.reshape(-1, left.shape[-1]),
        right.reshape(-1, right.shape[-1]),
        (((0,), (0,)), ((), ())),
        preferred_element_type=f32,
    )


def step_route(count, distance):
    return [(i - distance, i) for i in range(count) if 0 <= i - distance < count]


def diagonal_route(distance):
    return [
        ((r - distance) * PARTS + c - distance, r * PARTS + c)
        for r in range(PARTS)
        for c in range(PARTS)
        if 0 <= r - distance < PARTS and 0 <= c - distance < PARTS
    ]


def rims(edge_row, edge_col, corner, distance):
    return (
        lax.ppermute(edge_row, ROW, step_route(PARTS, distance)),
        lax.ppermute(edge_col, COL, step_route(PARTS, distance)),
        lax.ppermute(corner, GRID_AXES, diagonal_route(distance)),
    )


def around(distance):
    place = [y % 4 * 2 + y // 4 for y in range(8)]
    return [(place[y], place[(y + distance) % 8]) for y in range(8)]


def swap_cores(block):
    return lax.ppermute(block, "core", [(0, 1), (1, 0)])


def exchange(block, axes):
    return lax.all_to_all(block, axes, 0, 0, tiled=True)


def spread(block, axes, count):
    return exchange(jnp.broadcast_to(block[None], (count,) + block.shape), axes)


def gather_weights(w_proj, w_qkv, w_out):
    flat = jnp.concatenate([w.reshape(-1, 128) for w in (w_proj, w_qkv, w_out)], axis=0)
    core = lax.axis_index("core")
    other = swap_cores(flat)
    pair = jnp.where(core == 0, jnp.stack([flat, other]), jnp.stack([other, flat]))
    below = lax.ppermute(pair, RING, around(1))
    above = lax.ppermute(pair, RING, around(7))
    half = pair.shape[1] // 2
    far_a = lax.ppermute(pair[:, :half], RING, around(2))
    far_b = lax.ppermute(pair[:, half:], RING, around(6))
    far = jnp.concatenate([far_a, far_b], axis=1)
    ring = jnp.stack([pair, above, far, below])
    turned = jnp.take(ring, (jnp.arange(4) - lax.axis_index("ylo")) % 4, axis=0)
    shards = turned.reshape((8,) + flat.shape)
    cuts = [w.size // 128 for w in (w_proj, w_qkv, w_out)]
    proj = shards[:, : cuts[0]].reshape(-1, w_proj.shape[1])
    qkv = shards[:, cuts[0] : cuts[0] + cuts[1]].reshape(-1, w_qkv.shape[1])
    out = shards[:, cuts[0] + cuts[1] :].reshape(-1, w_out.shape[1])
    return proj, qkv, out


def to_units(tokens):
    rows = tokens.shape[0]
    moved = tokens.transpose(2, 0, 1, 3)
    padded = jnp.pad(moved, ((0, 0), (0, 0), (0, 4), (0, 0)))
    quads = padded.reshape(HEADS, rows, 2, 2, 4, 128)
    odd = lax.axis_index("z") % 2 == 1
    quads = jnp.where(odd, quads[:, :, :, ::-1], quads)
    pieces = quads.reshape(HEADS, rows, 2, 8, 128).transpose(0, 3, 1, 2, 4)
    got = exchange(pieces.reshape(64, rows * 2, 128), GRID_AXES)
    got = got.reshape(8, 8, rows, 2, 128).transpose(0, 2, 1, 3, 4)
    got = got.reshape(8 * rows, 4, 2, 2, 128)
    high = lax.axis_index("z") >= 4
    second = jnp.where(high, got[:, :, 1, 1], got[:, :, 0, 1])
    first = got[:, :, :, 0].reshape(8 * rows, 8, 128)
    cols = jnp.concatenate([first, second], axis=1)
    return cols.reshape(12, 8, 12, 128).transpose(1, 0, 2, 3).reshape(8, 144, 128)


def from_units(units):
    rows = 12
    cols = units.reshape(8, 12, 12, 128).transpose(1, 0, 2, 3).reshape(8 * rows, 12, 128)
    first = cols[:, :8].reshape(8 * rows, 4, 2, 128)
    second = jnp.broadcast_to(cols[:, 8:, None], (8 * rows, 4, 2, 128))
    sent = jnp.stack([first, second], axis=3).reshape(8, rows, 8, 2, 128)
    sent = sent.transpose(0, 2, 1, 3, 4).reshape(64, rows * 2, 128)
    got = exchange(sent, GRID_AXES).reshape(HEADS, 8, rows, 2, 128)
    got = got.transpose(0, 2, 3, 1, 4).reshape(HEADS, rows, 2, 2, 4, 128)
    odd = lax.axis_index("z") % 2 == 1
    got = jnp.where(odd, got[:, :, :, ::-1], got).reshape(HEADS, rows, 16, 128)
    return got[:, :, :12].transpose(1, 2, 0, 3)


def attention(units):
    query, key, value, d_mix = (units[..., 32 * i : 32 * i + 32] for i in range(4))
    scale = 1.0 / math.sqrt(32)

    def batched(form, left, right):
        return jnp.einsum(form, left, right, preferred_element_type=f32)

    raised = jnp.exp(batched("uqd,ukd->uqk", query, key) * scale)
    weights32 = raised / jnp.sum(raised, axis=-1, keepdims=True)
    weights = weights32.astype(bf16)
    mixture = batched("uqk,ukd->uqd", weights, value)
    d_weights = batched("uqd,ukd->uqk", d_mix, value)
    d_value = batched("uqk,uqd->ukd", weights, d_mix)
    d_scores = (
        weights32 * (d_weights - jnp.sum(weights32 * d_weights, axis=-1, keepdims=True))
    ).astype(bf16)
    d_query = batched("uqk,ukd->uqd", d_scores, key) * scale
    d_key = batched("uqk,uqd->ukd", d_scores, query) * scale
    return jnp.concatenate([d_query, d_key, d_value, mixture], axis=-1).astype(bf16)


def all_sums(part_proj, part_qkv, part_out, part_expand, part_depth, part_short):
    matrix = jnp.concatenate(
        [part.astype(bf16).reshape(8, -1) for part in (part_proj, part_qkv, part_out)], axis=1
    ).reshape(4, 2, 64, 16, 128)
    rest = jnp.concatenate(
        [part.astype(bf16).reshape(-1, 128) for part in (part_expand, part_depth, part_short)]
    )
    rest_rows = rest.shape[0]
    rest = jnp.pad(rest, ((0, 4096 - rest_rows), (0, 0))).reshape(4, 2, 64, 8, 128)
    both = jnp.concatenate([matrix, rest], axis=3)
    core = lax.axis_index("core")
    mine = jnp.where(core == 0, both[:, 0], both[:, 1])
    theirs = jnp.where(core == 0, both[:, 1], both[:, 0])
    pair = (mine.astype(f32) + swap_cores(theirs).astype(f32)).astype(bf16)
    pieces = exchange(pair.reshape(256, 24, 128), CHIPS)
    grad_scale = 1.0 / math.sqrt(8 * 96 * 96)
    total = (jnp.sum(pieces.astype(f32), axis=0) * grad_scale).astype(bf16)
    near = spread(total, GRID_AXES, 64)
    flat = near[:, :16].reshape(-1).astype(f32)
    sizes = [part.size // 8 for part in (part_proj, part_qkv, part_out)]
    grad_proj = flat[: sizes[0]].reshape(-1, part_proj.shape[1])
    grad_qkv = flat[sizes[0] : sizes[0] + sizes[1]].reshape(-1, part_qkv.shape[1])
    grad_out = flat[sizes[0] + sizes[1] :].reshape(-1, part_out.shape[1])
    mine = near[:, 16:].reshape(512, 128)
    other = swap_cores(mine)
    pair = jnp.where(core == 0, jnp.stack([mine, other]), jnp.stack([other, mine]))
    rest = spread(pair, ("ylo",), 4).reshape(4096, 128).astype(f32)
    cut = part_expand.size // 128
    end = cut + part_depth.size // 128
    return (
        rest[:cut].reshape(part_expand.shape),
        rest[cut:end].reshape(part_depth.shape),
        rest[end:rest_rows].reshape(part_short.shape),
        grad_proj,
        grad_qkv,
        grad_out,
    )


def on_device(images, w_expand, w_depth, w_short, w_proj, w_qkv, w_out, cotangent):
    images = images[0]
    cotangent = cotangent[0]
    top, left, corner = rims(images[-1:], images[:, -1:], images[-1:, -1:], 1)
    proj, qkv, out = gather_weights(w_proj, w_qkv, w_out)

    cells = images.reshape(12, 2, 12, 2, 256)
    top_cells = top.reshape(1, 12, 2, 256)
    left_cells = left.reshape(12, 2, 1, 256)
    planes = {
        (0, 0): cells[:, 0, :, 0],
        (0, 1): jnp.concatenate([left_cells[:, 0], cells[:, 0, :, 1]], axis=1),
        (1, 0): jnp.concatenate([top_cells[:, :, 0], cells[:, 1, :, 0]], axis=0),
        (1, 1): jnp.concatenate(
            [
                jnp.concatenate([corner, top_cells[:, :, 1]], axis=1),
                jnp.concatenate([left_cells[:, 1], cells[:, 1, :, 1]], axis=1),
            ],
            axis=0,
        ),
    }
    expanded, slopes = {}, {}
    for place, plane in planes.items():
        value, slope = gelu_both(dot(plane, w_expand))
        expanded[place] = value.astype(bf16)
        slopes[place] = slope[place[0] :, place[1] :]
    taps = w_depth.astype(f32)

    def window(row_tap, col_tap):
        plane = expanded[(row_tap + 1) % 2, (col_tap + 1) % 2]
        row, col = row_tap // 2, col_tap // 2
        return plane[row : row + 12, col : col + 12].astype(f32)

    conv_out = sum(window(a, b) * taps[a, b] for a in range(3) for b in range(3))
    value, conv_slope = gelu_both(conv_out)
    activated = value.astype(bf16)
    wide = cells.astype(f32)
    pooled = (
        (wide[:, 0, :, 0] + wide[:, 0, :, 1] + wide[:, 1, :, 0] + wide[:, 1, :, 1]) * 0.25
    ).astype(bf16)

    section_out = (dot(activated, proj) + dot(pooled, w_short)).astype(bf16).astype(f32)
    centred = section_out - jnp.mean(section_out, axis=-1, keepdims=True)
    inv_std = lax.rsqrt(jnp.mean(centred * centred, axis=-1, keepdims=True) + norm_epsilon)
    normalized = centred * inv_std
    normed = normalized.astype(bf16)
    packed = dot(normed, qkv).astype(bf16).reshape(12, 12, 3, HEADS, 32)
    d_mixture = dot_t(cotangent, out).astype(bf16).reshape(12, 12, 1, HEADS, 32)
    tokens = jnp.concatenate([packed, d_mixture], axis=2).transpose(0, 1, 3, 2, 4)
    results = from_units(attention(to_units(tokens.reshape(12, 12, HEADS, 128))))
    results = results.reshape(12, 12, HEADS, 4, 32).transpose(0, 1, 3, 2, 4)
    d_packed = results[:, :, :3].reshape(12, 12, 768)
    mixture = results[:, :, 3].reshape(12, 12, 256)

    part_out = outer_sum(mixture, cotangent)
    part_qkv = outer_sum(normed, d_packed)
    d_normed = dot_t(d_packed, qkv)
    d_section = (
        cotangent.astype(f32)
        + inv_std
        * (
            d_normed
            - jnp.mean(d_normed, axis=-1, keepdims=True)
            - normalized * jnp.mean(d_normed * normalized, axis=-1, keepdims=True)
        )
    ).astype(bf16)
    part_proj = outer_sum(activated, d_section)
    part_short = outer_sum(pooled, d_section)
    d_conv = (dot_t(d_section, proj) * conv_slope).astype(bf16)
    below, right, beyond = rims(d_conv[:1], d_conv[:, :1], d_conv[:1, :1], -1)
    d_wide = jnp.concatenate(
        [
            jnp.concatenate([d_conv, right], axis=1),
            jnp.concatenate([below, beyond], axis=1),
        ],
        axis=0,
    ).astype(f32)
    here = d_conv.astype(f32)
    part_depth = jnp.stack(
        [
            jnp.stack([jnp.sum(window(a, b) * here, axis=(0, 1)) for b in range(3)])
            for a in range(3)
        ]
    )
    d_pooled = dot_t(d_section, w_short) * 0.25
    row_terms = {0: ((1, 0),), 1: ((2, 0), (0, 1))}
    part_expand = 0.0
    grads = []
    for row in range(2):
        in_row = []
        for col in range(2):
            d_cells = sum(
                d_wide[i : i + 12, j : j + 12] * taps[a, b]
                for a, i in row_terms[row]
                for b, j in row_terms[col]
            )
            d_pre = (d_cells * slopes[row, col]).astype(bf16)
            part_expand = part_expand + outer_sum(cells[:, row, :, col], d_pre)
            in_row.append((dot_t(d_pre, w_expand) + d_pooled).astype(bf16))
        grads.append(jnp.stack(in_row, axis=2))
    grad_image = jnp.stack(grads, axis=1).reshape(1, 24, 24, 256)
    return (grad_image,) + all_sums(
        part_proj, part_qkv, part_out, part_expand, part_depth, part_short
    )


def solution(mesh):
    fine = Mesh(mesh.devices.reshape(4, 2, 2, 4, 8), ("ylo", "core", "yhi", "x", "z"))
    cells = P(SAMPLE, ROW, COL, None)
    rows = P(SAMPLE, None)
    return jax.shard_map(
        on_device,
        mesh=fine,
        in_specs=(cells, P(), P(), P(), rows, rows, rows, cells),
        out_specs=(cells, P(), P(), P(), rows, rows, rows),
        check_vma=False,
    )
```

time: 1600 us -> 344 us (0.21)
  the two profiles are of different devices: /device:TPU:8 before, /device:TPU:1 now
where the time goes in v1:
time: 344 us; the launch traced here: 339 us
  blocking collectives  83.6 us (24%)
  starting transfers between devices  78 us (23%)
  waiting for transfers between devices  62.3 us (18%)
  local copies, waits for them, and re-layouts  60 us (17%)
  matrix products  31.3 us (9%)
  other arithmetic  20.7 us (6%)
    all_to_all x2, blocking collectives, exchange(): return lax.all_to_all(block, axes, 0, 0, tiled=True)  83.6 us
    all_to_all x3, waiting for transfers between devices, exchange(): return lax.all_to_all(block, axes, 0, 0, tiled=True)  45.4 us
    all_to_all x3, starting transfers between devices, exchange(): return lax.all_to_all(block, axes, 0, 0, tiled=True)  31.4 us
    ppermute x3, starting transfers between devices, swap_cores(): return lax.ppermute(block, 'core', [(0, 1), (1, 0)])  14.6 us
    dot_general x7, matrix products, dot(): lax.dot_general(left, right, (((left.ndim - 1,), (0,)), ((), ())), prefer...  10.8 us
    unnamed x153, local copies, waits for them, and re-layouts  9.39 us
    dot_general x8, matrix products, dot_t(): lax.dot_general(left, right, (((left.ndim - 1,), (1,)), ((), ())), prefer...  7.78 us
    ppermute x1, waiting for transfers between devices, gather_weights(): far_a = lax.ppermute(pair[:, :half], RING, around(2))  7.54 us
  transfers between devices with their start and end apart: 16, of which 7 were waited for; matrix products, arithmetic and copies ran while one was open for 10% of the time, Pallas kernels for 0%

profile of v1, /device:TPU:1, one launch (start us, length us, event | category | flops | bytes accessed | tf_op | source)
XLA Modules:
  0.0 338.7 jit_solution(8567918973923211730)
XLA Ops:
  1.4 5.7 %collective-permute-start = (bf16[1,1,256]{2,1,0:T(2,128)(2,1)S(1)}, bf16[1,1,256]{2,1,0:T(2,128)(2,1)S(1)}, u32[]{:S(2)}, u32[]{:S(2)}) collective-permute-start(bf16[1,1,256]{2,1,0:T(2,128)(2,1)S(1)} %slice.324), channel_id=1, source_target_pairs={{0,9},{1,10},{2,11},{3,12},{4,13},{5,14},{6,15},{8,17},{9,18},{10,... | collective-permute-start | bytes 1544 | tf_op jit(solution)/shard_map/ppermute | solution.py:74
  7.9 3.1 collective-permute-start.1
  11.9 4.0 %collective-permute-start.2 = (bf16[24,1,256]{2,1,0:T(2,128)(2,1)S(1)}, bf16[24,1,256]{2,1,0:T(2,128)(2,1)S(1)}, u32[]{:S(2)}, u32[]{:S(2)}) collective-permute-start(bf16[24,1,256]{2,1,0:T(2,128)(2,1)S(1)} %slice.326), channel_id=1, source_target_pairs={{0,1},{1,2},{2,3},{3,4},{4,5},{5,6},{6,7},{8,9},{9,10},{10,11},{11... | collective-permute-start | bytes 36872 | tf_op jit(solution)/shard_map/ppermute | solution.py:73
  18.8 3.4 %collective-permute-start.3 = (bf16[1024,128]{1,0:T(8,128)(2,1)S(1)}, bf16[1024,128]{1,0:T(8,128)(2,1)S(1)}, u32[]{:S(2)}, u32[]{:S(2)}) collective-permute-start(bf16[1024,128]{1,0:T(8,128)(2,1)S(1)} %constant_dynamic-update-slice_fusion), channel_id=1, source_target_pairs={{0,64},{64,0},{1,65},{65,1},{2,66},{66,2},{3,67},{67,3},{4,68},{68... | collective-permute-start | bytes 786440 | tf_op jit(solution)/shard_map/ppermute | solution.py:84
  26.2 2.1 fusion.28
  28.4 2.1 fusion.30
  30.5 2.1 fusion.40
  32.7 3.2 collective-permute-start.7
  35.9 3.8 %collective-permute-start.4 = (bf16[2,1024,128]{2,1,0:T(8,128)(2,1)S(1)}, bf16[2,1024,128]{2,1,0:T(8,128)(2,1)S(1)}, u32[]{:S(2)}, u32[]{:S(2)}) collective-permute-start(bf16[2,1024,128]{2,1,0:T(8,128)(2,1)S(1)} %maximum_select_fusion.1), channel_id=1, source_target_pairs={{0,416},{128,0},{256,128},{384,256},{32,384},{160,32},{288,160},{4... | collective-permute-start | bytes 1572872 | tf_op jit(solution)/shard_map/ppermute | solution.py:101
  39.7 2.5 collective-permute-start.5
  42.2 5.4 %collective-permute-start.6 = (bf16[2,512,128]{2,1,0:T(8,128)(2,1)S(1)}, bf16[2,512,128]{2,1,0:T(8,128)(2,1)S(1)}, u32[]{:S(2)}, u32[]{:S(2)}) collective-permute-start(bf16[2,512,128]{2,1,0:T(8,128)(2,1)S(1)} %get-tuple-element.43), channel_id=1, source_target_pairs={{0,288},{128,416},{256,0},{384,128},{32,256},{160,384},{288,32},{4... | collective-permute-start | bytes 786440 | tf_op jit(solution)/shard_map/ppermute | solution.py:104
  47.8 2.5 multiply_convert_fusion.3
  50.4 7.5 %collective-permute-done.5 = bf16[2,512,128]{2,1,0:T(8,128)(2,1)S(1)} collective-permute-done((bf16[2,512,128]{2,1,0:T(8,128)(2,1)S(1)}, bf16[2,512,128]{2,1,0:T(8,128)(2,1)S(1)}, u32[]{:S(2)}, u32[]{:S(2)}) %collective-permute-start.5) | collective-permute-done | bytes 262176 | tf_op jit(solution)/shard_map/ppermute | solution.py:103
  57.9 5.4 %collective-permute-done.6 = bf16[2,512,128]{2,1,0:T(8,128)(2,1)S(1)} collective-permute-done((bf16[2,512,128]{2,1,0:T(8,128)(2,1)S(1)}, bf16[2,512,128]{2,1,0:T(8,128)(2,1)S(1)}, u32[]{:S(2)}, u32[]{:S(2)}) %collective-permute-start.6) | collective-permute-done | bytes 262176 | tf_op jit(solution)/shard_map/ppermute | solution.py:104
  63.6 2.2 gather_fusion
  80.3 14.4 %all-to-all-start = ((bf16[64,24,128]{2,1,0:T(8,128)(2,1)}), bf16[64,24,128]{2,1,0:T(8,128)(2,1)S(1)}, u32[]{:S(2)}, u32[]{:S(2)}) async-start(bf16[64,24,128]{2,1,0:T(8,128)(2,1)} %copy.333), calls=%async_computation | async-start | bytes 786432 | tf_op jit(solution)/shard_map/all_to_all | solution.py:88
  94.7 14.9 %all-to-all-done = bf16[64,24,128]{2,1,0:T(8,128)(2,1)S(1)} async-done(((bf16[64,24,128]{2,1,0:T(8,128)(2,1)}), bf16[64,24,128]{2,1,0:T(8,128)(2,1)S(1)}, u32[]{:S(2)}, u32[]{:S(2)}) %all-to-all-start) | async-done | bytes 393248 | tf_op jit(solution)/shard_map/all_to_all | solution.py:88
  113.4 2.0 convolution_convert_fusion.4
  123.7 9.8 %all-to-all-start.1 = ((bf16[64,24,128]{2,1,0:T(8,128)(2,1)}), bf16[64,24,128]{2,1,0:T(8,128)(2,1)S(1)}, u32[]{:S(2)}, u32[]{:S(2)}) async-start(bf16[64,24,128]{2,1,0:T(8,128)(2,1)} %copy.355), calls=%async_computation.1 | async-start | bytes 786432 | tf_op jit(solution)/shard_map/all_to_all | solution.py:88
  136.9 11.6 %all-to-all-done.1 = bf16[64,24,128]{2,1,0:T(8,128)(2,1)S(1)} async-done(((bf16[64,24,128]{2,1,0:T(8,128)(2,1)}), bf16[64,24,128]{2,1,0:T(8,128)(2,1)S(1)}, u32[]{:S(2)}, u32[]{:S(2)}) %all-to-all-start.1) | async-done | bytes 393248 | tf_op jit(solution)/shard_map/all_to_all | solution.py:88
  149.4 2.6 slice_reduce_fusion
  156.6 3.3 fusion.68
  173.1 2.0 copy.411
  177.0 3.4 fusion.57
  187.5 4.1 %fusion.52 = (bf16[12,12,1024]{2,0,1:T(8,128)(2,1)}, bf16[12,12,1024]{2,0,1:T(8,128)(2,1)S(1)}) fusion(f32[12,12,1024]{2,0,1:T(8,128)} %get-tuple-element.70, f32[13,13,1024]{2,0,1:T(8,128)S(1)} %maximum_convert_fusion, f32[1024]{0:T(1024)S(1)} %bitcast.293, f32[13,13,1024]{2,0,1:T(8,128)} %get-tuple-element.67, f32[13,13,1024]{2,0,1:T(8,128)} %get-tuple-element.34, ...), kind=kLoop, calls=%fused_computation.118 | loop fusion | flops 5750784 | bytes 5918720 | tf_op jit(solution)/shard_map/convert_element_type | solution.py:304
  201.8 6.7 %collective-permute-start.11 = (bf16[4,64,24,128]{3,2,1,0:T(8,128)(2,1)S(1)}, bf16[4,64,24,128]{3,2,1,0:T(8,128)(2,1)S(1)}, u32[]{:S(2)}, u32[]{:S(2)}) collective-permute-start(bf16[4,64,24,128]{3,2,1,0:T(8,128)(2,1)S(1)} %fusion.4), channel_id=1, source_target_pairs={{0,64},{64,0},{1,65},{65,1},{2,66},{66,2},{3,67},{67,3},{4,68},{68... | collective-permute-start | bytes 4718600 | tf_op jit(solution)/shard_map/ppermute | solution.py:84
  208.5 3.0 collective-permute-done.11
  212.2 62.6 %all_to_all.25 = bf16[256,24,128]{2,1,0:T(8,128)(2,1)S(1)} all-to-all(bf16[256,24,128]{2,1,0:T(8,128)(2,1)S(1)} %bitcast.255), channel_id=1, replica_groups=mesh['ylo'=4,'core'=2,'yhi'=2,'x'=4,'z'=8] {'ylo','yhi','x','z'}, dimensions={0} | all-to-all | bytes 3145728 | tf_op jit(solution)/shard_map/all_to_all | solution.py:88
  275.1 21.0 %all_to_all.26 = bf16[64,24,128]{2,1,0:T(8,128)(2,1)S(1)} all-to-all(bf16[64,24,128]{2,1,0:T(8,128)(2,1)S(1)} %broadcast_in_dim.37), channel_id=1, replica_groups=mesh['ylo'=4,'core'=2,'yhi'=2,'x'=4,'z'=8] {'yhi','x','z'}, dimensions={0} | all-to-all | bytes 786432 | tf_op jit(solution)/shard_map/all_to_all | solution.py:88
  296.2 4.5 %collective-permute-start.12 = (bf16[512,128]{1,0:T(8,128)(2,1)S(1)}, bf16[512,128]{1,0:T(8,128)(2,1)S(1)}, u32[]{:S(2)}, u32[]{:S(2)}) collective-permute-start(bf16[512,128]{1,0:T(8,128)(2,1)S(1)} %get-tuple-element.45), channel_id=1, source_target_pairs={{0,64},{64,0},{1,65},{65,1},{2,66},{66,2},{3,67},{67,3},{4,68},{68... | collective-permute-start | bytes 393224 | tf_op jit(solution)/shard_map/ppermute | solution.py:84
  302.8 7.3 %all-to-all-start.4 = ((bf16[4,2,512,128]{3,2,1,0:T(8,128)(2,1)}), bf16[4,2,512,128]{3,2,1,0:T(8,128)(2,1)S(1)}, u32[]{:S(2)}, u32[]{:S(2)}) async-start(bf16[4,2,512,128]{3,2,1,0:T(8,128)(2,1)} %broadcast_in_dim.38), calls=%async_computation.4 | async-start | bytes 2097152 | tf_op jit(solution)/shard_map/all_to_all | solution.py:88
  316.4 18.9 %all-to-all-done.4 = bf16[4,2,512,128]{3,2,1,0:T(8,128)(2,1)S(1)} async-done(((bf16[4,2,512,128]{3,2,1,0:T(8,128)(2,1)}), bf16[4,2,512,128]{3,2,1,0:T(8,128)(2,1)S(1)}, u32[]{:S(2)}, u32[]{:S(2)}) %all-to-all-start.4) | async-done | bytes 1048608 | tf_op jit(solution)/shard_map/all_to_all | solution.py:88
  (341 shorter events, 88.6 us)
Async XLA Ops:
  0.6 25.6 %copy-start = (bf16[256,1024]{1,0:T(8,128)(2,1)S(1)}, bf16[256,1024]{1,0:T(8,128)(2,1)}, u32[]{:S(2)}) copy-start(bf16[256,1024]{1,0:T(8,128)(2,1)} %param.9) | copy-start | bytes 1572868
  1.4 24.8 %collective-permute-start = (bf16[1,1,256]{2,1,0:T(2,128)(2,1)S(1)}, bf16[1,1,256]{2,1,0:T(2,128)(2,1)S(1)}, u32[]{:S(2)}, u32[]{:S(2)}) collective-permute-start(bf16[1,1,256]{2,1,0:T(2,128)(2,1)S(1)} %slice.324), channel_id=1, source_target_pairs={{0,9},{1,10},{2,11},{3,12},{4,13},{5,14},{6,15},{8,17},{9,18},{10,... | collective-permute-start | bytes 1544 | tf_op jit(solution)/shard_map/ppermute | solution.py:74
  7.9 18.1 %collective-permute-start.1 = (bf16[1,24,256]{2,1,0:T(8,128)(2,1)S(1)}, bf16[1,24,256]{2,1,0:T(8,128)(2,1)S(1)}, u32[]{:S(2)}, u32[]{:S(2)}) collective-permute-start(bf16[1,24,256]{2,1,0:T(8,128)(2,1)S(1)} %slice_bitcast_fusion.6), channel_id=1, source_target_pairs={{0,8},{8,16},{16,24},{24,32},{32,40},{40,48},{48,56},{1,9},{9,17},... | collective-permute-start | bytes 36872 | tf_op jit(solution)/shard_map/ppermute | solution.py:72
  11.9 14.1 %collective-permute-start.2 = (bf16[24,1,256]{2,1,0:T(2,128)(2,1)S(1)}, bf16[24,1,256]{2,1,0:T(2,128)(2,1)S(1)}, u32[]{:S(2)}, u32[]{:S(2)}) collective-permute-start(bf16[24,1,256]{2,1,0:T(2,128)(2,1)S(1)} %slice.326), channel_id=1, source_target_pairs={{0,1},{1,2},{2,3},{3,4},{4,5},{5,6},{6,7},{8,9},{9,10},{10,11},{11... | collective-permute-start | bytes 36872 | tf_op jit(solution)/shard_map/ppermute | solution.py:73
  18.8 13.8 %collective-permute-start.3 = (bf16[1024,128]{1,0:T(8,128)(2,1)S(1)}, bf16[1024,128]{1,0:T(8,128)(2,1)S(1)}, u32[]{:S(2)}, u32[]{:S(2)}) collective-permute-start(bf16[1024,128]{1,0:T(8,128)(2,1)S(1)} %constant_dynamic-update-slice_fusion), channel_id=1, source_target_pairs={{0,64},{64,0},{1,65},{65,1},{2,66},{66,2},{3,67},{67,3},{4,68},{68... | collective-permute-start | bytes 786440 | tf_op jit(solution)/shard_map/ppermute | solution.py:84
  25.2 22.5 %copy-start.51 = (f32[1,1,1024]{2,1,0:T(1,128)}, f32[1,1,1024]{2,1,0:T(1,128)S(1)}, u32[]{:S(2)}) copy-start(f32[1,1,1024]{2,1,0:T(1,128)S(1)} %get-tuple-element.54) | copy-start | bytes 12292
  25.2 22.5 %copy-start.53 = (f32[1,1,1024]{2,1,0:T(1,128)}, f32[1,1,1024]{2,1,0:T(1,128)S(1)}, u32[]{:S(2)}) copy-start(f32[1,1,1024]{2,1,0:T(1,128)S(1)} %get-tuple-element.56) | copy-start | bytes 12292
  25.2 22.5 %copy-start.55 = (f32[1,1,1024]{2,1,0:T(1,128)}, f32[1,1,1024]{2,1,0:T(1,128)S(1)}, u32[]{:S(2)}) copy-start(f32[1,1,1024]{2,1,0:T(1,128)S(1)} %get-tuple-element.58) | copy-start | bytes 12292
  25.2 22.5 %copy-start.57 = (f32[1,1,1024]{2,1,0:T(1,128)}, f32[1,1,1024]{2,1,0:T(1,128)S(1)}, u32[]{:S(2)}) copy-start(f32[1,1,1024]{2,1,0:T(1,128)S(1)} %get-tuple-element.60) | copy-start | bytes 12292
  25.2 22.5 %copy-start.59 = (f32[1,1,1024]{2,1,0:T(1,128)}, f32[1,1,1024]{2,1,0:T(1,128)S(1)}, u32[]{:S(2)}) copy-start(f32[1,1,1024]{2,1,0:T(1,128)S(1)} %get-tuple-element.62) | copy-start | bytes 12292
  25.2 22.5 %copy-start.61 = (f32[1,1,1024]{2,1,0:T(1,128)}, f32[1,1,1024]{2,1,0:T(1,128)S(1)}, u32[]{:S(2)}) copy-start(f32[1,1,1024]{2,1,0:T(1,128)S(1)} %get-tuple-element.55) | copy-start | bytes 12292
  25.3 22.5 %copy-start.63 = (f32[1,1,1024]{2,1,0:T(1,128)}, f32[1,1,1024]{2,1,0:T(1,128)S(1)}, u32[]{:S(2)}) copy-start(f32[1,1,1024]{2,1,0:T(1,128)S(1)} %get-tuple-element.57) | copy-start | bytes 12292
  25.3 22.5 %copy-start.65 = (f32[1,1,1024]{2,1,0:T(1,128)}, f32[1,1,1024]{2,1,0:T(1,128)S(1)}, u32[]{:S(2)}) copy-start(f32[1,1,1024]{2,1,0:T(1,128)S(1)} %get-tuple-element.59) | copy-start | bytes 12292
  25.3 22.5 %copy-start.67 = (f32[1,1,1024]{2,1,0:T(1,128)}, f32[1,1,1024]{2,1,0:T(1,128)S(1)}, u32[]{:S(2)}) copy-start(f32[1,1,1024]{2,1,0:T(1,128)S(1)} %get-tuple-element.61) | copy-start | bytes 12292
  25.6 48.9 %copy-start.39 = (bf16[12,1,12,1,256]{4,3,2,1,0:T(2,128)(2,1)}, bf16[12,1,12,1,256]{4,3,2,1,0:T(2,128)(2,1)S(1)}, u32[]{:S(2)}) copy-start(bf16[12,1,12,1,256]{4,3,2,1,0:T(2,128)(2,1)S(1)} %fusion.109) | copy-start | bytes 221188
  28.4 19.4 %copy-start.35 = (bf16[13,13,1024]{2,0,1:T(8,128)(2,1)}, bf16[13,13,1024]{2,0,1:T(8,128)(2,1)S(1)}, u32[]{:S(2)}) copy-start(bf16[13,13,1024]{2,0,1:T(8,128)(2,1)S(1)} %get-tuple-element.36) | copy-start | bytes 1038340
  30.5 17.3 %copy-start.37 = (bf16[12,13,1024]{2,0,1:T(8,128)(2,1)}, bf16[12,13,1024]{2,0,1:T(8,128)(2,1)S(1)}, u32[]{:S(2)}) copy-start(bf16[12,13,1024]{2,0,1:T(8,128)(2,1)S(1)} %get-tuple-element.32) | copy-start | bytes 958468
  32.6 17.7 %copy-start.41 = (bf16[13,12,1024]{2,0,1:T(8,128)(2,1)}, bf16[13,12,1024]{2,0,1:T(8,128)(2,1)S(1)}, u32[]{:S(2)}) copy-start(bf16[13,12,1024]{2,0,1:T(8,128)(2,1)S(1)} %get-tuple-element.40) | copy-start | bytes 958468
  32.7 30.6 %collective-permute-start.7 = (bf16[2,1024,128]{2,1,0:T(8,128)(2,1)S(1)}, bf16[2,1024,128]{2,1,0:T(8,128)(2,1)S(1)}, u32[]{:S(2)}, u32[]{:S(2)}) collective-permute-start(bf16[2,1024,128]{2,1,0:T(8,128)(2,1)S(1)} %maximum_select_fusion.1), channel_id=1, source_target_pairs={{0,128},{128,256},{256,384},{384,32},{32,160},{160,288},{288,416},... | collective-permute-start | bytes 1572872 | tf_op jit(solution)/shard_map/ppermute | solution.py:100
  35.9 27.4 %collective-permute-start.4 = (bf16[2,1024,128]{2,1,0:T(8,128)(2,1)S(1)}, bf16[2,1024,128]{2,1,0:T(8,128)(2,1)S(1)}, u32[]{:S(2)}, u32[]{:S(2)}) collective-permute-start(bf16[2,1024,128]{2,1,0:T(8,128)(2,1)S(1)} %maximum_select_fusion.1), channel_id=1, source_target_pairs={{0,416},{128,0},{256,128},{384,256},{32,384},{160,32},{288,160},{4... | collective-permute-start | bytes 1572872 | tf_op jit(solution)/shard_map/ppermute | solution.py:101
  39.7 18.2 %collective-permute-start.5 = (bf16[2,512,128]{2,1,0:T(8,128)(2,1)S(1)}, bf16[2,512,128]{2,1,0:T(8,128)(2,1)S(1)}, u32[]{:S(2)}, u32[]{:S(2)}) collective-permute-start(bf16[2,512,128]{2,1,0:T(8,128)(2,1)S(1)} %get-tuple-element.42), channel_id=1, source_target_pairs={{0,256},{128,384},{256,32},{384,160},{32,288},{160,416},{288,0},{4... | collective-permute-start | bytes 786440 | tf_op jit(solution)/shard_map/ppermute | solution.py:103
  42.2 21.1 %collective-permute-start.6 = (bf16[2,512,128]{2,1,0:T(8,128)(2,1)S(1)}, bf16[2,512,128]{2,1,0:T(8,128)(2,1)S(1)}, u32[]{:S(2)}, u32[]{:S(2)}) collective-permute-start(bf16[2,512,128]{2,1,0:T(8,128)(2,1)S(1)} %get-tuple-element.43), channel_id=1, source_target_pairs={{0,288},{128,416},{256,0},{384,128},{32,256},{160,384},{288,32},{4... | collective-permute-start | bytes 786440 | tf_op jit(solution)/shard_map/ppermute | solution.py:104
  80.3 29.3 %all-to-all-start = ((bf16[64,24,128]{2,1,0:T(8,128)(2,1)}), bf16[64,24,128]{2,1,0:T(8,128)(2,1)S(1)}, u32[]{:S(2)}, u32[]{:S(2)}) async-start(bf16[64,24,128]{2,1,0:T(8,128)(2,1)} %copy.333), calls=%async_computation | async-start | bytes 786432 | tf_op jit(solution)/shard_map/all_to_all | solution.py:88
  122.5 11.7 %copy-start.23 = (bf16[12,1,12,1,256]{4,3,2,1,0:T(2,128)(2,1)S(1)}, bf16[12,1,12,1,256]{4,3,2,1,0:T(2,128)(2,1)}, u32[]{:S(2)}) copy-start(bf16[12,1,12,1,256]{4,3,2,1,0:T(2,128)(2,1)} %copy-done.22) | copy-start | bytes 221188
  122.6 12.3 %copy-start.44 = (bf16[12,12,256]{2,1,0:T(8,128)(2,1)S(1)}, bf16[12,12,256]{2,1,0:T(8,128)(2,1)}, u32[]{:S(2)}) copy-start(bf16[12,12,256]{2,1,0:T(8,128)(2,1)} %get-tuple-element.23) | copy-start | bytes 221188
  123.7 24.8 %all-to-all-start.1 = ((bf16[64,24,128]{2,1,0:T(8,128)(2,1)}), bf16[64,24,128]{2,1,0:T(8,128)(2,1)S(1)}, u32[]{:S(2)}, u32[]{:S(2)}) async-start(bf16[64,24,128]{2,1,0:T(8,128)(2,1)} %copy.355), calls=%async_computation.1 | async-start | bytes 786432 | tf_op jit(solution)/shard_map/all_to_all | solution.py:88
  163.3 11.8 %collective-permute-start.10 = (bf16[1,1,1024]{2,0,1:T(2,128)(2,1)S(1)}, bf16[1,1,1024]{2,0,1:T(2,128)(2,1)S(1)}, u32[]{:S(2)}, u32[]{:S(2)}) collective-permute-start(bf16[1,1,1024]{2,0,1:T(2,128)(2,1)S(1)} %slice.373), channel_id=1, source_target_pairs={{9,0},{10,1},{11,2},{12,3},{13,4},{14,5},{15,6},{17,8},{18,9},{19,... | collective-permute-start | bytes 6152 | tf_op jit(solution)/shard_map/ppermute | solution.py:74
  164.6 10.5 %collective-permute-start.8 = (bf16[12,1,1024]{2,0,1:T(8,128)(2,1)S(1)}, bf16[12,1,1024]{2,0,1:T(8,128)(2,1)S(1)}, u32[]{:S(2)}, u32[]{:S(2)}) collective-permute-start(bf16[12,1,1024]{2,0,1:T(8,128)(2,1)S(1)} %slice.371), channel_id=1, source_target_pairs={{1,0},{2,1},{3,2},{4,3},{5,4},{6,5},{7,6},{9,8},{10,9},{11,10},{12... | collective-permute-start | bytes 73736 | tf_op jit(solution)/shard_map/ppermute | solution.py:73
  165.9 9.8 %collective-permute-start.9 = (bf16[1,12,1024]{2,0,1:T(2,128)(2,1)S(1)}, bf16[1,12,1024]{2,0,1:T(2,128)(2,1)S(1)}, u32[]{:S(2)}, u32[]{:S(2)}) collective-permute-start(bf16[1,12,1024]{2,0,1:T(2,128)(2,1)S(1)} %slice.372), channel_id=1, source_target_pairs={{8,0},{16,8},{24,16},{32,24},{40,32},{48,40},{56,48},{9,1},{17,9},... | collective-permute-start | bytes 73736 | tf_op jit(solution)/shard_map/ppermute | solution.py:72
  201.8 9.7 %collective-permute-start.11 = (bf16[4,64,24,128]{3,2,1,0:T(8,128)(2,1)S(1)}, bf16[4,64,24,128]{3,2,1,0:T(8,128)(2,1)S(1)}, u32[]{:S(2)}, u32[]{:S(2)}) collective-permute-start(bf16[4,64,24,128]{3,2,1,0:T(8,128)(2,1)S(1)} %fusion.4), channel_id=1, source_target_pairs={{0,64},{64,0},{1,65},{65,1},{2,66},{66,2},{3,67},{67,3},{4,68},{68... | collective-permute-start | bytes 4718600 | tf_op jit(solution)/shard_map/ppermute | solution.py:84
  296.2 5.5 %collective-permute-start.12 = (bf16[512,128]{1,0:T(8,128)(2,1)S(1)}, bf16[512,128]{1,0:T(8,128)(2,1)S(1)}, u32[]{:S(2)}, u32[]{:S(2)}) collective-permute-start(bf16[512,128]{1,0:T(8,128)(2,1)S(1)} %get-tuple-element.45), channel_id=1, source_target_pairs={{0,64},{64,0},{1,65},{65,1},{2,66},{66,2},{3,67},{67,3},{4,68},{68... | collective-permute-start | bytes 393224 | tf_op jit(solution)/shard_map/ppermute | solution.py:84
  302.8 32.5 %all-to-all-start.4 = ((bf16[4,2,512,128]{3,2,1,0:T(8,128)(2,1)}), bf16[4,2,512,128]{3,2,1,0:T(8,128)(2,1)S(1)}, u32[]{:S(2)}, u32[]{:S(2)}) async-start(bf16[4,2,512,128]{3,2,1,0:T(8,128)(2,1)} %broadcast_in_dim.38), calls=%async_computation.4 | async-start | bytes 2097152 | tf_op jit(solution)/shard_map/all_to_all | solution.py:88
  (56 other events, 194.2 us)

commit v2 on v1

v2 whole, which is shorter than its diff:
```python
import math

import jax
import jax.numpy as jnp
import numpy as np
from jax import lax
from jax.experimental import pallas as pl
from jax.experimental.pallas import tpu as pltpu
from jax.sharding import Mesh
from jax.sharding import PartitionSpec as P

HEADS = 8
PARTS = 8

SAMPLE = ("ylo", "core")
ROW = ("yhi", "x")
COL = "z"
GRID_AXES = ("yhi", "x", "z")
CHIPS = ("ylo", "yhi", "x", "z")
RING = ("ylo", "yhi")

norm_epsilon = 1e-05
tanh_coeff = 0.7978845608028654
cubic_coeff = 0.044715

bf16 = jnp.bfloat16
f32 = jnp.float32


def gelu_both(values):
    inner = jnp.tanh(tanh_coeff * (values + cubic_coeff * values * values * values))
    value = 0.5 * values * (1.0 + inner)
    slope = 0.5 * (1.0 + inner) + 0.5 * values * (1.0 - inner * inner) * tanh_coeff * (
        1.0 + 3.0 * cubic_coeff * values * values
    )
    return value, slope


def dot(left, right):
    return lax.dot_general(
        left, right, (((left.ndim - 1,), (0,)), ((), ())), preferred_element_type=f32
    )


def dot_t(left, right):
    return lax.dot_general(
        left, right, (((left.ndim - 1,), (1,)), ((), ())), preferred_element_type=f32
    )


def dot_tt(left, right):
    return lax.dot_general(left, right, (((0,), (0,)), ((), ())), preferred_element_type=f32)


def outer_sum(left, right):
    return lax.dot_general(
        left.reshape(-1, left.shape[-1]),
        right.reshape(-1, right.shape[-1]),
        (((0,), (0,)), ((), ())),
        preferred_element_type=f32,
    )


def step_route(count, distance):
    return [(i - distance, i) for i in range(count) if 0 <= i - distance < count]


def diagonal_route(distance):
    return [
        ((r - distance) * PARTS + c - distance, r * PARTS + c)
        for r in range(PARTS)
        for c in range(PARTS)
        if 0 <= r - distance < PARTS and 0 <= c - distance < PARTS
    ]


def rims(edge_row, edge_col, corner, distance):
    return (
        lax.ppermute(edge_row, ROW, step_route(PARTS, distance)),
        lax.ppermute(edge_col, COL, step_route(PARTS, distance)),
        lax.ppermute(corner, GRID_AXES, diagonal_route(distance)),
    )


def around(distance):
    place = [y % 4 * 2 + y // 4 for y in range(8)]
    return [(place[y], place[(y + distance) % 8]) for y in range(8)]


def swap_cores(block):
    return lax.ppermute(block, "core", [(0, 1), (1, 0)])


def exchange(block, axes):
    return lax.all_to_all(block, axes, 0, 0, tiled=True)


def spread(block, axes, count):
    return exchange(jnp.broadcast_to(block[None], (count,) + block.shape), axes)


def gather_weights(w_proj, w_qkv, w_out):
    tail = w_qkv[:, 512:]
    own = jnp.concatenate(
        [w_proj, w_qkv[:, :512], w_out, jnp.concatenate([tail[:32], tail[32:]], axis=1)], axis=0
    )
    below = lax.ppermute(own, RING, around(1))
    above = lax.ppermute(own, RING, around(7))
    far = jnp.concatenate(
        [lax.ppermute(own[:128], RING, around(2)), lax.ppermute(own[128:], RING, around(6))]
    )
    ring = jnp.stack([own, above, far, below])
    both = jnp.concatenate([ring, swap_cores(ring)])
    shard = jnp.arange(8)
    side = (shard % 2 + lax.axis_index("core")) % 2
    place = side * 4 + (shard // 2 - lax.axis_index("ylo")) % 4
    shards = jnp.take(both, place, axis=0)
    proj = shards[:, :128].reshape(1024, 512)
    lower = shards[:, 224:]
    tails = jnp.concatenate([lower[:, :, :256], lower[:, :, 256:]], axis=1)
    qkv = jnp.concatenate([shards[:, 128:192], tails], axis=2).reshape(512, 768)
    return proj, qkv, shards[:, 192:224].reshape(256, 512)


def head_order():
    target = np.arange(1024)
    wanted = target // 32 % 4 * 256 + target // 128 * 32 + target % 32
    return jnp.asarray(target[:, None] == wanted[None, :], bf16)


def slot_order():
    target = np.arange(192)
    both = []
    for odd in range(2):
        group = (target // 24 + odd * 4) % 8
        wanted = target // 2 % 12 * 16 + target % 2 * 8 + group
        both.append(target[None, :] == wanted[:, None])
    both = jnp.asarray(np.stack(both), bf16)
    return lax.dynamic_index_in_dim(both, lax.axis_index("z") % 2, 0, keepdims=False)


def row_order():
    target = np.arange(192)
    wanted = target // 2 % 8 * 24 + target // 16 * 2 + target % 2
    return jnp.asarray(target[None, :] == wanted[:, None], bf16)


def dot_kt(left, right):
    return lax.dot_general(left, right, (((1,), (1,)), ((), ())), preferred_element_type=f32)


def attention_kernel(slots_ref, order_ref, valid_ref, out_ref, sorted_ref, result_ref):
    scale = 1.0 / math.sqrt(32)
    order = order_ref[...]
    valid = valid_ref[...] > 0.0
    for part in range(8):
        sorted_ref[part * 192 : part * 192 + 192] = dot(order, slots_ref[part]).astype(bf16)
    for group in range(8):
        blocks = [row * 16 for row in range(96) if row % 8 == group]
        unit = jnp.concatenate([sorted_ref[at : at + 16] for at in blocks], axis=0)
        query, key, value, d_mix = (unit[:, 32 * i : 32 * i + 32] for i in range(4))
        raised = jnp.where(valid, jnp.exp(dot_kt(query, key) * scale), 0.0)
        weights32 = raised / jnp.sum(raised, axis=-1, keepdims=True)
        weights = weights32.astype(bf16)
        mixture = dot(weights, value)
        d_weights = dot_kt(d_mix, value)
        d_value = dot_tt(weights, d_mix)
        d_scores = (
            weights32 * (d_weights - jnp.sum(weights32 * d_weights, axis=-1, keepdims=True))
        ).astype(bf16)
        d_query = dot(d_scores, key) * scale
        d_key = dot_tt(d_scores, query) * scale
        result = jnp.concatenate([d_query, d_key, d_value, mixture], axis=-1).astype(bf16)
        for index, at in enumerate(blocks):
            result_ref[at : at + 16] = result[index * 16 : index * 16 + 16]
    for part in range(8):
        out_ref[part] = dot_tt(order, result_ref[part * 192 : part * 192 + 192]).astype(bf16)


def attention(slots):
    slot = lax.broadcasted_iota(jnp.int32, (1, 192), 1)
    high = (lax.axis_index("z") >= 4).astype(jnp.int32)
    valid = ((slot % 2 == 0) | (slot // 2 % 2 == high)).astype(f32)
    return pl.pallas_call(
        attention_kernel,
        out_shape=jax.ShapeDtypeStruct((8, 192, 128), bf16),
        scratch_shapes=[pltpu.VMEM((1536, 128), bf16), pltpu.VMEM((1536, 128), bf16)],
        cost_estimate=pl.CostEstimate(
            flops=500_000_000, bytes_accessed=1_000_000, transcendentals=300_000
        ),
        name="attention",
    )(slots, row_order(), valid)


def mix_tokens(tokens, heads, slots):
    sorted_tokens = dot(slots, dot(tokens, heads).astype(bf16)).astype(bf16)
    pieces = sorted_tokens.reshape(192, HEADS, 128).transpose(1, 0, 2)
    got = exchange(pieces.reshape(64, 24, 128), GRID_AXES)
    results = attention(got.reshape(8, 192, 128))
    got = exchange(results.reshape(64, 24, 128), GRID_AXES).reshape(HEADS, 192, 128)
    got = got.transpose(1, 0, 2).reshape(192, 1024)
    return dot_t(dot_tt(slots, got).astype(bf16), heads).astype(bf16)


def tiles(part, shards, height):
    rows, columns = part.shape
    cut = part.astype(bf16).reshape(shards, rows // shards // height, height, columns // 128, 128)
    return cut.transpose(0, 1, 3, 2, 4).reshape(shards, -1, height, 128)


def untiled(pieces, rows, columns):
    height = pieces.shape[1]
    cut = pieces.reshape(rows // height, columns // 128, height, 128)
    return cut.transpose(0, 2, 1, 3).reshape(rows, columns).astype(f32)


def add_cores(halves, axis):
    core = lax.axis_index("core")
    mine = lax.dynamic_index_in_dim(halves, core, axis, keepdims=False)
    theirs = lax.dynamic_index_in_dim(halves, 1 - core, axis, keepdims=False)
    return mine, theirs


def paired_sum(mine, theirs):
    pair = (mine.astype(f32) + swap_cores(theirs).astype(f32)).astype(bf16)
    pieces = exchange(pair, CHIPS)
    grad_scale = 1.0 / math.sqrt(8 * 96 * 96)
    return (jnp.sum(pieces.astype(f32), axis=0) * grad_scale).astype(bf16)


def all_sums(part_proj, part_qkv, part_out, part_expand, part_depth, part_short):
    matrix = jnp.concatenate(
        [tiles(part, 8, 16) for part in (part_proj, part_qkv, part_out)], axis=1
    ).reshape(4, 2, 64, 16, 128)
    rest = jnp.concatenate(
        [
            tiles(part_expand, 1, 8)[0],
            tiles(part_short, 1, 8)[0],
            part_depth.astype(bf16).reshape(9, 8, 128),
        ]
    )
    rest = jnp.pad(rest, ((0, 512 - rest.shape[0]), (0, 0), (0, 0))).reshape(2, 256, 8, 128)
    matrix_mine, matrix_theirs = add_cores(matrix, 1)
    rest_mine, rest_theirs = add_cores(rest, 0)
    mine = jnp.concatenate([matrix_mine.reshape(256, 16, 128), rest_mine], axis=1)
    theirs = jnp.concatenate([matrix_theirs.reshape(256, 16, 128), rest_theirs], axis=1)
    near = spread(paired_sum(mine, theirs), GRID_AXES, 64)
    grad_proj = untiled(near[:32, :16], 128, 512)
    grad_qkv = untiled(near[32:56, :16], 64, 768)
    grad_out = untiled(near[56:, :16], 32, 512)
    own = near[:, 16:]
    ring = jnp.stack(
        [own] + [lax.ppermute(own, RING, around(step)) for step in (7, 2, 1)]
    )
    both = jnp.concatenate([ring, swap_cores(ring)])
    shard = jnp.arange(8)
    side = (shard // 4 + lax.axis_index("core")) % 2
    place = side * 4 + (shard % 4 - lax.axis_index("ylo")) % 4
    both = jnp.take(both, place, axis=0).reshape(512, 8, 128)
    grad_expand = untiled(both[:256], 256, 1024)
    grad_short = untiled(both[256:384], 256, 512)
    grad_depth = both[384:393].reshape(3, 3, 1024).astype(f32)
    return grad_expand, grad_depth, grad_short, grad_proj, grad_qkv, grad_out


def slots16(cells, last=None):
    rows, _, width = cells.shape
    if last is None:
        return jnp.pad(cells, ((0, 0), (0, 4), (0, 0)))
    return jnp.concatenate([cells, jnp.zeros((rows, 3, width), cells.dtype), last], axis=1)


def on_device(images, w_expand, w_depth, w_short, w_proj, w_qkv, w_out, cotangent):
    images = images[0]
    cotangent = slots16(cotangent[0])
    proj, qkv, out = gather_weights(w_proj, w_qkv, w_out)
    top, left, corner = rims(images[-1:], images[:, -1:], images[-1:, -1:], 1)
    heads, slots = head_order(), slot_order()
    used = lax.broadcasted_iota(jnp.int32, (1, 16, 1), 1) < 12

    cells = images.reshape(12, 2, 12, 2, 256)
    top_cells = top.reshape(1, 12, 2, 256)
    left_cells = left.reshape(12, 2, 1, 256)
    planes = {
        (0, 0): slots16(cells[:, 0, :, 0]),
        (0, 1): slots16(cells[:, 0, :, 1], left_cells[:, 0]),
        (1, 0): jnp.concatenate([slots16(top_cells[:, :, 0]), slots16(cells[:, 1, :, 0])]),
        (1, 1): jnp.concatenate(
            [
                slots16(top_cells[:, :, 1], corner),
                slots16(cells[:, 1, :, 1], left_cells[:, 1]),
            ]
        ),
    }
    expanded, slopes = {}, {}
    for place, plane in planes.items():
        value, slope = gelu_both(dot(plane, w_expand))
        expanded[place] = value.astype(bf16)
        slopes[place] = slope[place[0] :].astype(bf16)
    taps = w_depth.astype(f32)

    def window(row_tap, odd_col):
        plane = expanded[(row_tap + 1) % 2, odd_col]
        return plane[row_tap // 2 : row_tap // 2 + 12].astype(f32)

    straight = sum(
        window(a, 0) * taps[a, 1] + window(a, 1) * taps[a, 2] for a in range(3)
    )
    moved = sum(window(a, 1) * taps[a, 0] for a in range(3))
    value, conv_slope = gelu_both(straight + jnp.roll(moved, 1, axis=1))
    activated = value.astype(bf16)
    conv_slope = conv_slope.astype(bf16)
    wide = cells.astype(f32)
    pooled = slots16(
        ((wide[:, 0, :, 0] + wide[:, 0, :, 1] + wide[:, 1, :, 0] + wide[:, 1, :, 1]) * 0.25).astype(bf16)
    )

    section_out = (dot(activated, proj) + dot(pooled, w_short)).astype(bf16).astype(f32)
    centred = section_out - jnp.mean(section_out, axis=-1, keepdims=True)
    inv_std = lax.rsqrt(jnp.mean(centred * centred, axis=-1, keepdims=True) + norm_epsilon)
    normalized = centred * inv_std
    normed = jnp.where(used, normalized.astype(bf16), jnp.zeros((), bf16))
    packed = dot(normed, qkv).astype(bf16)
    d_mixture = dot_t(cotangent, out).astype(bf16)
    tokens = jnp.concatenate([packed, d_mixture], axis=-1).reshape(192, 1024)
    results = mix_tokens(tokens, heads, slots)
    results = jnp.where(used, results.reshape(12, 16, 1024), jnp.zeros((), bf16))
    d_packed = results[:, :, :768]
    mixture = results[:, :, 768:]

    part_out = outer_sum(mixture, cotangent)
    part_qkv = outer_sum(normed, d_packed)
    d_normed = dot_t(d_packed, qkv)
    d_section = (
        cotangent.astype(f32)
        + inv_std
        * (
            d_normed
            - jnp.mean(d_normed, axis=-1, keepdims=True)
            - normalized * jnp.mean(d_normed * normalized, axis=-1, keepdims=True)
        )
    ).astype(bf16)
    d_section = jnp.where(used, d_section, jnp.zeros((), bf16))
    d_conv = (dot_t(d_section, proj) * conv_slope.astype(f32)).astype(bf16)
    below, right, beyond = rims(d_conv[:1, :12], d_conv[:, :1], d_conv[:1, :1], -1)
    part_proj = outer_sum(activated, d_section)
    part_short = outer_sum(pooled, d_section)
    here = d_conv.astype(f32)
    back = jnp.roll(here, -1, axis=1)
    part_depth = jnp.stack(
        [
            jnp.stack(
                [
                    jnp.sum(window(a, 1) * back, axis=(0, 1)),
                    jnp.sum(window(a, 0) * here, axis=(0, 1)),
                    jnp.sum(window(a, 1) * here, axis=(0, 1)),
                ]
            )
            for a in range(3)
        ]
    )
    rows = jnp.concatenate([d_conv, slots16(below)], axis=0)
    column = jnp.concatenate([right, beyond], axis=0)
    slot = lax.broadcasted_iota(jnp.int32, (1, 16, 1), 1)
    after = jnp.where(slot == 11, column, jnp.roll(rows, -1, axis=1)).astype(f32)
    rows = rows.astype(f32)
    d_pooled = dot_t(d_section, w_short) * 0.25
    row_terms = {0: ((1, 0),), 1: ((2, 0), (0, 1))}
    col_terms = {0: ((1, rows),), 1: ((2, rows), (0, after))}
    part_expand = 0.0
    grads = []
    for row in range(2):
        in_row = []
        for col in range(2):
            d_cells = sum(
                source[i : i + 12] * taps[a, b]
                for a, i in row_terms[row]
                for b, source in col_terms[col]
            )
            d_pre = (d_cells * slopes[row, col].astype(f32)).astype(bf16)
            d_pre = jnp.where(used, d_pre, jnp.zeros((), bf16))
            part_expand = part_expand + outer_sum(planes[row, col][row:], d_pre)
            in_row.append((dot_t(d_pre, w_expand) + d_pooled).astype(bf16)[:, :12])
        grads.append(jnp.stack(in_row, axis=2))
    grad_image = jnp.stack(grads, axis=1).reshape(1, 24, 24, 256)
    return (grad_image,) + all_sums(
        part_proj, part_qkv, part_out, part_expand, part_depth, part_short
    )


def solution(mesh):
    fine = Mesh(mesh.devices.reshape(4, 2, 2, 4, 8), ("ylo", "core", "yhi", "x", "z"))
    cells = P(SAMPLE, ROW, COL, None)
    rows = P(SAMPLE, None)
    return jax.shard_map(
        on_device,
        mesh=fine,
        in_specs=(cells, P(), P(), P(), rows, rows, rows, cells),
        out_specs=(cells, P(), P(), P(), rows, rows, rows),
        check_vma=False,
    )
```

time: 344 us -> 289 us (0.84); the launches traced: 339 us -> 288 us
  blocking collectives: 83.6 us -> 0 us
  starting transfers between devices: 78 us -> 116 us
  local copies, waits for them, and re-layouts: 60 us -> 31.4 us
  waiting for transfers between devices: 62.3 us -> 88.4 us
  matrix products: 31.3 us -> 23.6 us
  Pallas kernels: 0 us -> 6.29 us
    all_to_all x2 -> x0, blocking collectives: 83.6 us -> none  [exchange(): return lax.all_to_all(block, axes, 0, 0, tiled=True)]
    all_to_all x3 -> x4, waiting for transfers between devices: 45.4 us -> 81.4 us  [exchange(): return lax.all_to_all(block, axes, 0, 0, tiled=True)]
    reshape x29 -> x5, local copies, waits for them, and re-layouts: 24.6 us -> 2.65 us  [tiles(): part.astype(bf16)]
    all_to_all x3 -> x4, starting transfers between devices: 31.4 us -> 52.8 us  [exchange(): return lax.all_to_all(block, axes, 0, 0, tiled=True)]
    ppermute x4 -> x7, starting transfers between devices: 14.9 us -> 30.8 us  [the longest x3 14.7 us: all_sums(): lax.ppermute(own, RING, around(step))]
    ppermute x4 -> x7, waiting for transfers between devices: 12.9 us -> 1.92 us  [the longest x3 1.91 us: all_sums(): lax.ppermute(own, RING, around(step))]
    pallas_call x0 -> x1, Pallas kernels: none -> 6.29 us  [attention(): pl.pallas_call(attention_kernel, out_shape=jax.ShapeDtypeStruct((8, 192,...]
    dot_general x6 -> x0, matrix products: 6.23 us -> none  [batched(): return jnp.einsum(form, left, right, preferred_element_type=f32)]
  transfers between devices with their start and end apart: 16 -> 20, of which waited for: 7 -> 8; matrix products, arithmetic and copies ran while one was open for 10% -> 12% of each run, Pallas kernels for 0% -> 0%
where the time goes in v2:
time: 289 us; the launch traced here: 288 us
  starting transfers between devices  116 us (40%)
  waiting for transfers between devices  88.4 us (31%)
  local copies, waits for them, and re-layouts  31.4 us (11%)
  matrix products  23.6 us (8%)
  other arithmetic  19.1 us (7%)
  Pallas kernels  6.29 us (2%)
    all_to_all x4, waiting for transfers between devices, exchange(): return lax.all_to_all(block, axes, 0, 0, tiled=True)  81.4 us
    all_to_all x4, starting transfers between devices, exchange(): return lax.all_to_all(block, axes, 0, 0, tiled=True)  52.8 us
    ppermute x3, starting transfers between devices, swap_cores(): return lax.ppermute(block, 'core', [(0, 1), (1, 0)])  16.8 us
    ppermute x3, starting transfers between devices, all_sums(): lax.ppermute(own, RING, around(step))  14.7 us
    unnamed x159, local copies, waits for them, and re-layouts  11.3 us
    dot_general x8, matrix products, dot(): lax.dot_general(left, right, (((left.ndim - 1,), (0,)), ((), ())), prefer...  11.2 us
    dot_general x9, matrix products, dot_t(): lax.dot_general(left, right, (((left.ndim - 1,), (1,)), ((), ())), prefer...  7.29 us
    ppermute x2, starting transfers between devices, rims(): lax.ppermute(corner, GRID_AXES, diagonal_route(distance))  6.32 us
  transfers between devices with their start and end apart: 20, of which 8 were waited for; matrix products, arithmetic and copies ran while one was open for 12% of the time, Pallas kernels for 0%

profile of v2, /device:TPU:1, one launch (start us, length us, event | category | flops | bytes accessed | tf_op | source)
XLA Modules:
  0.0 287.7 jit_solution(13185759082058561316)
XLA Ops:
  0.6 5.2 %collective-permute-start.4 = (bf16[128,512]{1,0:T(8,128)(2,1)}, bf16[128,512]{1,0:T(8,128)(2,1)S(1)}, u32[]{:S(2)}, u32[]{:S(2)}) collective-permute-start(bf16[128,512]{1,0:T(8,128)(2,1)} %param.15), channel_id=1, source_target_pairs={{0,256},{128,384},{256,32},{384,160},{32,288},{160,416},{288,0},{4... | collective-permute-start | bytes 393224 | tf_op jit(solution)/shard_map/ppermute | solution.py:110
  9.1 3.2 %collective-permute-start.6 = (bf16[256,512]{1,0:T(8,128)(2,1)S(1)}, bf16[256,512]{1,0:T(8,128)(2,1)S(1)}, u32[]{:S(2)}, u32[]{:S(2)}) collective-permute-start(bf16[256,512]{1,0:T(8,128)(2,1)S(1)} %get-tuple-element.25), channel_id=1, source_target_pairs={{0,128},{128,256},{256,384},{384,32},{32,160},{160,288},{288,416},... | collective-permute-start | bytes 786440 | tf_op jit(solution)/shard_map/ppermute | solution.py:107
  12.3 3.3 %collective-permute-start.3 = (bf16[256,512]{1,0:T(8,128)(2,1)S(1)}, bf16[256,512]{1,0:T(8,128)(2,1)S(1)}, u32[]{:S(2)}, u32[]{:S(2)}) collective-permute-start(bf16[256,512]{1,0:T(8,128)(2,1)S(1)} %get-tuple-element.25), channel_id=1, source_target_pairs={{0,416},{128,0},{256,128},{384,256},{32,384},{160,32},{288,160},{4... | collective-permute-start | bytes 786440 | tf_op jit(solution)/shard_map/ppermute | solution.py:108
  16.3 4.9 %collective-permute-start.1 = (bf16[1,1,256]{2,1,0:T(2,128)(2,1)S(1)}, bf16[1,1,256]{2,1,0:T(2,128)(2,1)S(1)}, u32[]{:S(2)}, u32[]{:S(2)}) collective-permute-start(bf16[1,1,256]{2,1,0:T(2,128)(2,1)S(1)} %slice.309), channel_id=1, source_target_pairs={{0,9},{1,10},{2,11},{3,12},{4,13},{5,14},{6,15},{8,17},{9,18},{10,... | collective-permute-start | bytes 1544 | tf_op jit(solution)/shard_map/ppermute | solution.py:81
  21.9 3.1 %collective-permute-start = (bf16[1,24,256]{2,1,0:T(8,128)(2,1)S(1)}, bf16[1,24,256]{2,1,0:T(8,128)(2,1)S(1)}, u32[]{:S(2)}, u32[]{:S(2)}) collective-permute-start(bf16[1,24,256]{2,1,0:T(8,128)(2,1)S(1)} %slice_bitcast_fusion.6), channel_id=1, source_target_pairs={{0,8},{8,16},{16,24},{24,32},{32,40},{40,48},{48,56},{1,9},{9,17},... | collective-permute-start | bytes 36872 | tf_op jit(solution)/shard_map/ppermute | solution.py:79
  30.5 4.0 %collective-permute-start.2 = (bf16[24,1,256]{2,1,0:T(2,128)(2,1)S(1)}, bf16[24,1,256]{2,1,0:T(2,128)(2,1)S(1)}, u32[]{:S(2)}, u32[]{:S(2)}) collective-permute-start(bf16[24,1,256]{2,1,0:T(2,128)(2,1)S(1)} %slice.311), channel_id=1, source_target_pairs={{0,1},{1,2},{2,3},{3,4},{4,5},{5,6},{6,7},{8,9},{9,10},{10,11},{11... | collective-permute-start | bytes 36872 | tf_op jit(solution)/shard_map/ppermute | solution.py:80
  35.4 4.4 %collective-permute-start.5 = (bf16[128,512]{1,0:T(8,128)(2,1)S(1)}, bf16[128,512]{1,0:T(8,128)(2,1)S(1)}, u32[]{:S(2)}, u32[]{:S(2)}) collective-permute-start(bf16[128,512]{1,0:T(8,128)(2,1)S(1)} %maximum_maximum_fusion.2), channel_id=1, source_target_pairs={{0,288},{128,416},{256,0},{384,128},{32,256},{160,384},{288,32},{4... | collective-permute-start | bytes 393224 | tf_op jit(solution)/shard_map/ppermute | solution.py:110
  40.0 2.2 fusion.69
  42.2 2.1 fusion.71
  44.5 5.7 %collective-permute-start.7 = (bf16[4,256,512]{2,1,0:T(8,128)(2,1)S(1)}, bf16[4,256,512]{2,1,0:T(8,128)(2,1)S(1)}, u32[]{:S(2)}, u32[]{:S(2)}) collective-permute-start(bf16[4,256,512]{2,1,0:T(8,128)(2,1)S(1)} %pad_maximum_fusion.2), channel_id=1, source_target_pairs={{0,64},{64,0},{1,65},{65,1},{2,66},{66,2},{3,67},{67,3},{4,68},{68... | collective-permute-start | bytes 3145736 | tf_op jit(solution)/shard_map/ppermute | solution.py:91
  51.8 1.9 fusion.23
  57.0 2.3 gather_fusion
  63.1 2.4 fusion.10
  66.4 16.0 %all-to-all-start = ((bf16[64,24,128]{2,1,0:T(8,128)(2,1)}), bf16[64,24,128]{2,1,0:T(8,128)(2,1)S(1)}, u32[]{:S(2)}, u32[]{:S(2)}) async-start(bf16[64,24,128]{2,1,0:T(8,128)(2,1)} %bitcast.37), calls=%async_computation | async-start | bytes 786432 | tf_op jit(solution)/shard_map/all_to_all | solution.py:95
  83.0 15.2 %all-to-all-done = bf16[64,24,128]{2,1,0:T(8,128)(2,1)S(1)} async-done(((bf16[64,24,128]{2,1,0:T(8,128)(2,1)}), bf16[64,24,128]{2,1,0:T(8,128)(2,1)S(1)}, u32[]{:S(2)}, u32[]{:S(2)}) %all-to-all-start) | async-done | bytes 393248 | tf_op jit(solution)/shard_map/all_to_all | solution.py:95
  99.0 6.3 %attention.1 = bf16[8,192,128]{2,1,0:T(8,128)(2,1)} custom-call(bf16[8,192,128]{2,1,0:T(8,128)(2,1)} %bitcast.290, bf16[192,192]{1,0:T(8,128)(2,1)} %constant.230.clone.order_ref, f32[1,192]{1,0:T(1,128)} %or_convert_fusion.valid_ref), custom_call_target="tpu_custom_call" | custom-call | flops 500000000 | bytes 1000000 | tf_op jit(solution)/shard_map/attention/pallas_call | solution.py:184
  105.3 9.0 %all-to-all-start.1 = ((bf16[64,24,128]{2,1,0:T(8,128)(2,1)}), bf16[64,24,128]{2,1,0:T(8,128)(2,1)S(1)}, u32[]{:S(2)}, u32[]{:S(2)}) async-start(bf16[64,24,128]{2,1,0:T(8,128)(2,1)} %bitcast.289), calls=%async_computation.1 | async-start | bytes 786432 | tf_op jit(solution)/shard_map/all_to_all | solution.py:95
  114.9 14.7 %all-to-all-done.1 = bf16[64,24,128]{2,1,0:T(8,128)(2,1)S(1)} async-done(((bf16[64,24,128]{2,1,0:T(8,128)(2,1)}), bf16[64,24,128]{2,1,0:T(8,128)(2,1)S(1)}, u32[]{:S(2)}, u32[]{:S(2)}) %all-to-all-start.1) | async-done | bytes 393248 | tf_op jit(solution)/shard_map/all_to_all | solution.py:95
  129.6 2.6 convolution_convert_fusion
  145.5 2.0 reshape.617
  148.9 2.5 fusion.57
  162.5 6.6 %collective-permute-start.11 = (bf16[256,24,128]{2,1,0:T(8,128)(2,1)S(1)}, bf16[256,24,128]{2,1,0:T(8,128)(2,1)S(1)}, u32[]{:S(2)}, u32[]{:S(2)}) collective-permute-start(bf16[256,24,128]{2,1,0:T(8,128)(2,1)S(1)} %pad_maximum_fusion.1), channel_id=1, source_target_pairs={{0,64},{64,0},{1,65},{65,1},{2,66},{66,2},{3,67},{67,3},{4,68},{68... | collective-permute-start | bytes 4718600 | tf_op jit(solution)/shard_map/ppermute | solution.py:91
  169.1 2.8 collective-permute-done.11
  173.5 21.6 %all-to-all-start.2 = ((bf16[256,24,128]{2,1,0:T(8,128)(2,1)}), bf16[256,24,128]{2,1,0:T(8,128)(2,1)S(1)}, u32[]{:S(2)}, u32[]{:S(2)}) async-start(bf16[256,24,128]{2,1,0:T(8,128)(2,1)} %add_convert_fusion), calls=%async_computation.2 | async-start | bytes 3145728 | tf_op jit(solution)/shard_map/all_to_all | solution.py:95
  198.3 38.2 %all-to-all-done.2 = bf16[256,24,128]{2,1,0:T(8,128)(2,1)S(1)} async-done(((bf16[256,24,128]{2,1,0:T(8,128)(2,1)}), bf16[256,24,128]{2,1,0:T(8,128)(2,1)S(1)}, u32[]{:S(2)}, u32[]{:S(2)}) %all-to-all-start.2) | async-done | bytes 1572896 | tf_op jit(solution)/shard_map/all_to_all | solution.py:95
  237.6 6.2 %all-to-all-start.3 = ((bf16[64,24,128]{2,1,0:T(8,128)(2,1)}), bf16[64,24,128]{2,1,0:T(8,128)(2,1)S(1)}, u32[]{:S(2)}, u32[]{:S(2)}) async-start(bf16[64,24,128]{2,1,0:T(8,128)(2,1)} %broadcast_in_dim.124), calls=%async_computation.3 | async-start | bytes 786432 | tf_op jit(solution)/shard_map/all_to_all | solution.py:95
  245.6 13.2 %all-to-all-done.3 = bf16[64,24,128]{2,1,0:T(8,128)(2,1)S(1)} async-done(((bf16[64,24,128]{2,1,0:T(8,128)(2,1)}), bf16[64,24,128]{2,1,0:T(8,128)(2,1)S(1)}, u32[]{:S(2)}, u32[]{:S(2)}) %all-to-all-start.3) | async-done | bytes 393248 | tf_op jit(solution)/shard_map/all_to_all | solution.py:95
  258.8 9.5 %collective-permute-start.13 = (bf16[64,8,128]{2,1,0:T(8,128)(2,1)S(1)}, bf16[64,8,128]{2,1,0:T(8,128)(2,1)S(1)}, u32[]{:S(2)}, u32[]{:S(2)}) collective-permute-start(bf16[64,8,128]{2,1,0:T(8,128)(2,1)S(1)} %get-tuple-element.47), channel_id=1, source_target_pairs={{0,256},{128,384},{256,32},{384,160},{32,288},{160,416},{288,0},{4... | collective-permute-start | bytes 393224 | tf_op jit(solution)/shard_map/ppermute | solution.py:253
  268.3 2.7 collective-permute-start.12
  271.0 2.6 collective-permute-start.14
  276.0 1.9 collective-permute-done.14
  278.0 4.5 %collective-permute-start.15 = (bf16[4,64,8,128]{3,2,1,0:T(8,128)(2,1)S(1)}, bf16[4,64,8,128]{3,2,1,0:T(8,128)(2,1)S(1)}, u32[]{:S(2)}, u32[]{:S(2)}) collective-permute-start(bf16[4,64,8,128]{3,2,1,0:T(8,128)(2,1)S(1)} %pad_maximum_fusion.4), channel_id=1, source_target_pairs={{0,64},{64,0},{1,65},{65,1},{2,66},{66,2},{3,67},{67,3},{4,68},{68... | collective-permute-start | bytes 1572872 | tf_op jit(solution)/shard_map/ppermute | solution.py:91
  (316 shorter events, 62.4 us)
Async XLA Ops:
  0.6 39.3 %copy-start = (bf16[256,1024]{1,0:T(8,128)(2,1)S(1)}, bf16[256,1024]{1,0:T(8,128)(2,1)}, u32[]{:S(2)}) copy-start(bf16[256,1024]{1,0:T(8,128)(2,1)} %param.12) | copy-start | bytes 1572868
  0.6 43.7 %collective-permute-start.4 = (bf16[128,512]{1,0:T(8,128)(2,1)}, bf16[128,512]{1,0:T(8,128)(2,1)S(1)}, u32[]{:S(2)}, u32[]{:S(2)}) collective-permute-start(bf16[128,512]{1,0:T(8,128)(2,1)} %param.15), channel_id=1, source_target_pairs={{0,256},{128,384},{256,32},{384,160},{32,288},{160,416},{288,0},{4... | collective-permute-start | bytes 393224 | tf_op jit(solution)/shard_map/ppermute | solution.py:110
  9.1 35.3 %collective-permute-start.6 = (bf16[256,512]{1,0:T(8,128)(2,1)S(1)}, bf16[256,512]{1,0:T(8,128)(2,1)S(1)}, u32[]{:S(2)}, u32[]{:S(2)}) collective-permute-start(bf16[256,512]{1,0:T(8,128)(2,1)S(1)} %get-tuple-element.25), channel_id=1, source_target_pairs={{0,128},{128,256},{256,384},{384,32},{32,160},{160,288},{288,416},... | collective-permute-start | bytes 786440 | tf_op jit(solution)/shard_map/ppermute | solution.py:107
  12.3 32.1 %collective-permute-start.3 = (bf16[256,512]{1,0:T(8,128)(2,1)S(1)}, bf16[256,512]{1,0:T(8,128)(2,1)S(1)}, u32[]{:S(2)}, u32[]{:S(2)}) collective-permute-start(bf16[256,512]{1,0:T(8,128)(2,1)S(1)} %get-tuple-element.25), channel_id=1, source_target_pairs={{0,416},{128,0},{256,128},{384,256},{32,384},{160,32},{288,160},{4... | collective-permute-start | bytes 786440 | tf_op jit(solution)/shard_map/ppermute | solution.py:108
  16.3 23.7 %collective-permute-start.1 = (bf16[1,1,256]{2,1,0:T(2,128)(2,1)S(1)}, bf16[1,1,256]{2,1,0:T(2,128)(2,1)S(1)}, u32[]{:S(2)}, u32[]{:S(2)}) collective-permute-start(bf16[1,1,256]{2,1,0:T(2,128)(2,1)S(1)} %slice.309), channel_id=1, source_target_pairs={{0,9},{1,10},{2,11},{3,12},{4,13},{5,14},{6,15},{8,17},{9,18},{10,... | collective-permute-start | bytes 1544 | tf_op jit(solution)/shard_map/ppermute | solution.py:81
  21.9 8.6 %collective-permute-start = (bf16[1,24,256]{2,1,0:T(8,128)(2,1)S(1)}, bf16[1,24,256]{2,1,0:T(8,128)(2,1)S(1)}, u32[]{:S(2)}, u32[]{:S(2)}) collective-permute-start(bf16[1,24,256]{2,1,0:T(8,128)(2,1)S(1)} %slice_bitcast_fusion.6), channel_id=1, source_target_pairs={{0,8},{8,16},{16,24},{24,32},{32,40},{40,48},{48,56},{1,9},{9,17},... | collective-permute-start | bytes 36872 | tf_op jit(solution)/shard_map/ppermute | solution.py:79
  28.4 23.4 %copy-start.48 = (f32[1,1,1024]{2,1,0:T(1,128)}, f32[1,1,1024]{2,1,0:T(1,128)S(1)}, u32[]{:S(2)}) copy-start(f32[1,1,1024]{2,1,0:T(1,128)S(1)} %get-tuple-element.61) | copy-start | bytes 12292
  28.4 23.4 %copy-start.50 = (f32[1,1,1024]{2,1,0:T(1,128)}, f32[1,1,1024]{2,1,0:T(1,128)S(1)}, u32[]{:S(2)}) copy-start(f32[1,1,1024]{2,1,0:T(1,128)S(1)} %get-tuple-element.63) | copy-start | bytes 12292
  28.4 23.4 %copy-start.52 = (f32[1,1,1024]{2,1,0:T(1,128)}, f32[1,1,1024]{2,1,0:T(1,128)S(1)}, u32[]{:S(2)}) copy-start(f32[1,1,1024]{2,1,0:T(1,128)S(1)} %get-tuple-element.65) | copy-start | bytes 12292
  28.4 23.4 %copy-start.60 = (f32[1,1,1024]{2,1,0:T(1,128)}, f32[1,1,1024]{2,1,0:T(1,128)S(1)}, u32[]{:S(2)}) copy-start(f32[1,1,1024]{2,1,0:T(1,128)S(1)} %get-tuple-element.60) | copy-start | bytes 12292
  28.4 23.4 %copy-start.62 = (f32[1,1,1024]{2,1,0:T(1,128)}, f32[1,1,1024]{2,1,0:T(1,128)S(1)}, u32[]{:S(2)}) copy-start(f32[1,1,1024]{2,1,0:T(1,128)S(1)} %get-tuple-element.62) | copy-start | bytes 12292
  28.4 23.4 %copy-start.64 = (f32[1,1,1024]{2,1,0:T(1,128)}, f32[1,1,1024]{2,1,0:T(1,128)S(1)}, u32[]{:S(2)}) copy-start(f32[1,1,1024]{2,1,0:T(1,128)S(1)} %get-tuple-element.64) | copy-start | bytes 12292
  29.3 22.5 %copy-start.42 = (bf16[12,12,256]{2,1,0:T(8,128)(2,1)}, bf16[12,12,256]{2,1,0:T(8,128)(2,1)S(1)}, u32[]{:S(2)}) copy-start(bf16[12,12,256]{2,1,0:T(8,128)(2,1)S(1)} %get-tuple-element.48) | copy-start | bytes 221188
  30.5 4.9 %collective-permute-start.2 = (bf16[24,1,256]{2,1,0:T(2,128)(2,1)S(1)}, bf16[24,1,256]{2,1,0:T(2,128)(2,1)S(1)}, u32[]{:S(2)}, u32[]{:S(2)}) collective-permute-start(bf16[24,1,256]{2,1,0:T(2,128)(2,1)S(1)} %slice.311), channel_id=1, source_target_pairs={{0,1},{1,2},{2,3},{3,4},{4,5},{5,6},{6,7},{8,9},{9,10},{10,11},{11... | collective-permute-start | bytes 36872 | tf_op jit(solution)/shard_map/ppermute | solution.py:80
  35.4 8.9 %collective-permute-start.5 = (bf16[128,512]{1,0:T(8,128)(2,1)S(1)}, bf16[128,512]{1,0:T(8,128)(2,1)S(1)}, u32[]{:S(2)}, u32[]{:S(2)}) collective-permute-start(bf16[128,512]{1,0:T(8,128)(2,1)S(1)} %maximum_maximum_fusion.2), channel_id=1, source_target_pairs={{0,288},{128,416},{256,0},{384,128},{32,256},{160,384},{288,32},{4... | collective-permute-start | bytes 393224 | tf_op jit(solution)/shard_map/ppermute | solution.py:110
  44.5 11.5 %collective-permute-start.7 = (bf16[4,256,512]{2,1,0:T(8,128)(2,1)S(1)}, bf16[4,256,512]{2,1,0:T(8,128)(2,1)S(1)}, u32[]{:S(2)}, u32[]{:S(2)}) collective-permute-start(bf16[4,256,512]{2,1,0:T(8,128)(2,1)S(1)} %pad_maximum_fusion.2), channel_id=1, source_target_pairs={{0,64},{64,0},{1,65},{65,1},{2,66},{66,2},{3,67},{67,3},{4,68},{68... | collective-permute-start | bytes 3145736 | tf_op jit(solution)/shard_map/ppermute | solution.py:91
  66.4 31.9 %all-to-all-start = ((bf16[64,24,128]{2,1,0:T(8,128)(2,1)}), bf16[64,24,128]{2,1,0:T(8,128)(2,1)S(1)}, u32[]{:S(2)}, u32[]{:S(2)}) async-start(bf16[64,24,128]{2,1,0:T(8,128)(2,1)} %bitcast.37), calls=%async_computation | async-start | bytes 786432 | tf_op jit(solution)/shard_map/all_to_all | solution.py:95
  105.3 24.3 %all-to-all-start.1 = ((bf16[64,24,128]{2,1,0:T(8,128)(2,1)}), bf16[64,24,128]{2,1,0:T(8,128)(2,1)S(1)}, u32[]{:S(2)}, u32[]{:S(2)}) async-start(bf16[64,24,128]{2,1,0:T(8,128)(2,1)} %bitcast.289), calls=%async_computation.1 | async-start | bytes 786432 | tf_op jit(solution)/shard_map/all_to_all | solution.py:95
  140.8 11.9 %collective-permute-start.10 = (bf16[1,1,1024]{2,1,0:T(2,128)(2,1)}, bf16[1,1,1024]{2,1,0:T(2,128)(2,1)}, u32[]{:S(2)}, u32[]{:S(2)}) collective-permute-start(bf16[1,1,1024]{2,1,0:T(2,128)(2,1)} %slice.344), channel_id=1, source_target_pairs={{9,0},{10,1},{11,2},{12,3},{13,4},{14,5},{15,6},{17,8},{18,9},{19,... | collective-permute-start | bytes 6152 | tf_op jit(solution)/shard_map/ppermute | solution.py:81
  142.2 10.2 %collective-permute-start.8 = (bf16[1,12,1024]{2,1,0:T(8,128)(2,1)}, bf16[1,12,1024]{2,1,0:T(8,128)(2,1)S(1)}, u32[]{:S(2)}, u32[]{:S(2)}) collective-permute-start(bf16[1,12,1024]{2,1,0:T(8,128)(2,1)} %slice.339), channel_id=1, source_target_pairs={{8,0},{16,8},{24,16},{32,24},{40,32},{48,40},{56,48},{9,1},{17,9},... | collective-permute-start | bytes 73736 | tf_op jit(solution)/shard_map/ppermute | solution.py:79
  143.5 9.2 %collective-permute-start.9 = (bf16[12,1,1024]{2,1,0:T(2,128)(2,1)S(1)}, bf16[12,1,1024]{2,1,0:T(2,128)(2,1)S(1)}, u32[]{:S(2)}, u32[]{:S(2)}) collective-permute-start(bf16[12,1,1024]{2,1,0:T(2,128)(2,1)S(1)} %slice.343), channel_id=1, source_target_pairs={{1,0},{2,1},{3,2},{4,3},{5,4},{6,5},{7,6},{9,8},{10,9},{11,10},{12... | collective-permute-start | bytes 73736 | tf_op jit(solution)/shard_map/ppermute | solution.py:80
  162.5 9.4 %collective-permute-start.11 = (bf16[256,24,128]{2,1,0:T(8,128)(2,1)S(1)}, bf16[256,24,128]{2,1,0:T(8,128)(2,1)S(1)}, u32[]{:S(2)}, u32[]{:S(2)}) collective-permute-start(bf16[256,24,128]{2,1,0:T(8,128)(2,1)S(1)} %pad_maximum_fusion.1), channel_id=1, source_target_pairs={{0,64},{64,0},{1,65},{65,1},{2,66},{66,2},{3,67},{67,3},{4,68},{68... | collective-permute-start | bytes 4718600 | tf_op jit(solution)/shard_map/ppermute | solution.py:91
  173.5 23.7 %copy-start.22 = (bf16[12,16,1024]{2,1,0:T(8,128)(2,1)S(1)}, bf16[12,16,1024]{2,1,0:T(8,128)(2,1)}, u32[]{:S(2)}) copy-start(bf16[12,16,1024]{2,1,0:T(8,128)(2,1)} %copy-done.21) | copy-start | bytes 1179652
  173.5 24.1 %copy-start.20 = (bf16[12,16,1024]{2,1,0:T(8,128)(2,1)S(1)}, bf16[12,16,1024]{2,1,0:T(8,128)(2,1)}, u32[]{:S(2)}) copy-start(bf16[12,16,1024]{2,1,0:T(8,128)(2,1)} %copy-done.19) | copy-start | bytes 1179652
  173.5 62.9 %all-to-all-start.2 = ((bf16[256,24,128]{2,1,0:T(8,128)(2,1)}), bf16[256,24,128]{2,1,0:T(8,128)(2,1)S(1)}, u32[]{:S(2)}, u32[]{:S(2)}) async-start(bf16[256,24,128]{2,1,0:T(8,128)(2,1)} %add_convert_fusion), calls=%async_computation.2 | async-start | bytes 3145728 | tf_op jit(solution)/shard_map/all_to_all | solution.py:95
  197.9 45.9 %copy-start.16 = (bf16[12,16,1024]{2,1,0:T(8,128)(2,1)S(1)}, bf16[12,16,1024]{2,1,0:T(8,128)(2,1)}, u32[]{:S(2)}) copy-start(bf16[12,16,1024]{2,1,0:T(8,128)(2,1)} %copy-done.15) | copy-start | bytes 1179652
  198.3 45.9 %copy-start.29 = (f32[12,16,256]{2,1,0:T(8,128)S(1)}, f32[12,16,256]{2,1,0:T(8,128)}, u32[]{:S(2)}) copy-start(f32[12,16,256]{2,1,0:T(8,128)} %convolution_multiply_fusion.1) | copy-start | bytes 589828
  237.6 21.2 %all-to-all-start.3 = ((bf16[64,24,128]{2,1,0:T(8,128)(2,1)}), bf16[64,24,128]{2,1,0:T(8,128)(2,1)S(1)}, u32[]{:S(2)}, u32[]{:S(2)}) async-start(bf16[64,24,128]{2,1,0:T(8,128)(2,1)} %broadcast_in_dim.124), calls=%async_computation.3 | async-start | bytes 786432 | tf_op jit(solution)/shard_map/all_to_all | solution.py:95
  258.8 17.2 %collective-permute-start.13 = (bf16[64,8,128]{2,1,0:T(8,128)(2,1)S(1)}, bf16[64,8,128]{2,1,0:T(8,128)(2,1)S(1)}, u32[]{:S(2)}, u32[]{:S(2)}) collective-permute-start(bf16[64,8,128]{2,1,0:T(8,128)(2,1)S(1)} %get-tuple-element.47), channel_id=1, source_target_pairs={{0,256},{128,384},{256,32},{384,160},{32,288},{160,416},{288,0},{4... | collective-permute-start | bytes 393224 | tf_op jit(solution)/shard_map/ppermute | solution.py:253
  268.3 7.7 %collective-permute-start.12 = (bf16[64,8,128]{2,1,0:T(8,128)(2,1)S(1)}, bf16[64,8,128]{2,1,0:T(8,128)(2,1)S(1)}, u32[]{:S(2)}, u32[]{:S(2)}) collective-permute-start(bf16[64,8,128]{2,1,0:T(8,128)(2,1)S(1)} %get-tuple-element.47), channel_id=1, source_target_pairs={{0,416},{128,0},{256,128},{384,256},{32,384},{160,32},{288,160},{4... | collective-permute-start | bytes 393224 | tf_op jit(solution)/shard_map/ppermute | solution.py:253
  271.0 6.9 %collective-permute-start.14 = (bf16[64,8,128]{2,1,0:T(8,128)(2,1)S(1)}, bf16[64,8,128]{2,1,0:T(8,128)(2,1)S(1)}, u32[]{:S(2)}, u32[]{:S(2)}) collective-permute-start(bf16[64,8,128]{2,1,0:T(8,128)(2,1)S(1)} %get-tuple-element.47), channel_id=1, source_target_pairs={{0,128},{128,256},{256,384},{384,32},{32,160},{160,288},{288,416},... | collective-permute-start | bytes 393224 | tf_op jit(solution)/shard_map/ppermute | solution.py:253
  278.0 6.0 %collective-permute-start.15 = (bf16[4,64,8,128]{3,2,1,0:T(8,128)(2,1)S(1)}, bf16[4,64,8,128]{3,2,1,0:T(8,128)(2,1)S(1)}, u32[]{:S(2)}, u32[]{:S(2)}) collective-permute-start(bf16[4,64,8,128]{3,2,1,0:T(8,128)(2,1)S(1)} %pad_maximum_fusion.4), channel_id=1, source_target_pairs={{0,64},{64,0},{1,65},{65,1},{2,66},{66,2},{3,67},{67,3},{4,68},{68... | collective-permute-start | bytes 1572872 | tf_op jit(solution)/shard_map/ppermute | solution.py:91
  (63 other events, 267.2 us)

commit v3 on v2

v3 whole, which is shorter than its diff:
```python
import math

import jax
import jax.numpy as jnp
import numpy as np
from jax import lax
from jax.experimental import pallas as pl
from jax.experimental.pallas import tpu as pltpu
from jax.sharding import Mesh
from jax.sharding import PartitionSpec as P

HEADS = 8
PARTS = 8

SAMPLE = ("ylo", "core")
ROW = ("yhi", "x")
COL = "z"
GRID_AXES = ("yhi", "x", "z")
CHIPS = ("ylo", "yhi", "x", "z")
RING = ("ylo", "yhi")

norm_epsilon = 1e-05
tanh_coeff = 0.7978845608028654
cubic_coeff = 0.044715

bf16 = jnp.bfloat16
f32 = jnp.float32


def gelu_both(values):
    inner = jnp.tanh(tanh_coeff * (values + cubic_coeff * values * values * values))
    value = 0.5 * values * (1.0 + inner)
    slope = 0.5 * (1.0 + inner) + 0.5 * values * (1.0 - inner * inner) * tanh_coeff * (
        1.0 + 3.0 * cubic_coeff * values * values
    )
    return value, slope


def dot(left, right):
    return lax.dot_general(
        left, right, (((left.ndim - 1,), (0,)), ((), ())), preferred_element_type=f32
    )


def dot_t(left, right):
    return lax.dot_general(
        left, right, (((left.ndim - 1,), (1,)), ((), ())), preferred_element_type=f32
    )


def dot_tt(left, right):
    return lax.dot_general(left, right, (((0,), (0,)), ((), ())), preferred_element_type=f32)


def outer_sum(left, right):
    return lax.dot_general(
        left.reshape(-1, left.shape[-1]),
        right.reshape(-1, right.shape[-1]),
        (((0,), (0,)), ((), ())),
        preferred_element_type=f32,
    )


def step_route(count, distance):
    return [(i - distance, i) for i in range(count) if 0 <= i - distance < count]


def row_rim(edge, distance):
    return lax.ppermute(edge, ROW, step_route(PARTS, distance))


def col_rim(edge, distance):
    return lax.ppermute(edge, COL, step_route(PARTS, distance))


def around(distance):
    place = [y % 4 * 2 + y // 4 for y in range(8)]
    return [(place[y], place[(y + distance) % 8]) for y in range(8)]


def swap_cores(block):
    return lax.ppermute(block, "core", [(0, 1), (1, 0)])


def exchange(block, axes):
    return lax.all_to_all(block, axes, 0, 0, tiled=True)


def spread(block, axes, count):
    return exchange(jnp.broadcast_to(block[None], (count,) + block.shape), axes)


def gather_weights(w_proj, w_qkv, w_out):
    tail = w_qkv[:, 512:]
    own = jnp.concatenate(
        [w_proj, w_qkv[:, :512], w_out, jnp.concatenate([tail[:32], tail[32:]], axis=1)], axis=0
    )
    below = lax.ppermute(own, RING, around(1))
    above = lax.ppermute(own, RING, around(7))
    far = lax.ppermute(own, RING, around(2))
    ring = jnp.stack([own, above, far, below])
    return ring, swap_cores(ring)


def head_order():
    target = np.arange(1024)
    wanted = target // 32 % 4 * 256 + target // 128 * 32 + target % 32
    return jnp.asarray(target[:, None] == wanted[None, :], bf16)


def slot_order():
    target = np.arange(192)
    both = []
    for odd in range(2):
        group = (target // 24 + odd * 4) % 8
        wanted = target // 2 % 12 * 16 + target % 2 * 8 + group
        both.append(target[None, :] == wanted[:, None])
    both = jnp.asarray(np.stack(both), bf16)
    return lax.dynamic_index_in_dim(both, lax.axis_index("z") % 2, 0, keepdims=False)


def row_order():
    target = np.arange(192)
    wanted = target // 2 % 8 * 24 + target // 16 * 2 + target % 2
    return jnp.asarray(target[None, :] == wanted[:, None], bf16)


def dot_kt(left, right):
    return lax.dot_general(left, right, (((1,), (1,)), ((), ())), preferred_element_type=f32)


def attention_kernel(slots_ref, order_ref, valid_ref, out_ref, sorted_ref, result_ref):
    scale = 1.0 / math.sqrt(32)
    order = order_ref[...]
    valid = valid_ref[...] > 0.0
    for part in range(8):
        sorted_ref[part * 192 : part * 192 + 192] = dot(order, slots_ref[part]).astype(bf16)
    for group in range(8):
        blocks = [row * 16 for row in range(96) if row % 8 == group]
        unit = jnp.concatenate([sorted_ref[at : at + 16] for at in blocks], axis=0)
        query, key, value, d_mix = (unit[:, 32 * i : 32 * i + 32] for i in range(4))
        raised = jnp.where(valid, jnp.exp(dot_kt(query, key) * scale), 0.0)
        weights32 = raised / jnp.sum(raised, axis=-1, keepdims=True)
        weights = weights32.astype(bf16)
        mixture = dot(weights, value)
        d_weights = dot_kt(d_mix, value)
        d_value = dot_tt(weights, d_mix)
        d_scores = (
            weights32 * (d_weights - jnp.sum(weights32 * d_weights, axis=-1, keepdims=True))
        ).astype(bf16)
        d_query = dot(d_scores, key) * scale
        d_key = dot_tt(d_scores, query) * scale
        result = jnp.concatenate([d_query, d_key, d_value, mixture], axis=-1).astype(bf16)
        for index, at in enumerate(blocks):
            result_ref[at : at + 16] = result[index * 16 : index * 16 + 16]
    for part in range(8):
        out_ref[part] = dot_tt(order, result_ref[part * 192 : part * 192 + 192]).astype(bf16)


def attention(slots):
    slot = lax.broadcasted_iota(jnp.int32, (1, 192), 1)
    high = (lax.axis_index("z") >= 4).astype(jnp.int32)
    valid = ((slot % 2 == 0) | (slot // 2 % 2 == high)).astype(f32)
    return pl.pallas_call(
        attention_kernel,
        out_shape=jax.ShapeDtypeStruct((8, 192, 128), bf16),
        scratch_shapes=[pltpu.VMEM((1536, 128), bf16), pltpu.VMEM((1536, 128), bf16)],
        cost_estimate=pl.CostEstimate(
            flops=500_000_000, bytes_accessed=1_000_000, transcendentals=300_000
        ),
        name="attention",
    )(slots, row_order(), valid)


def token_mask():
    return lax.broadcasted_iota(jnp.int32, (192, 1), 0) % 16 < 12


def normalize(section):
    wide = section.astype(f32)
    centred = wide - jnp.mean(wide, axis=-1, keepdims=True)
    inv_std = lax.rsqrt(jnp.mean(centred * centred, axis=-1, keepdims=True) + norm_epsilon)
    return centred * inv_std, inv_std


def call(body, name, out_shape, flops, scratch=(), **rest):
    return pl.pallas_call(
        body,
        out_shape=out_shape,
        scratch_shapes=scratch,
        compiler_params=pltpu.CompilerParams(vmem_limit_bytes=40 * 1024 * 1024),
        cost_estimate=pl.CostEstimate(flops=flops, bytes_accessed=8_000_000, transcendentals=0),
        name=name,
        **rest,
    )


def section_kernel(
    spot_ref, ring_ref, other_ref, activated_ref, pooled_ref, short_ref, cotangent_ref, heads_ref,
    slots_ref, pieces_ref, section_ref, normed_ref, proj_ref, qkv_ref, out_ref,
):
    core, y_lo = spot_ref[0], spot_ref[1]

    def place(shard, source, at):
        proj_ref[shard * 128 : shard * 128 + 128] = source[at, 0:128]
        qkv_ref[shard * 64 : shard * 64 + 64, 0:512] = source[at, 128:192]
        out_ref[shard * 32 : shard * 32 + 32] = source[at, 192:224]
        qkv_ref[shard * 64 : shard * 64 + 32, 512:768] = source[at, 224:256, 0:256]
        qkv_ref[shard * 64 + 32 : shard * 64 + 64, 512:768] = source[at, 224:256, 256:512]

    for shard in range(8):
        at = lax.rem(shard // 2 - y_lo + 4, 4)
        pl.when(core == shard % 2)(lambda: place(shard, ring_ref, at))
        pl.when(core != shard % 2)(lambda: place(shard, other_ref, at))
    section = (
        dot(activated_ref[...], proj_ref[...]) + dot(pooled_ref[...], short_ref[...])
    ).astype(bf16)
    section_ref[...] = section
    normed = jnp.where(token_mask(), normalize(section)[0], 0.0).astype(bf16)
    normed_ref[...] = normed
    packed = dot(normed, qkv_ref[...]).astype(bf16)
    d_mixture = dot_kt(cotangent_ref[...], out_ref[...]).astype(bf16)
    tokens = jnp.concatenate([packed, d_mixture], axis=1)
    tokens = dot(slots_ref[...], dot(tokens, heads_ref[...]).astype(bf16)).astype(bf16)
    for head in range(HEADS):
        pieces_ref[head] = tokens[:, head * 128 : head * 128 + 128]


def section_step(spot, ring, other, activated, pooled, w_short, cotangent, heads, slots):
    shapes = [(8, 192, 128), (192, 512), (192, 512), (1024, 512), (512, 768), (256, 512)]
    return call(
        section_kernel,
        "section",
        [jax.ShapeDtypeStruct(shape, bf16) for shape in shapes],
        1_500_000_000,
        in_specs=[pl.BlockSpec(memory_space=pltpu.SMEM)]
        + [pl.BlockSpec(memory_space=pltpu.VMEM)] * 8,
    )(spot, ring, other, activated, pooled, w_short, cotangent, heads, slots)[:5]


def back_kernel(
    got_ref, heads_ref, slots_ref, section_ref, cotangent_ref, proj_ref, qkv_ref, slope_ref,
    results_ref, d_section_ref, d_conv_ref,
):
    used = token_mask()
    got = jnp.concatenate([got_ref[head] for head in range(HEADS)], axis=1)
    results = dot_kt(dot_tt(slots_ref[...], got).astype(bf16), heads_ref[...])
    results = jnp.where(used, results, 0.0).astype(bf16)
    results_ref[...] = results
    normalized, inv_std = normalize(section_ref[...])
    d_normed = dot_kt(results[:, :768], qkv_ref[...])
    d_section = cotangent_ref[...].astype(f32) + inv_std * (
        d_normed
        - jnp.mean(d_normed, axis=-1, keepdims=True)
        - normalized * jnp.mean(d_normed * normalized, axis=-1, keepdims=True)
    )
    d_section = jnp.where(used, d_section, 0.0).astype(bf16)
    d_section_ref[...] = d_section
    d_activated = dot_kt(d_section, proj_ref[...])
    d_conv_ref[...] = (d_activated * slope_ref[...].astype(f32)).astype(bf16)


def back_step(*inputs):
    shapes = [(192, 1024), (192, 512), (192, 1024)]
    return call(
        back_kernel,
        "back",
        [jax.ShapeDtypeStruct(shape, bf16) for shape in shapes],
        1_200_000_000,
    )(*inputs)


def parts_kernel(
    results_ref, d_section_ref, normed_ref, cotangent_ref, activated_ref, pooled_ref, short_ref,
    matrix_ref, rest_ref, d_pooled_ref,
):
    results = results_ref[...]
    d_section = d_section_ref[...]

    def store(part, first, rows):
        lanes = part.shape[1] // 128
        for shard in range(8):
            for piece in range(rows // 16 * lanes):
                row = shard * rows + piece // lanes * 16
                lane = piece % lanes * 128
                index = first + piece
                at = shard // 2 * 32 + index % 2 * 16
                matrix_ref[shard % 2, index // 2, at : at + 16, :] = part[
                    row : row + 16, lane : lane + 128
                ]

    store(dot_tt(activated_ref[...], d_section).astype(bf16), 0, 128)
    store(dot_tt(normed_ref[...], results[:, :768]).astype(bf16), 32, 64)
    store(dot_tt(results[:, 768:], cotangent_ref[...]).astype(bf16), 56, 32)
    short = dot_tt(pooled_ref[...], d_section)
    rows = [short[:, lane * 128 : lane * 128 + 128].reshape(16, 2, 8, 128) for lane in range(4)]
    rest_ref[...] = jnp.concatenate(
        [rows[index % 4][:, index // 4] for index in range(8)], axis=1
    ).astype(bf16)
    d_pooled_ref[...] = dot_kt(d_section, short_ref[...]) * 0.25


def parts_step(*inputs):
    return call(
        parts_kernel,
        "parts",
        [
            jax.ShapeDtypeStruct((2, 32, 128, 128), bf16),
            jax.ShapeDtypeStruct((16, 64, 128), bf16),
            jax.ShapeDtypeStruct((192, 256), f32),
        ],
        600_000_000,
    )(*inputs)


def pixel_kernel(
    d_conv_ref, below_ref, right_ref, even_ref, odd_ref, slopes_ref, cells_ref, w_expand_ref,
    taps_ref, d_pooled_ref, image_ref, expand_ref, depth_ref, total_ref,
):
    step = pl.program_id(0)
    slot = lax.broadcasted_iota(jnp.int32, (1, 16, 1), 1)
    here = d_conv_ref[...].astype(f32).reshape(12, 16, 256)
    rows = jnp.concatenate([here, below_ref[...].astype(f32)], axis=0)
    turned = pltpu.roll(rows, 15, 1)
    after = jnp.where(slot == 11, right_ref[...].astype(f32), turned)
    back = turned[:12]
    taps = [[taps_ref[3 * a + b : 3 * a + b + 1, :].astype(f32) for b in range(3)] for a in range(3)]

    def window(row_tap, odd_col):
        source = even_ref if row_tap == 1 else odd_ref
        first = 16 * (row_tap // 2) if row_tap != 1 else 0
        return source[odd_col, first : first + 192, :].astype(f32).reshape(12, 16, 256)

    for a in range(3):
        odd = window(a, 1)
        even = window(a, 0)
        for b, product in ((0, odd * back), (1, even * here), (2, odd * here)):
            total = jnp.sum(jnp.sum(product, axis=0), axis=0, keepdims=True)
            depth_ref[3 * a + b : 3 * a + b + 1, :] = total
    row_terms = {0: ((1, 0),), 1: ((2, 0), (0, 1))}
    col_terms = {0: ((1, rows),), 1: ((2, rows), (0, after))}
    part_expand = 0.0
    for row in range(2):
        for col in range(2):
            d_cells = sum(
                source[i : i + 12] * taps[a][b]
                for a, i in row_terms[row]
                for b, source in col_terms[col]
            )
            d_cells = jnp.where(slot < 12, d_cells, 0.0).reshape(192, 256)
            plane = row * 2 + col
            d_pre = (d_cells * slopes_ref[plane].astype(f32)).astype(bf16)
            part_expand = part_expand + dot_tt(cells_ref[plane], d_pre)
            back_image = dot_kt(d_pre, w_expand_ref[...])

            @pl.when(step == 0)
            def _():
                total_ref[plane] = back_image + d_pooled_ref[...]

            @pl.when(step > 0)
            def _():
                total_ref[plane] += back_image

    expand_ref[...] = jnp.concatenate(
        [part_expand[:, :128].reshape(32, 8, 128), part_expand[:, 128:].reshape(32, 8, 128)],
        axis=1,
    ).astype(bf16)

    @pl.when(step == pl.num_programs(0) - 1)
    def _():
        image_ref[...] = total_ref[...].astype(bf16)


def pixel_step(*inputs):
    def chunk(*lead):
        return pl.BlockSpec(lead + (256,), lambda step: (0,) * len(lead) + (step,))

    def whole(*shape):
        return pl.BlockSpec(shape, lambda step: (0,) * len(shape))

    return call(
        pixel_kernel,
        "pixel",
        [
            jax.ShapeDtypeStruct((4, 192, 256), bf16),
            jax.ShapeDtypeStruct((32, 64, 128), bf16),
            jax.ShapeDtypeStruct((16, 1024), f32),
        ],
        1_200_000_000,
        scratch=[pltpu.VMEM((4, 192, 256), f32)],
        grid=(4,),
        in_specs=[
            chunk(192), chunk(1, 16), chunk(13, 1), chunk(2, 192), chunk(2, 208), chunk(4, 192),
            whole(4, 192, 256), chunk(256), chunk(16), whole(192, 256),
        ],
        out_specs=[
            whole(4, 192, 256),
            pl.BlockSpec((32, 16, 128), lambda step: (0, step, 0)),
            chunk(16),
        ],
    )(*inputs)


def untiled(pieces, rows, columns):
    height = pieces.shape[1]
    cut = pieces.reshape(rows // height, columns // 128, height, 128)
    return cut.transpose(0, 2, 1, 3).reshape(rows, columns).astype(f32)


def add_cores(halves, axis):
    core = lax.axis_index("core")
    mine = lax.dynamic_index_in_dim(halves, core, axis, keepdims=False)
    theirs = lax.dynamic_index_in_dim(halves, 1 - core, axis, keepdims=False)
    return mine, theirs


def all_sums(matrix, short, expand, depth):
    depth = depth[:9].astype(bf16).reshape(9, 8, 128)
    depth = jnp.pad(depth, ((0, 119), (0, 0), (0, 0))).reshape(16, 64, 128)
    short = jnp.concatenate([short, depth], axis=0)
    first = lax.axis_index("core") == 0
    mine, theirs = add_cores(matrix, 0)
    mine = jnp.concatenate([mine, jnp.where(first, expand, short)], axis=1)
    theirs = jnp.concatenate([theirs, jnp.where(first, short, expand)], axis=1)
    pair = (mine.astype(f32) + swap_cores(theirs).astype(f32)).astype(bf16)
    line = jnp.sum(exchange(pair, "x").reshape(4, 8, 192, 128).astype(f32), axis=0).astype(bf16)
    sheet = jnp.sum(exchange(line, "z").astype(f32), axis=0).astype(bf16)
    column = jnp.concatenate(
        [sheet[:128].reshape(4, 32, 128), jnp.broadcast_to(sheet[None, 128:], (4, 64, 128))], axis=1
    )
    column = jnp.broadcast_to(column[:, None], (4, 2, 96, 128)).reshape(8, 96, 128)
    grad_scale = 1.0 / math.sqrt(8 * 96 * 96)
    total = jnp.sum(exchange(column, RING).astype(f32), axis=0) * grad_scale
    near = spread(total.astype(bf16), ("x", "z"), 32)
    own = near[:, 32:].reshape(256, 8, 128)
    other = swap_cores(own)
    matrix = near[:, :32].reshape(64, 16, 128)
    grad_proj = untiled(matrix[:32], 128, 512)
    grad_qkv = untiled(matrix[32:56], 64, 768)
    grad_out = untiled(matrix[56:], 32, 512)
    low = jnp.where(first, own, other)
    high = jnp.where(first, other, own)
    grad_expand = untiled(low, 256, 1024)
    grad_short = untiled(high[:128], 256, 512)
    grad_depth = high[128:137].reshape(3, 3, 1024).astype(f32)
    return grad_expand, grad_depth, grad_short, grad_proj, grad_qkv, grad_out


def slots16(cells, last=None):
    rows, _, width = cells.shape
    if last is None:
        return jnp.pad(cells, ((0, 0), (0, 4), (0, 0)))
    return jnp.concatenate([cells, jnp.zeros((rows, 3, width), cells.dtype), last], axis=1)


def on_device(images, w_expand, w_depth, w_short, w_proj, w_qkv, w_out, cotangent):
    images = images[0]
    cotangent = slots16(cotangent[0])
    ring, other = gather_weights(w_proj, w_qkv, w_out)
    top = row_rim(images[-1:], 1)
    left = col_rim(jnp.concatenate([top[:, -1:], images[:, -1:]], axis=0), 1)
    heads, slots = head_order(), slot_order()
    used = lax.broadcasted_iota(jnp.int32, (1, 16, 1), 1) < 12

    cells = images.reshape(12, 2, 12, 2, 256)
    top_cells = top.reshape(1, 12, 2, 256)
    corner = left[:1]
    left_cells = left[1:].reshape(12, 2, 1, 256)
    planes = {
        (0, 0): slots16(cells[:, 0, :, 0]),
        (0, 1): slots16(cells[:, 0, :, 1], left_cells[:, 0]),
        (1, 0): jnp.concatenate([slots16(top_cells[:, :, 0]), slots16(cells[:, 1, :, 0])]),
        (1, 1): jnp.concatenate(
            [
                slots16(top_cells[:, :, 1], corner),
                slots16(cells[:, 1, :, 1], left_cells[:, 1]),
            ]
        ),
    }
    expanded, slopes = {}, {}
    for place, plane in planes.items():
        value, slope = gelu_both(dot(plane, w_expand))
        expanded[place] = value.astype(bf16)
        slopes[place] = slope[place[0] :].astype(bf16)
    taps = w_depth.astype(f32)

    def window(row_tap, odd_col):
        plane = expanded[(row_tap + 1) % 2, odd_col]
        return plane[row_tap // 2 : row_tap // 2 + 12].astype(f32)

    straight = sum(
        window(a, 0) * taps[a, 1] + window(a, 1) * taps[a, 2] for a in range(3)
    )
    moved = sum(window(a, 1) * taps[a, 0] for a in range(3))
    value, conv_slope = gelu_both(straight + jnp.roll(moved, 1, axis=1))
    activated = value.astype(bf16)
    conv_slope = conv_slope.astype(bf16)
    wide = cells.astype(f32)
    pooled = slots16(
        ((wide[:, 0, :, 0] + wide[:, 0, :, 1] + wide[:, 1, :, 0] + wide[:, 1, :, 1]) * 0.25).astype(bf16)
    )

    cotangent = cotangent.reshape(192, 512)
    activated = activated.reshape(192, 1024)
    pooled = pooled.reshape(192, 256)
    spot = jnp.stack([lax.axis_index("core"), lax.axis_index("ylo")]).astype(jnp.int32)
    pieces, section_out, normed, proj, qkv = section_step(
        spot, ring, other, activated, pooled, w_short, cotangent, heads, slots
    )
    got = exchange(pieces.reshape(64, 24, 128), GRID_AXES)
    mixed = attention(got.reshape(8, 192, 128))
    got = exchange(mixed.reshape(64, 24, 128), GRID_AXES).reshape(HEADS, 192, 128)
    results, d_section, d_conv = back_step(
        got, heads, slots, section_out, cotangent, proj, qkv, conv_slope.reshape(192, 1024)
    )
    below = row_rim(d_conv[:12].reshape(1, 12, 1024), -1)
    edge = d_conv.reshape(12, 16, 1024)[:, :1]
    right = col_rim(jnp.concatenate([edge, below[:, :1]], axis=0), -1)
    matrix, short, d_pooled = parts_step(
        results, d_section, normed, cotangent, activated, pooled, w_short
    )
    even = jnp.stack([expanded[0, 0], expanded[0, 1]]).reshape(2, 192, 1024)
    odd = jnp.stack([expanded[1, 0], expanded[1, 1]]).reshape(2, 208, 1024)
    order = [(row, col) for row in range(2) for col in range(2)]
    slope_planes = jnp.stack([slopes[place] for place in order]).reshape(4, 192, 1024)
    cell_planes = jnp.stack([planes[place][place[0] :] for place in order]).reshape(4, 192, 256)
    taps16 = jnp.pad(w_depth.reshape(9, 1024), ((0, 7), (0, 0)))
    image, expand, depth = pixel_step(
        d_conv, slots16(below), right, even, odd, slope_planes, cell_planes, w_expand, taps16,
        d_pooled,
    )
    image = image.reshape(2, 2, 12, 16, 256)[:, :, :, :12]
    grad_image = image.transpose(2, 0, 3, 1, 4).reshape(1, 24, 24, 256)
    return (grad_image,) + all_sums(matrix, short, expand, depth)


def solution(mesh):
    fine = Mesh(mesh.devices.reshape(4, 2, 2, 4, 8), ("ylo", "core", "yhi", "x", "z"))
    cells = P(SAMPLE, ROW, COL, None)
    rows = P(SAMPLE, None)
    return jax.shard_map(
        on_device,
        mesh=fine,
        in_specs=(cells, P(), P(), P(), rows, rows, rows, cells),
        out_specs=(cells, P(), P(), P(), rows, rows, rows),
        check_vma=False,
    )
```

time: 289 us -> 247 us (0.85)
  blocking collectives: 0 us -> 55.2 us
  waiting for transfers between devices: 88.4 us -> 46.1 us
  starting transfers between devices: 116 us -> 77.1 us
  matrix products: 23.6 us -> 9.1 us
  Pallas kernels: 6.29 us -> 17.2 us
  local copies, waits for them, and re-layouts: 31.4 us -> 24.2 us
  other arithmetic: 19.1 us -> 15.3 us
    all_to_all x0 -> x3, blocking collectives: none -> 55.2 us  [exchange(): return lax.all_to_all(block, axes, 0, 0, tiled=True)]
    all_to_all x4 -> x3, waiting for transfers between devices: 81.4 us -> 37 us  [exchange(): return lax.all_to_all(block, axes, 0, 0, tiled=True)]
    ppermute x11 -> x5, starting transfers between devices: 40.3 us -> 14.7 us  [the longest x2 5.29 us: col_rim(): return lax.ppermute(edge, COL, step_route(PARTS, distance))]
    all_to_all x4 -> x3, starting transfers between devices: 52.8 us -> 34.7 us  [exchange(): return lax.all_to_all(block, axes, 0, 0, tiled=True)]
    dot_general x17 -> x0, matrix products: 12.4 us -> none  [the longest x9 7.29 us: dot_t(): lax.dot_general(left, right, (((left.ndim - 1,), (1,)), ((), ())), prefer...]
    pallas_call x0 -> x4, Pallas kernels: none -> 10.8 us  [the longest x1 5.21 us: pixel_step(): call(pixel_kernel, 'pixel', [jax.ShapeDtypeStruct((4, 192, 256), bf16), j...]
    another operation x9 -> x8, other arithmetic: 0.38 us -> 6.72 us  [the longest x1 0.12 us: on_device(): grads.append(jnp.stack(in_row, axis=2))]
    ppermute x3, starting transfers between devices: 16.8 us -> 22.4 us  [swap_cores(): return lax.ppermute(block, 'core', [(0, 1), (1, 0)])]
  transfers between devices with their start and end apart: 20 -> 13, of which waited for: 8 -> 6; matrix products, arithmetic and copies ran while one was open for 12% -> 11% of each run, Pallas kernels for 0% -> 0%
where the time goes in v3:
time: 247 us; the launch traced here: 246 us
  starting transfers between devices  77.1 us (31%)
  blocking collectives  55.2 us (22%)
  waiting for transfers between devices  46.1 us (19%)
  local copies, waits for them, and re-layouts  24.2 us (10%)
  Pallas kernels  17.2 us (7%)
  other arithmetic  15.3 us (6%)
  matrix products  9.1 us (4%)
    all_to_all x3, blocking collectives, exchange(): return lax.all_to_all(block, axes, 0, 0, tiled=True)  55.2 us
    all_to_all x3, waiting for transfers between devices, exchange(): return lax.all_to_all(block, axes, 0, 0, tiled=True)  37 us
    all_to_all x3, starting transfers between devices, exchange(): return lax.all_to_all(block, axes, 0, 0, tiled=True)  34.7 us
    ppermute x3, starting transfers between devices, swap_cores(): return lax.ppermute(block, 'core', [(0, 1), (1, 0)])  22.4 us
    unnamed x101, local copies, waits for them, and re-layouts  13.8 us
    dot_general x4, matrix products, dot(): lax.dot_general(left, right, (((left.ndim - 1,), (0,)), ((), ())), prefer...  9.1 us
    pallas_call x1, Pallas kernels, attention(): pl.pallas_call(attention_kernel, out_shape=jax.ShapeDtypeStruct((8, 192,...  6.36 us
    ppermute x2, starting transfers between devices, col_rim(): return lax.ppermute(edge, COL, step_route(PARTS, distance))  5.29 us
  transfers between devices with their start and end apart: 13, of which 6 were waited for; matrix products, arithmetic and copies ran while one was open for 11% of the time, Pallas kernels for 0%

profile of v3, /device:TPU:1, one launch (start us, length us, event | category | flops | bytes accessed | tf_op | source)
XLA Modules:
  0.0 245.8 jit_solution(11737234969471670514)
XLA Ops:
  2.2 1.6 maximum_maximum_fusion
  3.9 5.0 %collective-permute-start.1 = (bf16[256,512]{1,0:T(8,128)(2,1)}, bf16[256,512]{1,0:T(8,128)(2,1)}, u32[]{:S(2)}, u32[]{:S(2)}) collective-permute-start(bf16[256,512]{1,0:T(8,128)(2,1)} %maximum_maximum_fusion), channel_id=1, source_target_pairs={{0,256},{128,384},{256,32},{384,160},{32,288},{160,416},{288,0},{4... | collective-permute-start | bytes 786440 | tf_op jit(solution)/shard_map/ppermute | solution.py:100
  8.9 3.3 %collective-permute-start = (bf16[256,512]{1,0:T(8,128)(2,1)}, bf16[256,512]{1,0:T(8,128)(2,1)}, u32[]{:S(2)}, u32[]{:S(2)}) collective-permute-start(bf16[256,512]{1,0:T(8,128)(2,1)} %maximum_maximum_fusion), channel_id=1, source_target_pairs={{0,416},{128,0},{256,128},{384,256},{32,384},{160,32},{288,160},{4... | collective-permute-start | bytes 786440 | tf_op jit(solution)/shard_map/ppermute | solution.py:99
  12.2 2.0 collective-permute-start.2
  14.9 3.1 %collective-permute-start.4 = (bf16[1,24,256]{2,1,0:T(8,128)(2,1)S(1)}, bf16[1,24,256]{2,1,0:T(8,128)(2,1)S(1)}, u32[]{:S(2)}, u32[]{:S(2)}) collective-permute-start(bf16[1,24,256]{2,1,0:T(8,128)(2,1)S(1)} %slice_bitcast_fusion.4), channel_id=1, source_target_pairs={{0,8},{8,16},{16,24},{24,32},{32,40},{40,48},{48,56},{1,9},{9,17},... | collective-permute-start | bytes 36872 | tf_op jit(solution)/shard_map/ppermute | solution.py:69
  24.6 4.0 %collective-permute-start.5 = (bf16[25,1,256]{2,1,0:T(2,128)(2,1)S(1)}, bf16[25,1,256]{2,1,0:T(2,128)(2,1)S(1)}, u32[]{:S(2)}, u32[]{:S(2)}) collective-permute-start(bf16[25,1,256]{2,1,0:T(2,128)(2,1)S(1)} %pad_maximum_fusion.11), channel_id=1, source_target_pairs={{0,1},{1,2},{2,3},{3,4},{4,5},{5,6},{6,7},{8,9},{9,10},{10,11},{11... | collective-permute-start | bytes 38408 | tf_op jit(solution)/shard_map/ppermute | solution.py:73
  28.6 1.9 fusion.42
  30.7 2.8 %fusion.40 = (f32[13,16,1024]{2,1,0:T(8,128)S(1)}, bf16[13,16,1024]{2,1,0:T(8,128)(2,1)S(1)}, f32[13,16,1024]{2,1,0:T(8,128)}, f32[13,16,1024]{2,1,0:T(8,128)}, f32[13,16,1024]{2,1,0:T(8,128)}) fusion(bf16[256,1024]{1,0:T(8,128)(2,1)S(1)} %copy-done, bf16[12,1,256]{2,1,0:T(2,128)(2,1)S(1)} %get-tuple-element.76, bf16[12,3,256]{2,1,0:T(4,128)(2,1)S(1)} %broadcast.201, ...), kind=kOutput, calls=%fused_computation.76 | convolution fusion | flops 111820800 | bytes 4463520 | tf_op jit(solution)/shard_map/dot_general | solution.py:40
  35.0 4.0 %collective-permute-start.3 = (bf16[4,256,512]{2,1,0:T(8,128)(2,1)S(1)}, bf16[4,256,512]{2,1,0:T(8,128)(2,1)S(1)}, u32[]{:S(2)}, u32[]{:S(2)}) collective-permute-start(bf16[4,256,512]{2,1,0:T(8,128)(2,1)S(1)} %pad_maximum_fusion.2.ring_ref), channel_id=1, source_target_pairs={{0,64},{64,0},{1,65},{65,1},{2,66},{66,2},{3,67},{67,3},{4,68},{68... | collective-permute-start | bytes 3145736 | tf_op jit(solution)/shard_map/ppermute | solution.py:82
  39.1 1.6 fusion.9
  40.9 2.8 %fusion.21 = (bf16[12,16,1024]{2,1,0:T(8,128)(2,1)}, f32[12,16,1024]{2,1,0:T(8,128)S(1)}, bf16[12,16,1024]{2,1,0:T(8,128)(2,1)}, bf16[12,16,1024]{2,1,0:T(8,128)(2,1)}) fusion(f32[12,15,1024]{2,1,0:T(8,128)S(1)} %bitcast.203, f32[12,1,1024]{2,1,0:T(1,128)S(1)} %slice.246, f32[1024]{0:T(1024)S(1)} %bitcast.199, ...), kind=kOutput, calls=%fused_computation.47 | convolution fusion | flops 111869952 | bytes 5341184 | tf_op jit(solution)/shard_map/dot_general | solution.py:40
  44.0 3.0 %section.1 = (bf16[8,192,128]{2,1,0:T(8,128)(2,1)}, bf16[192,512]{1,0:T(8,128)(2,1)S(1)}, bf16[192,512]{1,0:T(8,128)(2,1)S(1)}, bf16[1024,512]{1,0:T(8,128)(2,1)...) custom-call(s32[2]{0:T(128)S(1)} %pad_add_fusion.spot_ref, ...), custom_call_target="tpu_custom_call" | custom-call | flops 1500000000 | bytes 8000000 | tf_op jit(solution)/shard_map/section/pallas_call | solution.py:231
  50.2 21.2 %all-to-all-start = ((bf16[64,24,128]{2,1,0:T(8,128)(2,1)}), bf16[64,24,128]{2,1,0:T(8,128)(2,1)}, u32[]{:S(2)}, u32[]{:S(2)}) async-start(bf16[64,24,128]{2,1,0:T(8,128)(2,1)} %bitcast.31), calls=%async_computation | async-start | bytes 786432 | tf_op jit(solution)/shard_map/all_to_all | solution.py:86
  72.6 2.7 %fusion.33 = bf16[12,16,1024]{2,1,0:T(8,128)(2,1)} fusion(f32[13,16,1024]{2,1,0:T(8,128)} %get-tuple-element.48, f32[13,16,1024]{2,1,0:T(8,128)} %get-tuple-element.49, f32[13,16,1024]{2,1,0:T(8,128)} %get-tuple-element.78, f32[13,16,1024]{2,1,0:T(8,128)S(1)} %get-tuple-element.46), kind=kLoop, calls=%fused_computation.59 | loop fusion | flops 1966080 | bytes 3538944 | tf_op jit(solution)/shard_map/convert.20
  75.4 11.5 %all-to-all-done = bf16[64,24,128]{2,1,0:T(8,128)(2,1)} async-done(((bf16[64,24,128]{2,1,0:T(8,128)(2,1)}), bf16[64,24,128]{2,1,0:T(8,128)(2,1)}, u32[]{:S(2)}, u32[]{:S(2)}) %all-to-all-start) | async-done | bytes 393248 | tf_op jit(solution)/shard_map/all_to_all | solution.py:86
  86.9 6.4 %attention.1 = bf16[8,192,128]{2,1,0:T(8,128)(2,1)} custom-call(bf16[8,192,128]{2,1,0:T(8,128)(2,1)} %bitcast.32.slots_ref, bf16[192,192]{1,0:T(8,128)(2,1)} %constant.107.clone.order_ref, f32[1,192]{1,0:T(1,128)} %or_convert_fusion.valid_ref), custom_call_target="tpu_custom_call" | custom-call | flops 500000000 | bytes 1000000 | tf_op jit(solution)/shard_map/attention/pallas_call | solution.py:164
  93.2 8.9 %all-to-all-start.1 = ((bf16[64,24,128]{2,1,0:T(8,128)(2,1)}), bf16[64,24,128]{2,1,0:T(8,128)(2,1)S(1)}, u32[]{:S(2)}, u32[]{:S(2)}) async-start(bf16[64,24,128]{2,1,0:T(8,128)(2,1)} %bitcast.175), calls=%async_computation.1 | async-start | bytes 786432 | tf_op jit(solution)/shard_map/all_to_all | solution.py:86
  103.0 2.1 pad_maximum_fusion.4.even_ref
  106.6 10.7 %all-to-all-done.1 = bf16[64,24,128]{2,1,0:T(8,128)(2,1)S(1)} async-done(((bf16[64,24,128]{2,1,0:T(8,128)(2,1)}), bf16[64,24,128]{2,1,0:T(8,128)(2,1)S(1)}, u32[]{:S(2)}, u32[]{:S(2)}) %all-to-all-start.1) | async-done | bytes 393248 | tf_op jit(solution)/shard_map/all_to_all | solution.py:86
  117.3 1.6 copy-done.3
  124.1 1.8 back.1
  128.1 2.4 collective-permute-done.6
  132.1 3.7 %collective-permute-done.7.right_ref = bf16[13,1,1024]{2,1,0:T(2,128)(2,1)S(1)} collective-permute-done((bf16[13,1,1024]{2,1,0:T(2,128)(2,1)S(1)}, bf16[13,1,1024]{2,1,0:T(2,128)(2,1)S(1)}, u32[]{:S(2)}, u32[]{:S(2)}) %collective-permute-start.7) | collective-permute-done | bytes 26656 | tf_op jit(solution)/shard_map/ppermute | solution.py:73
  135.8 5.2 %pixel.1 = (bf16[4,192,256]{2,1,0:T(8,128)(2,1)S(1)}, bf16[32,64,128]{2,1,0:T(8,128)(2,1)S(1)}, f32[16,1024]{1,0:T(8,128)S(1)}) custom-call(bf16[192,1024]{1,0:T(8,128)(2,1)S(1)} %get-tuple-element.25.d_conv_ref, bf16[1,16,1024]{2,1,0:T(8,128)(2,1)S(1)} %pad.35.below_ref, bf16[13,1,1024]{2,1,0:T(2,128)(2,1)S(1)} %collective-permute-done.7.right_ref, ...), custom_call_target="tpu_custom_call" | custom-call | flops 1200000000 | bytes 8000000 | tf_op jit(solution)/shard_map/pixel/pallas_call | solution.py:381
  141.3 8.5 %collective-permute-start.8 = (bf16[32,192,128]{2,1,0:T(8,128)(2,1)S(1)}, bf16[32,192,128]{2,1,0:T(8,128)(2,1)S(1)}, u32[]{:S(2)}, u32[]{:S(2)}) collective-permute-start(bf16[32,192,128]{2,1,0:T(8,128)(2,1)S(1)} %pad_maximum_fusion.1), channel_id=1, source_target_pairs={{0,64},{64,0},{1,65},{65,1},{2,66},{66,2},{3,67},{67,3},{4,68},{68... | collective-permute-start | bytes 4718600 | tf_op jit(solution)/shard_map/ppermute | solution.py:82
  149.8 3.0 %collective-permute-done.8 = bf16[32,192,128]{2,1,0:T(8,128)(2,1)S(1)} collective-permute-done((bf16[32,192,128]{2,1,0:T(8,128)(2,1)S(1)}, bf16[32,192,128]{2,1,0:T(8,128)(2,1)S(1)}, u32[]{:S(2)}, u32[]{:S(2)}) %collective-permute-start.8) | collective-permute-done | bytes 1572896 | tf_op jit(solution)/shard_map/ppermute | solution.py:82
  153.4 30.2 %all_to_all.30 = bf16[32,192,128]{2,1,0:T(8,128)(2,1)S(1)} all-to-all(bf16[32,192,128]{2,1,0:T(8,128)(2,1)S(1)} %add_convert_fusion), channel_id=1, replica_groups=mesh['ylo'=4,'core'=2,'yhi'=2,'x'=4,'z'=8] {'x'}, dimensions={0} | all-to-all | bytes 3145728 | tf_op jit(solution)/shard_map/all_to_all | solution.py:86
  183.9 14.7 %all_to_all.31 = bf16[8,192,128]{2,1,0:T(8,128)(2,1)S(1)} all-to-all(bf16[8,192,128]{2,1,0:T(8,128)(2,1)S(1)} %reduce_sum.33), channel_id=1, replica_groups=mesh['ylo'=4,'core'=2,'yhi'=2,'x'=4,'z'=8] {'z'}, dimensions={0} | all-to-all | bytes 786432 | tf_op jit(solution)/shard_map/all_to_all | solution.py:86
  198.8 10.3 %all_to_all.32 = bf16[8,96,128]{2,1,0:T(8,128)(2,1)S(1)} all-to-all(bf16[8,96,128]{2,1,0:T(8,128)(2,1)S(1)} %bitcast.169), channel_id=1, replica_groups=mesh['ylo'=4,'core'=2,'yhi'=2,'x'=4,'z'=8] {'ylo','yhi'}, dimensions={0} | all-to-all | bytes 393216 | tf_op jit(solution)/shard_map/all_to_all | solution.py:86
  210.1 4.7 %all-to-all-start.5 = ((bf16[32,96,128]{2,1,0:T(8,128)(2,1)}), bf16[32,96,128]{2,1,0:T(8,128)(2,1)S(1)}, u32[]{:S(2)}, u32[]{:S(2)}) async-start(bf16[32,96,128]{2,1,0:T(8,128)(2,1)} %broadcast_in_dim.11), calls=%async_computation.5 | async-start | bytes 1572864 | tf_op jit(solution)/shard_map/all_to_all | solution.py:86
  216.0 14.8 %all-to-all-done.5 = bf16[32,96,128]{2,1,0:T(8,128)(2,1)S(1)} async-done(((bf16[32,96,128]{2,1,0:T(8,128)(2,1)}), bf16[32,96,128]{2,1,0:T(8,128)(2,1)S(1)}, u32[]{:S(2)}, u32[]{:S(2)}) %all-to-all-start.5) | async-done | bytes 786464 | tf_op jit(solution)/shard_map/all_to_all | solution.py:86
  230.8 9.9 %collective-permute-start.9 = (bf16[256,8,128]{2,1,0:T(8,128)(2,1)S(1)}, bf16[256,8,128]{2,1,0:T(8,128)(2,1)S(1)}, u32[]{:S(2)}, u32[]{:S(2)}) collective-permute-start(bf16[256,8,128]{2,1,0:T(8,128)(2,1)S(1)} %bitcast.156), channel_id=1, source_target_pairs={{0,64},{64,0},{1,65},{65,1},{2,66},{66,2},{3,67},{67,3},{4,68},{68... | collective-permute-start | bytes 1572872 | tf_op jit(solution)/shard_map/ppermute | solution.py:82
  (190 shorter events, 34.9 us)
Async XLA Ops:
  3.9 29.6 %collective-permute-start.1 = (bf16[256,512]{1,0:T(8,128)(2,1)}, bf16[256,512]{1,0:T(8,128)(2,1)}, u32[]{:S(2)}, u32[]{:S(2)}) collective-permute-start(bf16[256,512]{1,0:T(8,128)(2,1)} %maximum_maximum_fusion), channel_id=1, source_target_pairs={{0,256},{128,384},{256,32},{384,160},{32,288},{160,416},{288,0},{4... | collective-permute-start | bytes 786440 | tf_op jit(solution)/shard_map/ppermute | solution.py:100
  8.9 24.6 %collective-permute-start = (bf16[256,512]{1,0:T(8,128)(2,1)}, bf16[256,512]{1,0:T(8,128)(2,1)}, u32[]{:S(2)}, u32[]{:S(2)}) collective-permute-start(bf16[256,512]{1,0:T(8,128)(2,1)} %maximum_maximum_fusion), channel_id=1, source_target_pairs={{0,416},{128,0},{256,128},{384,256},{32,384},{160,32},{288,160},{4... | collective-permute-start | bytes 786440 | tf_op jit(solution)/shard_map/ppermute | solution.py:99
  12.2 21.3 %collective-permute-start.2 = (bf16[256,512]{1,0:T(8,128)(2,1)}, bf16[256,512]{1,0:T(8,128)(2,1)}, u32[]{:S(2)}, u32[]{:S(2)}) collective-permute-start(bf16[256,512]{1,0:T(8,128)(2,1)} %maximum_maximum_fusion), channel_id=1, source_target_pairs={{0,128},{128,256},{256,384},{384,32},{32,160},{160,288},{288,416},... | collective-permute-start | bytes 786440 | tf_op jit(solution)/shard_map/ppermute | solution.py:98
  14.9 9.6 %collective-permute-start.4 = (bf16[1,24,256]{2,1,0:T(8,128)(2,1)S(1)}, bf16[1,24,256]{2,1,0:T(8,128)(2,1)S(1)}, u32[]{:S(2)}, u32[]{:S(2)}) collective-permute-start(bf16[1,24,256]{2,1,0:T(8,128)(2,1)S(1)} %slice_bitcast_fusion.4), channel_id=1, source_target_pairs={{0,8},{8,16},{16,24},{24,32},{32,40},{40,48},{48,56},{1,9},{9,17},... | collective-permute-start | bytes 36872 | tf_op jit(solution)/shard_map/ppermute | solution.py:69
  20.4 3.2 %copy-start.38 = (bf16[1,12,12,512]{3,2,1,0:T(8,128)(2,1)S(1)}, bf16[1,12,12,512]{3,2,1,0:T(8,128)(2,1)}, u32[]{:S(2)}) copy-start(bf16[1,12,12,512]{3,2,1,0:T(8,128)(2,1)} %param.18) | copy-start | bytes 442372
  21.5 7.1 %copy-start = (bf16[256,1024]{1,0:T(8,128)(2,1)S(1)}, bf16[256,1024]{1,0:T(8,128)(2,1)}, u32[]{:S(2)}) copy-start(bf16[256,1024]{1,0:T(8,128)(2,1)} %w_expand_ref.1) | copy-start | bytes 1572868
  21.9 22.1 %copy-start.12 = (bf16[192,192]{1,0:T(8,128)(2,1)}, bf16[192,192]{1,0:T(8,128)(2,1)S(1)}, u32[]{:S(2)}) copy-start(bf16[192,192]{1,0:T(8,128)(2,1)S(1)} %dynamic-slice_bitcast_fusion.2.slots_ref) | copy-start | bytes 221188
  23.7 20.3 %copy-start.17 = (bf16[12,16,256]{2,1,0:T(8,128)(2,1)}, bf16[12,16,256]{2,1,0:T(8,128)(2,1)S(1)}, u32[]{:S(2)}) copy-start(bf16[12,16,256]{2,1,0:T(8,128)(2,1)S(1)} %pad.33) | copy-start | bytes 294916
  24.4 6.1 %copy-start.29 = (bf16[12,16,256]{2,1,0:T(8,128)(2,1)}, bf16[12,16,256]{2,1,0:T(8,128)(2,1)S(1)}, u32[]{:S(2)}) copy-start(bf16[12,16,256]{2,1,0:T(8,128)(2,1)S(1)} %pad.31) | copy-start | bytes 294916
  24.6 5.9 %collective-permute-start.5 = (bf16[25,1,256]{2,1,0:T(2,128)(2,1)S(1)}, bf16[25,1,256]{2,1,0:T(2,128)(2,1)S(1)}, u32[]{:S(2)}, u32[]{:S(2)}) collective-permute-start(bf16[25,1,256]{2,1,0:T(2,128)(2,1)S(1)} %pad_maximum_fusion.11), channel_id=1, source_target_pairs={{0,1},{1,2},{2,3},{3,4},{4,5},{5,6},{6,7},{8,9},{9,10},{10,11},{11... | collective-permute-start | bytes 38408 | tf_op jit(solution)/shard_map/ppermute | solution.py:73
  33.5 7.3 %copy-start.26 = (bf16[13,16,1024]{2,1,0:T(8,128)(2,1)}, bf16[13,16,1024]{2,1,0:T(8,128)(2,1)S(1)}, u32[]{:S(2)}) copy-start(bf16[13,16,1024]{2,1,0:T(8,128)(2,1)S(1)} %get-tuple-element.51) | copy-start | bytes 1277956
  33.5 5.5 %copy-start.31 = (bf16[12,1,12,1,256]{4,2,0,3,1:T(8,128)(2,1)S(1)}, bf16[12,1,12,1,256]{4,2,0,3,1:T(8,128)(2,1)}, u32[]{:S(2)}) copy-start(bf16[12,1,12,1,256]{4,2,0,3,1:T(8,128)(2,1)} %copy.78) | copy-start | bytes 221188
  33.5 5.5 %copy-start.36 = (bf16[12,12,256]{2,1,0:T(8,128)(2,1)S(1)}, bf16[12,12,256]{2,1,0:T(8,128)(2,1)}, u32[]{:S(2)}) copy-start(bf16[12,12,256]{2,1,0:T(8,128)(2,1)} %get-tuple-element.79) | copy-start | bytes 221188
  33.5 5.6 %copy-start.43 = (f32[1,1,1024]{2,1,0:T(1,128)S(1)}, f32[1,1,1024]{2,1,0:T(1,128)}, u32[]{:S(2)}) copy-start(f32[1,1,1024]{2,1,0:T(1,128)} %get-tuple-element.70) | copy-start | bytes 12292
  33.5 5.6 %copy-start.44 = (f32[1,1,1024]{2,1,0:T(1,128)S(1)}, f32[1,1,1024]{2,1,0:T(1,128)}, u32[]{:S(2)}) copy-start(f32[1,1,1024]{2,1,0:T(1,128)} %get-tuple-element.71) | copy-start | bytes 12292
  33.5 5.6 %copy-start.45 = (f32[1,1,1024]{2,1,0:T(1,128)S(1)}, f32[1,1,1024]{2,1,0:T(1,128)}, u32[]{:S(2)}) copy-start(f32[1,1,1024]{2,1,0:T(1,128)} %get-tuple-element.72) | copy-start | bytes 12292
  35.0 8.9 %collective-permute-start.3 = (bf16[4,256,512]{2,1,0:T(8,128)(2,1)S(1)}, bf16[4,256,512]{2,1,0:T(8,128)(2,1)S(1)}, u32[]{:S(2)}, u32[]{:S(2)}) collective-permute-start(bf16[4,256,512]{2,1,0:T(8,128)(2,1)S(1)} %pad_maximum_fusion.2.ring_ref), channel_id=1, source_target_pairs={{0,64},{64,0},{1,65},{65,1},{2,66},{66,2},{3,67},{67,3},{4,68},{68... | collective-permute-start | bytes 3145736 | tf_op jit(solution)/shard_map/ppermute | solution.py:82
  40.8 3.1 %copy-start.2 = (bf16[1024,1024]{1,0:T(8,128)(2,1)S(1)}, bf16[1024,1024]{1,0:T(8,128)(2,1)}, u32[]{:S(2)}) copy-start(bf16[1024,1024]{1,0:T(8,128)(2,1)} %constant.105.clone.heads_ref) | copy-start | bytes 6291460
  40.8 3.1 %copy-start.19 = (bf16[256,512]{1,0:T(8,128)(2,1)S(1)}, bf16[256,512]{1,0:T(8,128)(2,1)}, u32[]{:S(2)}) copy-start(bf16[256,512]{1,0:T(8,128)(2,1)} %short_ref.3) | copy-start | bytes 786436
  50.2 36.7 %all-to-all-start = ((bf16[64,24,128]{2,1,0:T(8,128)(2,1)}), bf16[64,24,128]{2,1,0:T(8,128)(2,1)}, u32[]{:S(2)}, u32[]{:S(2)}) async-start(bf16[64,24,128]{2,1,0:T(8,128)(2,1)} %bitcast.31), calls=%async_computation | async-start | bytes 786432 | tf_op jit(solution)/shard_map/all_to_all | solution.py:86
  75.4 26.8 %copy-start.30 = (bf16[12,16,256]{2,1,0:T(8,128)(2,1)S(1)}, bf16[12,16,256]{2,1,0:T(8,128)(2,1)}, u32[]{:S(2)}) copy-start(bf16[12,16,256]{2,1,0:T(8,128)(2,1)} %copy-done.29) | copy-start | bytes 294916
  86.9 16.1 %copy-start.35 = (bf16[12,16,1024]{2,1,0:T(8,128)(2,1)S(1)}, bf16[12,16,1024]{2,1,0:T(8,128)(2,1)}, u32[]{:S(2)}) copy-start(bf16[12,16,1024]{2,1,0:T(8,128)(2,1)} %copy-done.34) | copy-start | bytes 1179652
  93.2 24.1 %all-to-all-start.1 = ((bf16[64,24,128]{2,1,0:T(8,128)(2,1)}), bf16[64,24,128]{2,1,0:T(8,128)(2,1)S(1)}, u32[]{:S(2)}, u32[]{:S(2)}) async-start(bf16[64,24,128]{2,1,0:T(8,128)(2,1)} %bitcast.175), calls=%async_computation.1 | async-start | bytes 786432 | tf_op jit(solution)/shard_map/all_to_all | solution.py:86
  124.1 3.1 %copy-start.22 = (bf16[192,512]{1,0:T(8,128)(2,1)S(1)}, bf16[192,512]{1,0:T(8,128)(2,1)}, u32[]{:S(2)}) copy-start(bf16[192,512]{1,0:T(8,128)(2,1)} %copy-done.21) | copy-start | bytes 589828
  125.9 4.7 %collective-permute-start.6 = (bf16[1,12,1024]{2,1,0:T(8,128)(2,1)S(1)}, bf16[1,12,1024]{2,1,0:T(8,128)(2,1)S(1)}, u32[]{:S(2)}, u32[]{:S(2)}) collective-permute-start(bf16[1,12,1024]{2,1,0:T(8,128)(2,1)S(1)} %slice_bitcast_fusion.1), channel_id=1, source_target_pairs={{8,0},{16,8},{24,16},{32,24},{40,32},{48,40},{56,48},{9,1},{17,9},... | collective-permute-start | bytes 73736 | tf_op jit(solution)/shard_map/ppermute | solution.py:69
  130.6 5.2 %collective-permute-start.7 = (bf16[13,1,1024]{2,1,0:T(2,128)(2,1)S(1)}, bf16[13,1,1024]{2,1,0:T(2,128)(2,1)S(1)}, u32[]{:S(2)}, u32[]{:S(2)}) collective-permute-start(bf16[13,1,1024]{2,1,0:T(2,128)(2,1)S(1)} %pad_maximum_fusion.10), channel_id=1, source_target_pairs={{1,0},{2,1},{3,2},{4,3},{5,4},{6,5},{7,6},{9,8},{10,9},{11,10},{12... | collective-permute-start | bytes 79880 | tf_op jit(solution)/shard_map/ppermute | solution.py:73
  131.9 3.9 %copy-start.1 = (bf16[2,192,1024]{2,1,0:T(8,128)(2,1)S(1)}, bf16[2,192,1024]{2,1,0:T(8,128)(2,1)}, u32[]{:S(2)}) copy-start(bf16[2,192,1024]{2,1,0:T(8,128)(2,1)} %pad_maximum_fusion.4.even_ref) | copy-start | bytes 2359300
  131.9 3.9 %copy-start.4 = (bf16[4,192,256]{2,1,0:T(8,128)(2,1)S(1)}, bf16[4,192,256]{2,1,0:T(8,128)(2,1)}, u32[]{:S(2)}) copy-start(bf16[4,192,256]{2,1,0:T(8,128)(2,1)} %pad_maximum_fusion.6.cells_ref) | copy-start | bytes 1179652
  131.9 3.9 %copy-start.16 = (bf16[16,1024]{1,0:T(8,128)(2,1)S(1)}, bf16[16,1024]{1,0:T(8,128)(2,1)}, u32[]{:S(2)}) copy-start(bf16[16,1024]{1,0:T(8,128)(2,1)} %pad.36.taps_ref) | copy-start | bytes 98308
  141.3 11.5 %collective-permute-start.8 = (bf16[32,192,128]{2,1,0:T(8,128)(2,1)S(1)}, bf16[32,192,128]{2,1,0:T(8,128)(2,1)S(1)}, u32[]{:S(2)}, u32[]{:S(2)}) collective-permute-start(bf16[32,192,128]{2,1,0:T(8,128)(2,1)S(1)} %pad_maximum_fusion.1), channel_id=1, source_target_pairs={{0,64},{64,0},{1,65},{65,1},{2,66},{66,2},{3,67},{67,3},{4,68},{68... | collective-permute-start | bytes 4718600 | tf_op jit(solution)/shard_map/ppermute | solution.py:82
  210.1 20.7 %all-to-all-start.5 = ((bf16[32,96,128]{2,1,0:T(8,128)(2,1)}), bf16[32,96,128]{2,1,0:T(8,128)(2,1)S(1)}, u32[]{:S(2)}, u32[]{:S(2)}) async-start(bf16[32,96,128]{2,1,0:T(8,128)(2,1)} %broadcast_in_dim.11), calls=%async_computation.5 | async-start | bytes 1572864 | tf_op jit(solution)/shard_map/all_to_all | solution.py:86
  230.8 12.3 %collective-permute-start.9 = (bf16[256,8,128]{2,1,0:T(8,128)(2,1)S(1)}, bf16[256,8,128]{2,1,0:T(8,128)(2,1)S(1)}, u32[]{:S(2)}, u32[]{:S(2)}) collective-permute-start(bf16[256,8,128]{2,1,0:T(8,128)(2,1)S(1)} %bitcast.156), channel_id=1, source_target_pairs={{0,64},{64,0},{1,65},{65,1},{2,66},{66,2},{3,67},{67,3},{4,68},{68... | collective-permute-start | bytes 1572872 | tf_op jit(solution)/shard_map/ppermute | solution.py:82
  (27 other events, 47.8 us)

commit v4 on v3

--- a/solution.py
+++ b/solution.py
@@ -73,6 +73,16 @@
     return lax.ppermute(edge, COL, step_route(PARTS, distance))
 
 
+def diagonal_rim(edge, distance):
+    route = [
+        ((r - distance) * PARTS + c - distance, r * PARTS + c)
+        for r in range(PARTS)
+        for c in range(PARTS)
+        if 0 <= r - distance < PARTS and 0 <= c - distance < PARTS
+    ]
+    return lax.ppermute(edge, GRID_AXES, route)
+
+
 def around(distance):
     place = [y % 4 * 2 + y // 4 for y in range(8)]
     return [(place[y], place[(y + distance) % 8]) for y in range(8)]
@@ -90,22 +100,22 @@
     return exchange(jnp.broadcast_to(block[None], (count,) + block.shape), axes)
 
 
-def gather_weights(w_proj, w_qkv, w_out):
+def first_transfers(images, w_proj, w_qkv, w_out):
     tail = w_qkv[:, 512:]
     own = jnp.concatenate(
         [w_proj, w_qkv[:, :512], w_out, jnp.concatenate([tail[:32], tail[32:]], axis=1)], axis=0
     )
+    top = row_rim(images[-1:], 1)
     below = lax.ppermute(own, RING, around(1))
     above = lax.ppermute(own, RING, around(7))
-    far = lax.ppermute(own, RING, around(2))
+    own, top = lax.optimization_barrier((own, top))
+    left = col_rim(jnp.concatenate([top[:, -1:], images[:, -1:]], axis=0), 1)
+    far = jnp.concatenate(
+        [lax.ppermute(own[:128], RING, around(2)), lax.ppermute(own[128:], RING, around(6))]
+    )
     ring = jnp.stack([own, above, far, below])
-    return ring, swap_cores(ring)
-
-
-def head_order():
-    target = np.arange(1024)
-    wanted = target // 32 % 4 * 256 + target // 128 * 32 + target % 32
-    return jnp.asarray(target[:, None] == wanted[None, :], bf16)
+    ring, left = lax.optimization_barrier((ring, left))
+    return top, left, ring, swap_cores(ring)
 
 
 def slot_order():
@@ -166,7 +176,7 @@
         out_shape=jax.ShapeDtypeStruct((8, 192, 128), bf16),
         scratch_shapes=[pltpu.VMEM((1536, 128), bf16), pltpu.VMEM((1536, 128), bf16)],
         cost_estimate=pl.CostEstimate(
-            flops=500_000_000, bytes_accessed=1_000_000, transcendentals=300_000
+            flops=7_000_000_000, bytes_accessed=1_000_000, transcendentals=300_000
         ),
         name="attention",
     )(slots, row_order(), valid)
@@ -188,18 +198,136 @@
         body,
         out_shape=out_shape,
         scratch_shapes=scratch,
-        compiler_params=pltpu.CompilerParams(vmem_limit_bytes=40 * 1024 * 1024),
+        compiler_params=pltpu.CompilerParams(vmem_limit_bytes=24 * 1024 * 1024),
         cost_estimate=pl.CostEstimate(flops=flops, bytes_accessed=8_000_000, transcendentals=0),
         name=name,
         **rest,
     )
 
 
+def held(shape, dtype=bf16):
+    return pltpu.HBM(shape, dtype)
+
+
+def expand_kernel(
+    images_ref, top_ref, left_ref, w_expand_ref, taps_ref,
+    even_ref, odd_ref, slopes_ref, activated_ref, conv_slope_ref, cells_ref, pooled_ref,
+    wide_ref, top_wide_ref, left_wide_ref, plane_ref, rows_ref,
+):
+    @pl.when(pl.program_id(0) == 0)
+    def _():
+        slot = lax.broadcasted_iota(jnp.int32, (1, 16, 1), 1)
+        for half in range(2):
+            lanes = slice(128 * half, 128 * half + 128)
+            wide_ref[half] = images_ref[:, :, lanes].astype(f32)
+            top_wide_ref[half] = top_ref[:, :, lanes].astype(f32)
+        left_wide_ref[...] = left_ref[...].astype(f32)
+        pooled = 0.0
+        for row in range(2):
+            for col in range(2):
+                plane = 2 * row + col
+                plane_ref[...] = jnp.zeros((13, 16, 256), f32)
+                for half in range(2):
+                    lanes = slice(128 * half, 128 * half + 128)
+                    plane_ref[row : row + 12, 0:12, lanes] = wide_ref[
+                        half, pl.ds(row, 12, stride=2), pl.ds(col, 12, stride=2), :
+                    ]
+                    if row:
+                        plane_ref[0:1, 0:12, lanes] = top_wide_ref[
+                            half, :, pl.ds(col, 12, stride=2), :
+                        ]
+                if col:
+                    plane_ref[row : row + 12, 15:16, :] = left_wide_ref[1:25].reshape(
+                        12, 2, 1, 256
+                    )[:, row]
+                if row and col:
+                    plane_ref[0:1, 15:16, :] = left_wide_ref[0:1]
+                cells = plane_ref[...]
+                rows_ref[plane] = cells.astype(bf16).reshape(208, 256)
+                cells = cells[row : row + 12]
+                cells_ref[plane] = cells.astype(bf16).reshape(192, 256)
+                pooled = pooled + cells
+        pooled = jnp.where(slot < 12, pooled * 0.25, 0.0)
+        pooled_ref[...] = pooled.astype(bf16).reshape(192, 256)
+
+    taps = [[taps_ref[3 * a + b : 3 * a + b + 1, :].astype(f32) for b in range(3)] for a in range(3)]
+    expanded = {}
+    for row in range(2):
+        for col in range(2):
+            count = 192 + 16 * row
+            value, slope = gelu_both(dot(rows_ref[2 * row + col, 0:count], w_expand_ref[...]))
+            value = value.astype(bf16)
+            (odd_ref if row else even_ref)[col] = value
+            slopes_ref[2 * row + col] = slope[16 * row :].astype(bf16)
+            expanded[row, col] = value.astype(f32).reshape(12 + row, 16, 256)
+
+    def window(row_tap, odd_col):
+        plane = expanded[(row_tap + 1) % 2, odd_col]
+        return plane[row_tap // 2 : row_tap // 2 + 12]
+
+    straight = sum(
+        window(a, 0) * taps[a][1] + window(a, 1) * taps[a][2] for a in range(3)
+    )
+    moved = sum(window(a, 1) * taps[a][0] for a in range(3))
+    value, slope = gelu_both(straight + pltpu.roll(moved, 1, 1))
+    activated_ref[...] = value.astype(bf16).reshape(192, 256)
+    conv_slope_ref[...] = slope.astype(bf16).reshape(192, 256)
+
+
+def expand_step(*inputs):
+    def chunk(*lead):
+        return pl.BlockSpec(lead + (256,), lambda step: (0,) * len(lead) + (step,))
+
+    def whole(*shape):
+        return pl.BlockSpec(shape, lambda step: (0,) * len(shape))
+
+    shapes = [
+        (2, 192, 1024), (2, 208, 1024), (4, 192, 1024), (192, 1024), (192, 1024), (4, 192, 256),
+        (192, 256),
+    ]
+    return call(
+        expand_kernel,
+        "expand",
+        [held(shape) for shape in shapes],
+        6_000_000_000,
+        scratch=[
+            pltpu.VMEM((2, 24, 24, 128), f32),
+            pltpu.VMEM((2, 1, 24, 128), f32),
+            pltpu.VMEM((25, 1, 256), f32),
+            pltpu.VMEM((13, 16, 256), f32),
+            pltpu.VMEM((4, 208, 256), bf16),
+        ],
+        grid=(4,),
+        in_specs=[whole(24, 24, 256), whole(1, 24, 256), whole(25, 1, 256), chunk(256), chunk(16)],
+        out_specs=[
+            chunk(2, 192), chunk(2, 208), chunk(4, 192), chunk(192), chunk(192),
+            whole(4, 192, 256), whole(192, 256),
+        ],
+    )(*inputs)
+
+
+def row_buffers():
+    return [
+        pltpu.VMEM((192, 1024), bf16),
+        pltpu.VMEM((192, 256), bf16),
+        pltpu.VMEM((192, 512), bf16),
+        pltpu.SemaphoreType.DMA((3,)),
+    ]
+
+
 def section_kernel(
-    spot_ref, ring_ref, other_ref, activated_ref, pooled_ref, short_ref, cotangent_ref, heads_ref,
-    slots_ref, pieces_ref, section_ref, normed_ref, proj_ref, qkv_ref, out_ref,
+    spot_ref, ring_ref, other_ref, activated_in, pooled_in, short_ref, cotangent_in, slots_ref,
+    pieces_ref, section_ref, normed_ref, proj_ref, qkv_ref, out_ref,
+    activated_ref, pooled_ref, cotangent_ref, sems,
 ):
     core, y_lo = spot_ref[0], spot_ref[1]
+    copies = [
+        pltpu.make_async_copy(activated_in, activated_ref, sems.at[0]),
+        pltpu.make_async_copy(pooled_in, pooled_ref, sems.at[1]),
+        pltpu.make_async_copy(cotangent_in, cotangent_ref, sems.at[2]),
+    ]
+    for copy in copies:
+        copy.start()
 
     def place(shard, source, at):
         proj_ref[shard * 128 : shard * 128 + 128] = source[at, 0:128]
@@ -212,6 +340,8 @@
         at = lax.rem(shard // 2 - y_lo + 4, 4)
         pl.when(core == shard % 2)(lambda: place(shard, ring_ref, at))
         pl.when(core != shard % 2)(lambda: place(shard, other_ref, at))
+    for copy in copies:
+        copy.wait()
     section = (
         dot(activated_ref[...], proj_ref[...]) + dot(pooled_ref[...], short_ref[...])
     ).astype(bf16)
@@ -221,33 +351,57 @@
     packed = dot(normed, qkv_ref[...]).astype(bf16)
     d_mixture = dot_kt(cotangent_ref[...], out_ref[...]).astype(bf16)
     tokens = jnp.concatenate([packed, d_mixture], axis=1)
-    tokens = dot(slots_ref[...], dot(tokens, heads_ref[...]).astype(bf16)).astype(bf16)
+    tokens = dot(slots_ref[...], tokens).astype(bf16)
     for head in range(HEADS):
-        pieces_ref[head] = tokens[:, head * 128 : head * 128 + 128]
-
-
-def section_step(spot, ring, other, activated, pooled, w_short, cotangent, heads, slots):
+        at = [part * 256 + head * 32 for part in range(4)]
+        pieces_ref[head] = jnp.concatenate([tokens[:, i : i + 32] for i in at], axis=1)
+
+
+def in_place(array):
+    return pltpu.with_memory_space_constraint(array, pltpu.HBM)
+
+
+def section_step(spot, ring, other, activated, pooled, w_short, cotangent, slots):
+    inputs = (spot, ring, other, in_place(activated), in_place(pooled), w_short, in_place(cotangent), slots)
     shapes = [(8, 192, 128), (192, 512), (192, 512), (1024, 512), (512, 768), (256, 512)]
     return call(
         section_kernel,
         "section",
-        [jax.ShapeDtypeStruct(shape, bf16) for shape in shapes],
-        1_500_000_000,
-        in_specs=[pl.BlockSpec(memory_space=pltpu.SMEM)]
-        + [pl.BlockSpec(memory_space=pltpu.VMEM)] * 8,
-    )(spot, ring, other, activated, pooled, w_short, cotangent, heads, slots)[:5]
+        [held(shape) for shape in shapes],
+        4_000_000_000,
+        scratch=row_buffers(),
+        in_specs=[
+            pl.BlockSpec(memory_space=space)
+            for space in (
+                pltpu.SMEM, pltpu.VMEM, pltpu.VMEM, pltpu.HBM, pltpu.HBM, pltpu.VMEM, pltpu.HBM,
+                pltpu.VMEM,
+            )
+        ],
+    )(*inputs)[:5]
 
 
 def back_kernel(
-    got_ref, heads_ref, slots_ref, section_ref, cotangent_ref, proj_ref, qkv_ref, slope_ref,
-    results_ref, d_section_ref, d_conv_ref,
+    got_ref, slots_ref, section_ref, cotangent_ref, proj_in, qkv_in, slope_in,
+    results_ref, d_section_ref, d_conv_ref, proj_ref, qkv_ref, slope_ref, sems,
 ):
+    copies = [
+        pltpu.make_async_copy(qkv_in, qkv_ref, sems.at[0]),
+        pltpu.make_async_copy(proj_in, proj_ref, sems.at[1]),
+        pltpu.make_async_copy(slope_in, slope_ref, sems.at[2]),
+    ]
+    for copy in copies:
+        copy.start()
     used = token_mask()
-    got = jnp.concatenate([got_ref[head] for head in range(HEADS)], axis=1)
-    results = dot_kt(dot_tt(slots_ref[...], got).astype(bf16), heads_ref[...])
+    got = [got_ref[head] for head in range(HEADS)]
+    got = jnp.concatenate(
+        [got[head][:, 32 * part : 32 * part + 32] for part in range(4) for head in range(HEADS)],
+        axis=1,
+    )
+    results = dot_tt(slots_ref[...], got)
     results = jnp.where(used, results, 0.0).astype(bf16)
     results_ref[...] = results
     normalized, inv_std = normalize(section_ref[...])
+    copies[0].wait()
     d_normed = dot_kt(results[:, :768], qkv_ref[...])
     d_section = cotangent_ref[...].astype(f32) + inv_std * (
         d_normed
@@ -256,24 +410,41 @@
     )
     d_section = jnp.where(used, d_section, 0.0).astype(bf16)
     d_section_ref[...] = d_section
+    copies[1].wait()
+    copies[2].wait()
     d_activated = dot_kt(d_section, proj_ref[...])
     d_conv_ref[...] = (d_activated * slope_ref[...].astype(f32)).astype(bf16)
 
 
-def back_step(*inputs):
+def back_step(got, slots, section, cotangent, proj, qkv, slope):
     shapes = [(192, 1024), (192, 512), (192, 1024)]
     return call(
         back_kernel,
         "back",
         [jax.ShapeDtypeStruct(shape, bf16) for shape in shapes],
-        1_200_000_000,
-    )(*inputs)
+        1_500_000_000,
+        scratch=[
+            pltpu.VMEM((1024, 512), bf16),
+            pltpu.VMEM((512, 768), bf16),
+            pltpu.VMEM((192, 1024), bf16),
+            pltpu.SemaphoreType.DMA((3,)),
+        ],
+        in_specs=[pl.BlockSpec(memory_space=pltpu.VMEM)] * 4
+        + [pl.BlockSpec(memory_space=pltpu.HBM)] * 3,
+    )(got, slots, section, cotangent, in_place(proj), in_place(qkv), in_place(slope))
 
 
 def parts_kernel(
-    results_ref, d_section_ref, normed_ref, cotangent_ref, activated_ref, pooled_ref, short_ref,
-    matrix_ref, rest_ref, d_pooled_ref,
+    results_ref, d_section_ref, normed_ref, cotangent_in, activated_in, pooled_in, short_ref,
+    early_ref, d_pooled_ref, activated_ref, pooled_ref, cotangent_ref, sems,
 ):
+    copies = [
+        pltpu.make_async_copy(activated_in, activated_ref, sems.at[0]),
+        pltpu.make_async_copy(pooled_in, pooled_ref, sems.at[1]),
+        pltpu.make_async_copy(cotangent_in, cotangent_ref, sems.at[2]),
+    ]
+    for copy in copies:
+        copy.start()
     results = results_ref[...]
     d_section = d_section_ref[...]
 
@@ -285,31 +456,41 @@
                 lane = piece % lanes * 128
                 index = first + piece
                 at = shard // 2 * 32 + index % 2 * 16
-                matrix_ref[shard % 2, index // 2, at : at + 16, :] = part[
+                early_ref[shard % 2, index // 2, at : at + 16, :] = part[
                     row : row + 16, lane : lane + 128
                 ]
 
+    store(dot_tt(normed_ref[...], results[:, :768]).astype(bf16), 32, 64)
+    for copy in copies:
+        copy.wait()
     store(dot_tt(activated_ref[...], d_section).astype(bf16), 0, 128)
-    store(dot_tt(normed_ref[...], results[:, :768]).astype(bf16), 32, 64)
     store(dot_tt(results[:, 768:], cotangent_ref[...]).astype(bf16), 56, 32)
     short = dot_tt(pooled_ref[...], d_section)
-    rows = [short[:, lane * 128 : lane * 128 + 128].reshape(16, 2, 8, 128) for lane in range(4)]
-    rest_ref[...] = jnp.concatenate(
-        [rows[index % 4][:, index // 4] for index in range(8)], axis=1
-    ).astype(bf16)
+    rows = [short[:, lane * 128 : lane * 128 + 128].reshape(32, 8, 128) for lane in range(4)]
+    for core in range(2):
+        early_ref[core, :, 128:144, :] = jnp.concatenate(
+            [rows[2 * core], rows[2 * core + 1]], axis=1
+        ).astype(bf16)
     d_pooled_ref[...] = dot_kt(d_section, short_ref[...]) * 0.25
 
 
-def parts_step(*inputs):
+def parts_step(results, d_section, normed, cotangent, activated, pooled, w_short):
+    inputs = (results, d_section, normed, in_place(cotangent), in_place(activated), in_place(pooled), w_short)
     return call(
         parts_kernel,
         "parts",
         [
-            jax.ShapeDtypeStruct((2, 32, 128, 128), bf16),
-            jax.ShapeDtypeStruct((16, 64, 128), bf16),
+            jax.ShapeDtypeStruct((2, 32, 144, 128), bf16),
             jax.ShapeDtypeStruct((192, 256), f32),
         ],
-        600_000_000,
+        1_000_000_000,
+        scratch=row_buffers(),
+        in_specs=[
+            pl.BlockSpec(memory_space=space)
+            for space in (
+                pltpu.VMEM, pltpu.VMEM, pltpu.VMEM, pltpu.HBM, pltpu.HBM, pltpu.HBM, pltpu.VMEM,
+            )
+        ],
     )(*inputs)
 
 
@@ -361,7 +542,7 @@
             def _():
                 total_ref[plane] += back_image
 
-    expand_ref[...] = jnp.concatenate(
+    expand_ref[0] = jnp.concatenate(
         [part_expand[:, :128].reshape(32, 8, 128), part_expand[:, 128:].reshape(32, 8, 128)],
         axis=1,
     ).astype(bf16)
@@ -383,10 +564,10 @@
         "pixel",
         [
             jax.ShapeDtypeStruct((4, 192, 256), bf16),
-            jax.ShapeDtypeStruct((32, 64, 128), bf16),
+            jax.ShapeDtypeStruct((2, 32, 32, 128), bf16),
             jax.ShapeDtypeStruct((16, 1024), f32),
         ],
-        1_200_000_000,
+        6_000_000_000,
         scratch=[pltpu.VMEM((4, 192, 256), f32)],
         grid=(4,),
         in_specs=[
@@ -395,7 +576,7 @@
         ],
         out_specs=[
             whole(4, 192, 256),
-            pl.BlockSpec((32, 16, 128), lambda step: (0, step, 0)),
+            pl.BlockSpec((1, 32, 16, 128), lambda step: (step // 2, 0, step % 2, 0)),
             chunk(16),
         ],
     )(*inputs)
@@ -407,131 +588,89 @@
     return cut.transpose(0, 2, 1, 3).reshape(rows, columns).astype(f32)
 
 
-def add_cores(halves, axis):
+def pair_sum(halves):
     core = lax.axis_index("core")
-    mine = lax.dynamic_index_in_dim(halves, core, axis, keepdims=False)
-    theirs = lax.dynamic_index_in_dim(halves, 1 - core, axis, keepdims=False)
-    return mine, theirs
-
-
-def all_sums(matrix, short, expand, depth):
-    depth = depth[:9].astype(bf16).reshape(9, 8, 128)
-    depth = jnp.pad(depth, ((0, 119), (0, 0), (0, 0))).reshape(16, 64, 128)
-    short = jnp.concatenate([short, depth], axis=0)
-    first = lax.axis_index("core") == 0
-    mine, theirs = add_cores(matrix, 0)
-    mine = jnp.concatenate([mine, jnp.where(first, expand, short)], axis=1)
-    theirs = jnp.concatenate([theirs, jnp.where(first, short, expand)], axis=1)
-    pair = (mine.astype(f32) + swap_cores(theirs).astype(f32)).astype(bf16)
-    line = jnp.sum(exchange(pair, "x").reshape(4, 8, 192, 128).astype(f32), axis=0).astype(bf16)
+    mine = lax.dynamic_index_in_dim(halves, core, 0, keepdims=False)
+    theirs = lax.dynamic_index_in_dim(halves, 1 - core, 0, keepdims=False)
+    return (mine.astype(f32) + swap_cores(theirs).astype(f32)).astype(bf16)
+
+
+def all_sums(early, expand, depth):
+    depth = jnp.pad(depth[:9].astype(bf16).reshape(9, 8, 128), ((0, 23), (0, 0), (0, 0)))
+    core = lax.axis_index("core")
+
+    def share(of):
+        own = lax.dynamic_index_in_dim(expand, of, 0, keepdims=False)
+        return jnp.concatenate([own, jnp.where(of == 0, depth, jnp.zeros((), bf16))], axis=1)
+
+    late = (share(core).astype(f32) + swap_cores(share(1 - core)).astype(f32)).astype(bf16)
+    pair = jnp.concatenate([early, late], axis=1)
+    line = jnp.sum(exchange(pair, "x").reshape(4, 8, 184, 128).astype(f32), axis=0).astype(bf16)
     sheet = jnp.sum(exchange(line, "z").astype(f32), axis=0).astype(bf16)
     column = jnp.concatenate(
-        [sheet[:128].reshape(4, 32, 128), jnp.broadcast_to(sheet[None, 128:], (4, 64, 128))], axis=1
-    )
-    column = jnp.broadcast_to(column[:, None], (4, 2, 96, 128)).reshape(8, 96, 128)
+        [sheet[:128].reshape(4, 32, 128), jnp.broadcast_to(sheet[None, 128:], (4, 56, 128))], axis=1
+    )
+    column = jnp.broadcast_to(column[:, None], (4, 2, 88, 128)).reshape(8, 88, 128)
     grad_scale = 1.0 / math.sqrt(8 * 96 * 96)
     total = jnp.sum(exchange(column, RING).astype(f32), axis=0) * grad_scale
     near = spread(total.astype(bf16), ("x", "z"), 32)
-    own = near[:, 32:].reshape(256, 8, 128)
+    own = near[:, 32:]
     other = swap_cores(own)
     matrix = near[:, :32].reshape(64, 16, 128)
     grad_proj = untiled(matrix[:32], 128, 512)
     grad_qkv = untiled(matrix[32:56], 64, 768)
     grad_out = untiled(matrix[56:], 32, 512)
-    low = jnp.where(first, own, other)
-    high = jnp.where(first, other, own)
-    grad_expand = untiled(low, 256, 1024)
-    grad_short = untiled(high[:128], 256, 512)
-    grad_depth = high[128:137].reshape(3, 3, 1024).astype(f32)
+    first = lax.axis_index("core") == 0
+    both = jnp.where(first, jnp.stack([own, other]), jnp.stack([other, own]))
+
+    def joined(start, count):
+        part = both[:, :, start : start + 8 * count].reshape(2, 32, count, 8, 128)
+        return part.transpose(1, 3, 0, 2, 4).reshape(256, 256 * count).astype(f32)
+
+    grad_short = joined(0, 2)
+    grad_expand = joined(16, 4)
+    grad_depth = both[0, :9, 48:].reshape(3, 3, 1024).astype(f32)
     return grad_expand, grad_depth, grad_short, grad_proj, grad_qkv, grad_out
 
 
-def slots16(cells, last=None):
-    rows, _, width = cells.shape
-    if last is None:
-        return jnp.pad(cells, ((0, 0), (0, 4), (0, 0)))
-    return jnp.concatenate([cells, jnp.zeros((rows, 3, width), cells.dtype), last], axis=1)
+def slots16(cells):
+    return jnp.pad(cells, ((0, 0), (0, 4), (0, 0)))
 
 
 def on_device(images, w_expand, w_depth, w_short, w_proj, w_qkv, w_out, cotangent):
     images = images[0]
     cotangent = slots16(cotangent[0])
-    ring, other = gather_weights(w_proj, w_qkv, w_out)
-    top = row_rim(images[-1:], 1)
-    left = col_rim(jnp.concatenate([top[:, -1:], images[:, -1:]], axis=0), 1)
-    heads, slots = head_order(), slot_order()
-    used = lax.broadcasted_iota(jnp.int32, (1, 16, 1), 1) < 12
-
-    cells = images.reshape(12, 2, 12, 2, 256)
-    top_cells = top.reshape(1, 12, 2, 256)
-    corner = left[:1]
-    left_cells = left[1:].reshape(12, 2, 1, 256)
-    planes = {
-        (0, 0): slots16(cells[:, 0, :, 0]),
-        (0, 1): slots16(cells[:, 0, :, 1], left_cells[:, 0]),
-        (1, 0): jnp.concatenate([slots16(top_cells[:, :, 0]), slots16(cells[:, 1, :, 0])]),
-        (1, 1): jnp.concatenate(
-            [
-                slots16(top_cells[:, :, 1], corner),
-                slots16(cells[:, 1, :, 1], left_cells[:, 1]),
-            ]
-        ),
-    }
-    expanded, slopes = {}, {}
-    for place, plane in planes.items():
-        value, slope = gelu_both(dot(plane, w_expand))
-        expanded[place] = value.astype(bf16)
-        slopes[place] = slope[place[0] :].astype(bf16)
-    taps = w_depth.astype(f32)
-
-    def window(row_tap, odd_col):
-        plane = expanded[(row_tap + 1) % 2, odd_col]
-        return plane[row_tap // 2 : row_tap // 2 + 12].astype(f32)
-
-    straight = sum(
-        window(a, 0) * taps[a, 1] + window(a, 1) * taps[a, 2] for a in range(3)
-    )
-    moved = sum(window(a, 1) * taps[a, 0] for a in range(3))
-    value, conv_slope = gelu_both(straight + jnp.roll(moved, 1, axis=1))
-    activated = value.astype(bf16)
-    conv_slope = conv_slope.astype(bf16)
-    wide = cells.astype(f32)
-    pooled = slots16(
-        ((wide[:, 0, :, 0] + wide[:, 0, :, 1] + wide[:, 1, :, 0] + wide[:, 1, :, 1]) * 0.25).astype(bf16)
-    )
-
+    top, left, ring, other = first_transfers(images, w_proj, w_qkv, w_out)
+    slots = slot_order()
+    taps16 = jnp.pad(w_depth.reshape(9, 1024), ((0, 7), (0, 0)))
+    even, odd, slopes, activated, conv_slope, cells, pooled = expand_step(
+        images, top, left, w_expand, taps16
+    )
     cotangent = cotangent.reshape(192, 512)
-    activated = activated.reshape(192, 1024)
-    pooled = pooled.reshape(192, 256)
     spot = jnp.stack([lax.axis_index("core"), lax.axis_index("ylo")]).astype(jnp.int32)
     pieces, section_out, normed, proj, qkv = section_step(
-        spot, ring, other, activated, pooled, w_short, cotangent, heads, slots
+        spot, ring, other, activated, pooled, w_short, cotangent, slots
     )
     got = exchange(pieces.reshape(64, 24, 128), GRID_AXES)
     mixed = attention(got.reshape(8, 192, 128))
     got = exchange(mixed.reshape(64, 24, 128), GRID_AXES).reshape(HEADS, 192, 128)
     results, d_section, d_conv = back_step(
-        got, heads, slots, section_out, cotangent, proj, qkv, conv_slope.reshape(192, 1024)
+        got, slots, section_out, cotangent, proj, qkv, conv_slope
     )
     below = row_rim(d_conv[:12].reshape(1, 12, 1024), -1)
     edge = d_conv.reshape(12, 16, 1024)[:, :1]
-    right = col_rim(jnp.concatenate([edge, below[:, :1]], axis=0), -1)
-    matrix, short, d_pooled = parts_step(
+    right = jnp.concatenate([col_rim(edge, -1), diagonal_rim(edge[:1], -1)], axis=0)
+    early, d_pooled = parts_step(
         results, d_section, normed, cotangent, activated, pooled, w_short
     )
-    even = jnp.stack([expanded[0, 0], expanded[0, 1]]).reshape(2, 192, 1024)
-    odd = jnp.stack([expanded[1, 0], expanded[1, 1]]).reshape(2, 208, 1024)
-    order = [(row, col) for row in range(2) for col in range(2)]
-    slope_planes = jnp.stack([slopes[place] for place in order]).reshape(4, 192, 1024)
-    cell_planes = jnp.stack([planes[place][place[0] :] for place in order]).reshape(4, 192, 256)
-    taps16 = jnp.pad(w_depth.reshape(9, 1024), ((0, 7), (0, 0)))
+    early = pair_sum(early)
     image, expand, depth = pixel_step(
-        d_conv, slots16(below), right, even, odd, slope_planes, cell_planes, w_expand, taps16,
+        d_conv, slots16(below), right, even, odd, slopes, cells, w_expand, taps16,
         d_pooled,
     )
     image = image.reshape(2, 2, 12, 16, 256)[:, :, :, :12]
     grad_image = image.transpose(2, 0, 3, 1, 4).reshape(1, 24, 24, 256)
-    return (grad_image,) + all_sums(matrix, short, expand, depth)
+    return (grad_image,) + all_sums(early, expand, depth)
 
 
 def solution(mesh):

time: 247 us -> 228 us (0.923)
  other arithmetic: 15.3 us -> 3.19 us
  local copies, waits for them, and re-layouts: 24.2 us -> 12.1 us
  matrix products: 9.1 us -> 0 us
  Pallas kernels: 17.2 us -> 25.1 us
  blocking collectives: 55.2 us -> 59.9 us
    unnamed x101 -> x32, local copies, waits for them, and re-layouts: 13.8 us -> 2.91 us
    dot_general x4 -> x0, matrix products: 9.1 us -> none  [dot(): lax.dot_general(left, right, (((left.ndim - 1,), (0,)), ((), ())), prefer...]
    another operation x9 -> x2, other arithmetic: 9.03 us -> 0.15 us  [first_transfers(): ring = jnp.stack([own, above, far, below])]
    pallas_call x2 -> x3, Pallas kernels: 3.88 us -> 11.1 us  [the longest x1 5.38 us: expand_step(): call(expand_kernel, 'expand', [held(shape) for shape in shapes], 60000000...]
    all_to_all x3, waiting for transfers between devices: 37 us -> 44 us  [exchange(): return lax.all_to_all(block, axes, 0, 0, tiled=True)]
    ppermute x3 -> x5, starting transfers between devices: 10.3 us -> 15.8 us  [the longest x1 5.1 us: first_transfers(): above = lax.ppermute(own, RING, around(7))]
    all_to_all x3, blocking collectives: 55.2 us -> 59.9 us  [exchange(): return lax.all_to_all(block, axes, 0, 0, tiled=True)]
    all_to_all x3, starting transfers between devices: 34.7 us -> 31.6 us  [exchange(): return lax.all_to_all(block, axes, 0, 0, tiled=True)]
  transfers between devices with their start and end apart: 13 -> 16, of which waited for: 6 -> 5; matrix products, arithmetic and copies ran while one was open for 11% -> 4% of each run, Pallas kernels for 0% -> 6%
where the time goes in v4:
time: 228 us; the launch traced here: 227 us
  starting transfers between devices  78.9 us (35%)
  blocking collectives  59.9 us (26%)
  waiting for transfers between devices  46.2 us (20%)
  Pallas kernels  25.1 us (11%)
  local copies, waits for them, and re-layouts  12.1 us (5%)
  other arithmetic  3.19 us (1%)
    all_to_all x3, blocking collectives, exchange(): return lax.all_to_all(block, axes, 0, 0, tiled=True)  59.9 us
    all_to_all x3, waiting for transfers between devices, exchange(): return lax.all_to_all(block, axes, 0, 0, tiled=True)  44 us
    all_to_all x3, starting transfers between devices, exchange(): return lax.all_to_all(block, axes, 0, 0, tiled=True)  31.6 us
    ppermute x4, starting transfers between devices, swap_cores(): return lax.ppermute(block, 'core', [(0, 1), (1, 0)])  20.7 us
    pallas_call x1, Pallas kernels, attention(): pl.pallas_call(attention_kernel, out_shape=jax.ShapeDtypeStruct((8, 192,...  6.33 us
    ppermute x2, starting transfers between devices, col_rim(): return lax.ppermute(edge, COL, step_route(PARTS, distance))  5.42 us
    ppermute x2, starting transfers between devices, row_rim(): return lax.ppermute(edge, ROW, step_route(PARTS, distance))  5.41 us
    pallas_call x1, Pallas kernels, expand_step(): call(expand_kernel, 'expand', [held(shape) for shape in shapes], 60000000...  5.38 us
  transfers between devices with their start and end apart: 16, of which 5 were waited for; matrix products, arithmetic and copies ran while one was open for 4% of the time, Pallas kernels for 6%

profile of v4, /device:TPU:1, one launch (start us, length us, event | category | flops | bytes accessed | tf_op | source)
XLA Modules:
  0.0 226.8 jit_solution(16334797024040259616)
XLA Ops:
  1.3 3.9 %collective-permute-start = (bf16[1,24,256]{2,1,0:T(8,128)(2,1)S(1)}, bf16[1,24,256]{2,1,0:T(8,128)(2,1)S(1)}, u32[]{:S(2)}, u32[]{:S(2)}) collective-permute-start(bf16[1,24,256]{2,1,0:T(8,128)(2,1)S(1)} %slice_bitcast_fusion.4), channel_id=1, source_target_pairs={{0,8},{8,16},{16,24},{24,32},{32,40},{40,48},{48,56},{1,9},{9,17},... | collective-permute-start | bytes 36872 | tf_op jit(solution)/shard_map/ppermute | solution.py:69
  6.9 0.9 maximum_maximum_fusion
  7.8 5.1 %collective-permute-start.1 = (bf16[256,512]{1,0:T(8,128)(2,1)S(1)}, bf16[256,512]{1,0:T(8,128)(2,1)S(1)}, u32[]{:S(2)}, u32[]{:S(2)}) collective-permute-start(bf16[256,512]{1,0:T(8,128)(2,1)S(1)} %maximum_maximum_fusion), channel_id=1, source_target_pairs={{0,416},{128,0},{256,128},{384,256},{32,384},{160,32},{288,160},{4... | collective-permute-start | bytes 786440 | tf_op jit(solution)/shard_map/ppermute | solution.py:110
  12.9 1.9 collective-permute-start.4
  14.9 2.6 %collective-permute-start.2 = (bf16[128,512]{1,0:T(8,128)(2,1)S(1)}, bf16[128,512]{1,0:T(8,128)(2,1)S(1)}, u32[]{:S(2)}, u32[]{:S(2)}) collective-permute-start(bf16[128,512]{1,0:T(8,128)(2,1)S(1)} %get-tuple-element.59), channel_id=1, source_target_pairs={{0,256},{128,384},{256,32},{384,160},{32,288},{160,416},{288,0},{4... | collective-permute-start | bytes 393224 | tf_op jit(solution)/shard_map/ppermute | solution.py:114
  17.5 4.9 %collective-permute-start.3 = (bf16[128,512]{1,0:T(8,128)(2,1)S(1)}, bf16[128,512]{1,0:T(8,128)(2,1)S(1)}, u32[]{:S(2)}, u32[]{:S(2)}) collective-permute-start(bf16[128,512]{1,0:T(8,128)(2,1)S(1)} %get-tuple-element.60), channel_id=1, source_target_pairs={{0,288},{128,416},{256,0},{384,128},{32,256},{160,384},{288,32},{4... | collective-permute-start | bytes 393224 | tf_op jit(solution)/shard_map/ppermute | solution.py:114
  23.5 4.1 %collective-permute-start.5 = (bf16[25,1,256]{2,1,0:T(2,128)(2,1)S(1)}, bf16[25,1,256]{2,1,0:T(2,128)(2,1)S(1)}, u32[]{:S(2)}, u32[]{:S(2)}) collective-permute-start(bf16[25,1,256]{2,1,0:T(2,128)(2,1)S(1)} %pad_maximum_fusion.5), channel_id=1, source_target_pairs={{0,1},{1,2},{2,3},{3,4},{4,5},{5,6},{6,7},{8,9},{9,10},{10,11},{11... | collective-permute-start | bytes 38408 | tf_op jit(solution)/shard_map/ppermute | solution.py:73
  28.5 4.5 %collective-permute-start.6 = (bf16[4,256,512]{2,1,0:T(8,128)(2,1)S(1)}, bf16[4,256,512]{2,1,0:T(8,128)(2,1)S(1)}, u32[]{:S(2)}, u32[]{:S(2)}) collective-permute-start(bf16[4,256,512]{2,1,0:T(8,128)(2,1)S(1)} %pad_maximum_fusion.1.ring_ref), channel_id=1, source_target_pairs={{0,64},{64,0},{1,65},{65,1},{2,66},{66,2},{3,67},{67,3},{4,68},{68... | collective-permute-start | bytes 3145736 | tf_op jit(solution)/shard_map/ppermute | solution.py:92
  34.0 5.4 %expand.1 = (bf16[2,192,1024]{2,1,0:T(8,128)(2,1)}, bf16[2,208,1024]{2,1,0:T(8,128)(2,1)}, bf16[4,192,1024]{2,1,0:T(8,128)(2,1)}, bf16[192,1024]{1,0:T(8,128)(2,...) custom-call(bf16[24,24,256]{2,1,0:T(8,128)(2,1)S(1)} %bitcast.95, ...), custom_call_target="tpu_custom_call" | custom-call | flops 6000000000 | bytes 8000000 | tf_op jit(solution)/shard_map/expand/pallas_call | solution.py:288
  39.4 3.8 %section.1 = (bf16[8,192,128]{2,1,0:T(8,128)(2,1)}, bf16[192,512]{1,0:T(8,128)(2,1)}, bf16[192,512]{1,0:T(8,128)(2,1)}, bf16[1024,512]{1,0:T(8,128)(2,1)}, bf16[...) custom-call(s32[2]{0:T(128)S(1)} %pad_add_fusion.spot_ref, bf16[4,256,512]{2,1,0:T(8,128)(2,1)S(1)} %pad_maximum_fusion.1.ring_ref, ...), custom_call_target="tpu_custom_call" | custom-call | flops 4000000000 | bytes 8000000 | tf_op jit(solution)/shard_map/section/pallas_call | solution.py:367
  43.2 18.2 %all-to-all-start = ((bf16[64,24,128]{2,1,0:T(8,128)(2,1)}), bf16[64,24,128]{2,1,0:T(8,128)(2,1)S(1)}, u32[]{:S(2)}, u32[]{:S(2)}) async-start(bf16[64,24,128]{2,1,0:T(8,128)(2,1)} %bitcast.106), calls=%async_computation | async-start | bytes 786432 | tf_op jit(solution)/shard_map/all_to_all | solution.py:96
  61.9 15.2 %all-to-all-done = bf16[64,24,128]{2,1,0:T(8,128)(2,1)S(1)} async-done(((bf16[64,24,128]{2,1,0:T(8,128)(2,1)}), bf16[64,24,128]{2,1,0:T(8,128)(2,1)S(1)}, u32[]{:S(2)}, u32[]{:S(2)}) %all-to-all-start) | async-done | bytes 393248 | tf_op jit(solution)/shard_map/all_to_all | solution.py:96
  77.9 6.3 %attention.1 = bf16[8,192,128]{2,1,0:T(8,128)(2,1)} custom-call(bf16[8,192,128]{2,1,0:T(8,128)(2,1)} %bitcast.107, bf16[192,192]{1,0:T(8,128)(2,1)} %constant.92.clone.order_ref, f32[1,192]{1,0:T(1,128)} %or_convert_fusion.valid_ref), custom_call_target="tpu_custom_call" | custom-call | flops 7000000000 | bytes 1000000 | tf_op jit(solution)/shard_map/attention/pallas_call | solution.py:174
  84.3 9.0 %all-to-all-start.1 = ((bf16[64,24,128]{2,1,0:T(8,128)(2,1)}), bf16[64,24,128]{2,1,0:T(8,128)(2,1)S(1)}, u32[]{:S(2)}, u32[]{:S(2)}) async-start(bf16[64,24,128]{2,1,0:T(8,128)(2,1)} %bitcast.105), calls=%async_computation.1 | async-start | bytes 786432 | tf_op jit(solution)/shard_map/all_to_all | solution.py:96
  93.2 15.2 %all-to-all-done.1 = bf16[64,24,128]{2,1,0:T(8,128)(2,1)S(1)} async-done(((bf16[64,24,128]{2,1,0:T(8,128)(2,1)}), bf16[64,24,128]{2,1,0:T(8,128)(2,1)S(1)}, u32[]{:S(2)}, u32[]{:S(2)}) %all-to-all-start.1) | async-done | bytes 393248 | tf_op jit(solution)/shard_map/all_to_all | solution.py:96
  108.4 2.3 back.1
  110.8 1.3 collective-permute-start.8
  112.1 1.3 collective-permute-start.9
  113.4 1.5 collective-permute-start.7
  114.9 2.0 parts.1
  117.0 4.5 %collective-permute-start.10 = (bf16[32,144,128]{2,1,0:T(8,128)(2,1)S(1)}, bf16[32,144,128]{2,1,0:T(8,128)(2,1)S(1)}, u32[]{:S(2)}, u32[]{:S(2)}) collective-permute-start(bf16[32,144,128]{2,1,0:T(8,128)(2,1)S(1)} %dynamic-slice_bitcast_fusion), channel_id=1, source_target_pairs={{0,64},{64,0},{1,65},{65,1},{2,66},{66,2},{3,67},{67,3},{4,68},{68... | collective-permute-start | bytes 3538952 | tf_op jit(solution)/shard_map/ppermute | solution.py:92
  121.6 5.4 %pixel.1 = (bf16[4,192,256]{2,1,0:T(8,128)(2,1)S(1)}, bf16[2,32,32,128]{3,2,1,0:T(8,128)(2,1)S(1)}, f32[16,1024]{1,0:T(8,128)S(1)}) custom-call(bf16[192,1024]{1,0:T(8,128)(2,1)S(1)} %get-tuple-element.42.d_conv_ref, bf16[1,16,1024]{2,1,0:T(8,128)(2,1)S(1)} %pad.18.below_ref, bf16[13,1,1024]{2,1,0:T(2,128)(2,1)S(1)} %pad_maximum_fusion.4.right_ref, ...), custom_call_target="tpu_custom_call" | custom-call | flops 6000000000 | bytes 8000000 | tf_op jit(solution)/shard_map/pixel/pallas_call | solution.py:562
  127.1 2.1 collective-permute-start.11
  129.2 1.5 collective-permute-done.11
  131.2 27.8 %all_to_all.30 = bf16[32,184,128]{2,1,0:T(8,128)(2,1)S(1)} all-to-all(bf16[32,184,128]{2,1,0:T(8,128)(2,1)S(1)} %pad_maximum_fusion), channel_id=1, replica_groups=mesh['ylo'=4,'core'=2,'yhi'=2,'x'=4,'z'=8] {'x'}, dimensions={0} | all-to-all | bytes 3014656 | tf_op jit(solution)/shard_map/all_to_all | solution.py:96
  159.4 19.1 %all_to_all.31 = bf16[8,184,128]{2,1,0:T(8,128)(2,1)S(1)} all-to-all(bf16[8,184,128]{2,1,0:T(8,128)(2,1)S(1)} %reduce_sum.33), channel_id=1, replica_groups=mesh['ylo'=4,'core'=2,'yhi'=2,'x'=4,'z'=8] {'z'}, dimensions={0} | all-to-all | bytes 753664 | tf_op jit(solution)/shard_map/all_to_all | solution.py:96
  178.6 13.0 %all_to_all.32 = bf16[8,88,128]{2,1,0:T(8,128)(2,1)S(1)} all-to-all(bf16[8,88,128]{2,1,0:T(8,128)(2,1)S(1)} %bitcast.101), channel_id=1, replica_groups=mesh['ylo'=4,'core'=2,'yhi'=2,'x'=4,'z'=8] {'ylo','yhi'}, dimensions={0} | all-to-all | bytes 360448 | tf_op jit(solution)/shard_map/all_to_all | solution.py:96
  191.6 1.0 broadcast_in_dim.26
  192.6 4.5 %all-to-all-start.5 = ((bf16[32,88,128]{2,1,0:T(8,128)(2,1)}), bf16[32,88,128]{2,1,0:T(8,128)(2,1)S(1)}, u32[]{:S(2)}, u32[]{:S(2)}) async-start(bf16[32,88,128]{2,1,0:T(8,128)(2,1)} %broadcast_in_dim.26), calls=%async_computation.5 | async-start | bytes 1441792 | tf_op jit(solution)/shard_map/all_to_all | solution.py:96
  198.3 13.6 %all-to-all-done.5 = bf16[32,88,128]{2,1,0:T(8,128)(2,1)S(1)} async-done(((bf16[32,88,128]{2,1,0:T(8,128)(2,1)}), bf16[32,88,128]{2,1,0:T(8,128)(2,1)S(1)}, u32[]{:S(2)}, u32[]{:S(2)}) %all-to-all-start.5) | async-done | bytes 720928 | tf_op jit(solution)/shard_map/all_to_all | solution.py:96
  212.0 9.6 %collective-permute-start.12 = (bf16[32,56,128]{2,1,0:T(8,128)(2,1)S(1)}, bf16[32,56,128]{2,1,0:T(8,128)(2,1)S(1)}, u32[]{:S(2)}, u32[]{:S(2)}) collective-permute-start(bf16[32,56,128]{2,1,0:T(8,128)(2,1)S(1)} %get-tuple-element.56), channel_id=1, source_target_pairs={{0,64},{64,0},{1,65},{65,1},{2,66},{66,2},{3,67},{67,3},{4,68},{68... | collective-permute-start | bytes 1376264 | tf_op jit(solution)/shard_map/ppermute | solution.py:92
  224.3 1.1 copy.31
  (101 shorter events, 13.1 us)
Async XLA Ops:
  1.3 13.5 %collective-permute-start = (bf16[1,24,256]{2,1,0:T(8,128)(2,1)S(1)}, bf16[1,24,256]{2,1,0:T(8,128)(2,1)S(1)}, u32[]{:S(2)}, u32[]{:S(2)}) collective-permute-start(bf16[1,24,256]{2,1,0:T(8,128)(2,1)S(1)} %slice_bitcast_fusion.4), channel_id=1, source_target_pairs={{0,8},{8,16},{16,24},{24,32},{32,40},{40,48},{48,56},{1,9},{9,17},... | collective-permute-start | bytes 36872 | tf_op jit(solution)/shard_map/ppermute | solution.py:69
  7.8 19.9 %collective-permute-start.1 = (bf16[256,512]{1,0:T(8,128)(2,1)S(1)}, bf16[256,512]{1,0:T(8,128)(2,1)S(1)}, u32[]{:S(2)}, u32[]{:S(2)}) collective-permute-start(bf16[256,512]{1,0:T(8,128)(2,1)S(1)} %maximum_maximum_fusion), channel_id=1, source_target_pairs={{0,416},{128,0},{256,128},{384,256},{32,384},{160,32},{288,160},{4... | collective-permute-start | bytes 786440 | tf_op jit(solution)/shard_map/ppermute | solution.py:110
  12.9 14.8 %collective-permute-start.4 = (bf16[256,512]{1,0:T(8,128)(2,1)S(1)}, bf16[256,512]{1,0:T(8,128)(2,1)S(1)}, u32[]{:S(2)}, u32[]{:S(2)}) collective-permute-start(bf16[256,512]{1,0:T(8,128)(2,1)S(1)} %maximum_maximum_fusion), channel_id=1, source_target_pairs={{0,128},{128,256},{256,384},{384,32},{32,160},{160,288},{288,416},... | collective-permute-start | bytes 786440 | tf_op jit(solution)/shard_map/ppermute | solution.py:109
  14.9 18.2 %copy-start.13 = (bf16[3,3,1024]{2,1,0:T(4,128)(2,1)S(1)}, bf16[3,3,1024]{2,1,0:T(4,128)(2,1)}, u32[]{:S(2)}) copy-start(bf16[3,3,1024]{2,1,0:T(4,128)(2,1)} %param.12) | copy-start | bytes 55300
  14.9 18.3 %copy-start.11 = (bf16[1,12,12,512]{3,2,1,0:T(8,128)(2,1)S(1)}, bf16[1,12,12,512]{3,2,1,0:T(8,128)(2,1)}, u32[]{:S(2)}) copy-start(bf16[1,12,12,512]{3,2,1,0:T(8,128)(2,1)} %param.17) | copy-start | bytes 442372
  14.9 12.7 %collective-permute-start.2 = (bf16[128,512]{1,0:T(8,128)(2,1)S(1)}, bf16[128,512]{1,0:T(8,128)(2,1)S(1)}, u32[]{:S(2)}, u32[]{:S(2)}) collective-permute-start(bf16[128,512]{1,0:T(8,128)(2,1)S(1)} %get-tuple-element.59), channel_id=1, source_target_pairs={{0,256},{128,384},{256,32},{384,160},{32,288},{160,416},{288,0},{4... | collective-permute-start | bytes 393224 | tf_op jit(solution)/shard_map/ppermute | solution.py:114
  17.5 10.1 %collective-permute-start.3 = (bf16[128,512]{1,0:T(8,128)(2,1)S(1)}, bf16[128,512]{1,0:T(8,128)(2,1)S(1)}, u32[]{:S(2)}, u32[]{:S(2)}) collective-permute-start(bf16[128,512]{1,0:T(8,128)(2,1)S(1)} %get-tuple-element.60), channel_id=1, source_target_pairs={{0,288},{128,416},{256,0},{384,128},{32,256},{160,384},{288,32},{4... | collective-permute-start | bytes 393224 | tf_op jit(solution)/shard_map/ppermute | solution.py:114
  23.4 10.5 %copy-start.12 = (bf16[2,192,192]{2,1,0:T(8,128)(2,1)S(1)}, bf16[2,192,192]{2,1,0:T(8,128)(2,1)}, u32[]{:S(2)}) copy-start(bf16[2,192,192]{2,1,0:T(8,128)(2,1)} %constant.91.clone) | copy-start | bytes 442372
  23.5 5.1 %collective-permute-start.5 = (bf16[25,1,256]{2,1,0:T(2,128)(2,1)S(1)}, bf16[25,1,256]{2,1,0:T(2,128)(2,1)S(1)}, u32[]{:S(2)}, u32[]{:S(2)}) collective-permute-start(bf16[25,1,256]{2,1,0:T(2,128)(2,1)S(1)} %pad_maximum_fusion.5), channel_id=1, source_target_pairs={{0,1},{1,2},{2,3},{3,4},{4,5},{5,6},{6,7},{8,9},{9,10},{10,11},{11... | collective-permute-start | bytes 38408 | tf_op jit(solution)/shard_map/ppermute | solution.py:73
  27.6 6.3 %copy-start.1 = (bf16[1,24,24,256]{3,2,1,0:T(8,128)(2,1)S(1)}, bf16[1,24,24,256]{3,2,1,0:T(8,128)(2,1)}, u32[]{:S(2)}) copy-start(bf16[1,24,24,256]{3,2,1,0:T(8,128)(2,1)} %param.10) | copy-start | bytes 884740
  27.7 6.3 %copy-start.2 = (bf16[256,1024]{1,0:T(8,128)(2,1)S(1)}, bf16[256,1024]{1,0:T(8,128)(2,1)}, u32[]{:S(2)}) copy-start(bf16[256,1024]{1,0:T(8,128)(2,1)} %w_expand_ref.3) | copy-start | bytes 1572868
  28.5 10.8 %collective-permute-start.6 = (bf16[4,256,512]{2,1,0:T(8,128)(2,1)S(1)}, bf16[4,256,512]{2,1,0:T(8,128)(2,1)S(1)}, u32[]{:S(2)}, u32[]{:S(2)}) collective-permute-start(bf16[4,256,512]{2,1,0:T(8,128)(2,1)S(1)} %pad_maximum_fusion.1.ring_ref), channel_id=1, source_target_pairs={{0,64},{64,0},{1,65},{65,1},{2,66},{66,2},{3,67},{67,3},{4,68},{68... | collective-permute-start | bytes 3145736 | tf_op jit(solution)/shard_map/ppermute | solution.py:92
  34.0 5.4 %copy-start.3 = (bf16[256,512]{1,0:T(8,128)(2,1)S(1)}, bf16[256,512]{1,0:T(8,128)(2,1)}, u32[]{:S(2)}) copy-start(bf16[256,512]{1,0:T(8,128)(2,1)} %short_ref.3) | copy-start | bytes 786436
  43.2 34.0 %all-to-all-start = ((bf16[64,24,128]{2,1,0:T(8,128)(2,1)}), bf16[64,24,128]{2,1,0:T(8,128)(2,1)S(1)}, u32[]{:S(2)}, u32[]{:S(2)}) async-start(bf16[64,24,128]{2,1,0:T(8,128)(2,1)} %bitcast.106), calls=%async_computation | async-start | bytes 786432 | tf_op jit(solution)/shard_map/all_to_all | solution.py:96
  77.2 0.8 copy-start.10
  77.9 30.5 %copy-start = (bf16[12,16,512]{2,1,0:T(8,128)(2,1)S(1)}, bf16[12,16,512]{2,1,0:T(8,128)(2,1)}, u32[]{:S(2)}) copy-start(bf16[12,16,512]{2,1,0:T(8,128)(2,1)} %pad.17) | copy-start | bytes 589828
  77.9 30.5 %copy-start.5 = (bf16[192,512]{1,0:T(8,128)(2,1)S(1)}, bf16[192,512]{1,0:T(8,128)(2,1)}, u32[]{:S(2)}) copy-start(bf16[192,512]{1,0:T(8,128)(2,1)} %get-tuple-element.38.section_ref) | copy-start | bytes 589828
  84.3 24.2 %all-to-all-start.1 = ((bf16[64,24,128]{2,1,0:T(8,128)(2,1)}), bf16[64,24,128]{2,1,0:T(8,128)(2,1)S(1)}, u32[]{:S(2)}, u32[]{:S(2)}) async-start(bf16[64,24,128]{2,1,0:T(8,128)(2,1)} %bitcast.105), calls=%async_computation.1 | async-start | bytes 786432 | tf_op jit(solution)/shard_map/all_to_all | solution.py:96
  108.4 6.4 %copy-start.4 = (bf16[192,512]{1,0:T(8,128)(2,1)S(1)}, bf16[192,512]{1,0:T(8,128)(2,1)}, u32[]{:S(2)}) copy-start(bf16[192,512]{1,0:T(8,128)(2,1)} %get-tuple-element.49.normed_ref) | copy-start | bytes 589828
  110.8 10.7 %collective-permute-start.8 = (bf16[12,1,1024]{2,1,0:T(2,128)(2,1)S(1)}, bf16[12,1,1024]{2,1,0:T(2,128)(2,1)S(1)}, u32[]{:S(2)}, u32[]{:S(2)}) collective-permute-start(bf16[12,1,1024]{2,1,0:T(2,128)(2,1)S(1)} %slice.105), channel_id=1, source_target_pairs={{1,0},{2,1},{3,2},{4,3},{5,4},{6,5},{7,6},{9,8},{10,9},{11,10},{12... | collective-permute-start | bytes 73736 | tf_op jit(solution)/shard_map/ppermute | solution.py:73
  112.1 9.4 %collective-permute-start.9 = (bf16[1,1,1024]{2,1,0:T(2,128)(2,1)S(1)}, bf16[1,1,1024]{2,1,0:T(2,128)(2,1)S(1)}, u32[]{:S(2)}, u32[]{:S(2)}) collective-permute-start(bf16[1,1,1024]{2,1,0:T(2,128)(2,1)S(1)} %slice.106), channel_id=1, source_target_pairs={{9,0},{10,1},{11,2},{12,3},{13,4},{14,5},{15,6},{17,8},{18,9},{19,... | collective-permute-start | bytes 6152 | tf_op jit(solution)/shard_map/ppermute | solution.py:83
  113.4 8.1 %collective-permute-start.7 = (bf16[1,12,1024]{2,1,0:T(8,128)(2,1)S(1)}, bf16[1,12,1024]{2,1,0:T(8,128)(2,1)S(1)}, u32[]{:S(2)}, u32[]{:S(2)}) collective-permute-start(bf16[1,12,1024]{2,1,0:T(8,128)(2,1)S(1)} %slice_bitcast_fusion.3), channel_id=1, source_target_pairs={{8,0},{16,8},{24,16},{32,24},{40,32},{48,40},{56,48},{9,1},{17,9},... | collective-permute-start | bytes 73736 | tf_op jit(solution)/shard_map/ppermute | solution.py:69
  114.9 6.7 %copy-start.8 = (bf16[2,192,1024]{2,1,0:T(8,128)(2,1)S(1)}, bf16[2,192,1024]{2,1,0:T(8,128)(2,1)}, u32[]{:S(2)}) copy-start(bf16[2,192,1024]{2,1,0:T(8,128)(2,1)} %get-tuple-element.43.even_ref) | copy-start | bytes 2359300
  114.9 6.7 %copy-start.9 = (bf16[4,192,256]{2,1,0:T(8,128)(2,1)S(1)}, bf16[4,192,256]{2,1,0:T(8,128)(2,1)}, u32[]{:S(2)}) copy-start(bf16[4,192,256]{2,1,0:T(8,128)(2,1)} %get-tuple-element.46.cells_ref) | copy-start | bytes 1179652
  116.8 4.8 %copy-start.6 = (bf16[4,192,1024]{2,1,0:T(8,128)(2,1)S(1)}, bf16[4,192,1024]{2,1,0:T(8,128)(2,1)}, u32[]{:S(2)}) copy-start(bf16[4,192,1024]{2,1,0:T(8,128)(2,1)} %get-tuple-element.45.slopes_ref) | copy-start | bytes 4718596
  116.8 4.8 %copy-start.7 = (bf16[2,208,1024]{2,1,0:T(8,128)(2,1)S(1)}, bf16[2,208,1024]{2,1,0:T(8,128)(2,1)}, u32[]{:S(2)}) copy-start(bf16[2,208,1024]{2,1,0:T(8,128)(2,1)} %get-tuple-element.44.odd_ref) | copy-start | bytes 2555908
  117.0 13.8 %collective-permute-start.10 = (bf16[32,144,128]{2,1,0:T(8,128)(2,1)S(1)}, bf16[32,144,128]{2,1,0:T(8,128)(2,1)S(1)}, u32[]{:S(2)}, u32[]{:S(2)}) collective-permute-start(bf16[32,144,128]{2,1,0:T(8,128)(2,1)S(1)} %dynamic-slice_bitcast_fusion), channel_id=1, source_target_pairs={{0,64},{64,0},{1,65},{65,1},{2,66},{66,2},{3,67},{67,3},{4,68},{68... | collective-permute-start | bytes 3538952 | tf_op jit(solution)/shard_map/ppermute | solution.py:92
  127.1 3.5 %collective-permute-start.11 = (bf16[32,40,128]{2,1,0:T(8,128)(2,1)S(1)}, bf16[32,40,128]{2,1,0:T(8,128)(2,1)S(1)}, u32[]{:S(2)}, u32[]{:S(2)}) collective-permute-start(bf16[32,40,128]{2,1,0:T(8,128)(2,1)S(1)} %pad_maximum_fusion.2), channel_id=1, source_target_pairs={{0,64},{64,0},{1,65},{65,1},{2,66},{66,2},{3,67},{67,3},{4,68},{68... | collective-permute-start | bytes 983048 | tf_op jit(solution)/shard_map/ppermute | solution.py:92
  192.6 19.3 %all-to-all-start.5 = ((bf16[32,88,128]{2,1,0:T(8,128)(2,1)}), bf16[32,88,128]{2,1,0:T(8,128)(2,1)S(1)}, u32[]{:S(2)}, u32[]{:S(2)}) async-start(bf16[32,88,128]{2,1,0:T(8,128)(2,1)} %broadcast_in_dim.26), calls=%async_computation.5 | async-start | bytes 1441792 | tf_op jit(solution)/shard_map/all_to_all | solution.py:96
  212.0 12.0 %collective-permute-start.12 = (bf16[32,56,128]{2,1,0:T(8,128)(2,1)S(1)}, bf16[32,56,128]{2,1,0:T(8,128)(2,1)S(1)}, u32[]{:S(2)}, u32[]{:S(2)}) collective-permute-start(bf16[32,56,128]{2,1,0:T(8,128)(2,1)S(1)} %get-tuple-element.56), channel_id=1, source_target_pairs={{0,64},{64,0},{1,65},{65,1},{2,66},{66,2},{3,67},{67,3},{4,68},{68... | collective-permute-start | bytes 1376264 | tf_op jit(solution)/shard_map/ppermute | solution.py:92

commit v5 on v4

--- a/solution.py
+++ b/solution.py
@@ -28,11 +28,11 @@
 
 
 def gelu_both(values):
-    inner = jnp.tanh(tanh_coeff * (values + cubic_coeff * values * values * values))
-    value = 0.5 * values * (1.0 + inner)
-    slope = 0.5 * (1.0 + inner) + 0.5 * values * (1.0 - inner * inner) * tanh_coeff * (
-        1.0 + 3.0 * cubic_coeff * values * values
-    )
+    square = values * values
+    inner = jnp.tanh(values * (tanh_coeff * cubic_coeff * square + tanh_coeff))
+    half = 0.5 * inner + 0.5
+    value = values * half
+    slope = half + value * (1.0 - inner) * (3.0 * tanh_coeff * cubic_coeff * square + tanh_coeff)
     return value, slope
 
 
@@ -100,11 +100,49 @@
     return exchange(jnp.broadcast_to(block[None], (count,) + block.shape), axes)
 
 
+def call(body, name, out_shape, flops, scratch=(), **rest):
+    return pl.pallas_call(
+        body,
+        out_shape=out_shape,
+        scratch_shapes=scratch,
+        compiler_params=pltpu.CompilerParams(vmem_limit_bytes=24 * 1024 * 1024),
+        cost_estimate=pl.CostEstimate(flops=flops, bytes_accessed=8_000_000, transcendentals=0),
+        name=name,
+        **rest,
+    )
+
+
+def in_place(array):
+    return pltpu.with_memory_space_constraint(array, pltpu.HBM)
+
+
+def shard_kernel(proj_ref, qkv_ref, out_ref, own_ref, sems):
+    moves = [
+        (proj_ref, own_ref.at[0:128]),
+        (qkv_ref.at[:, 0:512], own_ref.at[128:192]),
+        (out_ref, own_ref.at[192:224]),
+        (qkv_ref.at[0:32, 512:768], own_ref.at[224:256, 0:256]),
+        (qkv_ref.at[32:64, 512:768], own_ref.at[224:256, 256:512]),
+    ]
+    copies = [
+        pltpu.make_async_copy(source, target, sems.at[index])
+        for index, (source, target) in enumerate(moves)
+    ]
+    for copy in copies:
+        copy.start()
+    for copy in copies:
+        copy.wait()
+
+
 def first_transfers(images, w_proj, w_qkv, w_out):
-    tail = w_qkv[:, 512:]
-    own = jnp.concatenate(
-        [w_proj, w_qkv[:, :512], w_out, jnp.concatenate([tail[:32], tail[32:]], axis=1)], axis=0
-    )
+    own = call(
+        shard_kernel,
+        "shard",
+        jax.ShapeDtypeStruct((256, 512), bf16),
+        1_000_000,
+        scratch=[pltpu.SemaphoreType.DMA((5,))],
+        in_specs=[pl.BlockSpec(memory_space=pltpu.HBM)] * 3,
+    )(in_place(w_proj), in_place(w_qkv), in_place(w_out))
     top = row_rim(images[-1:], 1)
     below = lax.ppermute(own, RING, around(1))
     above = lax.ppermute(own, RING, around(7))
@@ -150,7 +188,7 @@
         unit = jnp.concatenate([sorted_ref[at : at + 16] for at in blocks], axis=0)
         query, key, value, d_mix = (unit[:, 32 * i : 32 * i + 32] for i in range(4))
         raised = jnp.where(valid, jnp.exp(dot_kt(query, key) * scale), 0.0)
-        weights32 = raised / jnp.sum(raised, axis=-1, keepdims=True)
+        weights32 = raised * (1.0 / jnp.sum(raised, axis=-1, keepdims=True))
         weights = weights32.astype(bf16)
         mixture = dot(weights, value)
         d_weights = dot_kt(d_mix, value)
@@ -191,18 +229,6 @@
     centred = wide - jnp.mean(wide, axis=-1, keepdims=True)
     inv_std = lax.rsqrt(jnp.mean(centred * centred, axis=-1, keepdims=True) + norm_epsilon)
     return centred * inv_std, inv_std
-
-
-def call(body, name, out_shape, flops, scratch=(), **rest):
-    return pl.pallas_call(
-        body,
-        out_shape=out_shape,
-        scratch_shapes=scratch,
-        compiler_params=pltpu.CompilerParams(vmem_limit_bytes=24 * 1024 * 1024),
-        cost_estimate=pl.CostEstimate(flops=flops, bytes_accessed=8_000_000, transcendentals=0),
-        name=name,
-        **rest,
-    )
 
 
 def held(shape, dtype=bf16):
@@ -298,7 +324,7 @@
             pltpu.VMEM((4, 208, 256), bf16),
         ],
         grid=(4,),
-        in_specs=[whole(24, 24, 256), whole(1, 24, 256), whole(25, 1, 256), chunk(256), chunk(16)],
+        in_specs=[whole(24, 24, 256), whole(1, 24, 256), whole(25, 1, 256), chunk(256), chunk(9)],
         out_specs=[
             chunk(2, 192), chunk(2, 208), chunk(4, 192), chunk(192), chunk(192),
             whole(4, 192, 256), whole(192, 256),
@@ -357,10 +383,6 @@
         pieces_ref[head] = jnp.concatenate([tokens[:, i : i + 32] for i in at], axis=1)
 
 
-def in_place(array):
-    return pltpu.with_memory_space_constraint(array, pltpu.HBM)
-
-
 def section_step(spot, ring, other, activated, pooled, w_short, cotangent, slots):
     inputs = (spot, ring, other, in_place(activated), in_place(pooled), w_short, in_place(cotangent), slots)
     shapes = [(8, 192, 128), (192, 512), (192, 512), (1024, 512), (512, 768), (256, 512)]
@@ -498,67 +520,57 @@
     d_conv_ref, below_ref, right_ref, even_ref, odd_ref, slopes_ref, cells_ref, w_expand_ref,
     taps_ref, d_pooled_ref, image_ref, expand_ref, depth_ref, total_ref,
 ):
-    step = pl.program_id(0)
     slot = lax.broadcasted_iota(jnp.int32, (1, 16, 1), 1)
-    here = d_conv_ref[...].astype(f32).reshape(12, 16, 256)
-    rows = jnp.concatenate([here, below_ref[...].astype(f32)], axis=0)
-    turned = pltpu.roll(rows, 15, 1)
-    after = jnp.where(slot == 11, right_ref[...].astype(f32), turned)
-    back = turned[:12]
-    taps = [[taps_ref[3 * a + b : 3 * a + b + 1, :].astype(f32) for b in range(3)] for a in range(3)]
-
-    def window(row_tap, odd_col):
-        source = even_ref if row_tap == 1 else odd_ref
-        first = 16 * (row_tap // 2) if row_tap != 1 else 0
-        return source[odd_col, first : first + 192, :].astype(f32).reshape(12, 16, 256)
-
-    for a in range(3):
-        odd = window(a, 1)
-        even = window(a, 0)
-        for b, product in ((0, odd * back), (1, even * here), (2, odd * here)):
-            total = jnp.sum(jnp.sum(product, axis=0), axis=0, keepdims=True)
-            depth_ref[3 * a + b : 3 * a + b + 1, :] = total
     row_terms = {0: ((1, 0),), 1: ((2, 0), (0, 1))}
-    col_terms = {0: ((1, rows),), 1: ((2, rows), (0, after))}
-    part_expand = 0.0
-    for row in range(2):
-        for col in range(2):
-            d_cells = sum(
-                source[i : i + 12] * taps[a][b]
-                for a, i in row_terms[row]
-                for b, source in col_terms[col]
-            )
-            d_cells = jnp.where(slot < 12, d_cells, 0.0).reshape(192, 256)
-            plane = row * 2 + col
-            d_pre = (d_cells * slopes_ref[plane].astype(f32)).astype(bf16)
-            part_expand = part_expand + dot_tt(cells_ref[plane], d_pre)
-            back_image = dot_kt(d_pre, w_expand_ref[...])
-
-            @pl.when(step == 0)
-            def _():
-                total_ref[plane] = back_image + d_pooled_ref[...]
-
-            @pl.when(step > 0)
-            def _():
-                total_ref[plane] += back_image
-
-    expand_ref[0] = jnp.concatenate(
-        [part_expand[:, :128].reshape(32, 8, 128), part_expand[:, 128:].reshape(32, 8, 128)],
-        axis=1,
-    ).astype(bf16)
-
-    @pl.when(step == pl.num_programs(0) - 1)
-    def _():
-        image_ref[...] = total_ref[...].astype(bf16)
+    for step in range(4):
+        lanes = slice(step * 256, step * 256 + 256)
+        here = d_conv_ref[:, lanes].astype(f32).reshape(12, 16, 256)
+        rows = jnp.concatenate([here, below_ref[:, :, lanes].astype(f32)], axis=0)
+        turned = pltpu.roll(rows, 15, 1)
+        after = jnp.where(slot == 11, right_ref[:, :, lanes].astype(f32), turned)
+        back = turned[:12]
+        taps = [
+            [taps_ref[3 * a + b : 3 * a + b + 1, lanes].astype(f32) for b in range(3)]
+            for a in range(3)
+        ]
+
+        def window(row_tap, odd_col):
+            source = even_ref if row_tap == 1 else odd_ref
+            first = 16 * (row_tap // 2) if row_tap != 1 else 0
+            return source[odd_col, first : first + 192, lanes].astype(f32).reshape(12, 16, 256)
+
+        for a in range(3):
+            odd = window(a, 1)
+            even = window(a, 0)
+            for b, product in ((0, odd * back), (1, even * here), (2, odd * here)):
+                total = jnp.sum(jnp.sum(product, axis=0), axis=0, keepdims=True)
+                depth_ref[3 * a + b : 3 * a + b + 1, lanes] = total
+        col_terms = {0: ((1, rows),), 1: ((2, rows), (0, after))}
+        part_expand = 0.0
+        for row in range(2):
+            for col in range(2):
+                d_cells = sum(
+                    source[i : i + 12] * taps[a][b]
+                    for a, i in row_terms[row]
+                    for b, source in col_terms[col]
+                )
+                d_cells = jnp.where(slot < 12, d_cells, 0.0).reshape(192, 256)
+                plane = row * 2 + col
+                d_pre = (d_cells * slopes_ref[plane, :, lanes].astype(f32)).astype(bf16)
+                part_expand = part_expand + dot_tt(cells_ref[plane], d_pre)
+                back_image = dot_kt(d_pre, w_expand_ref[:, lanes])
+                so_far = d_pooled_ref[...] if step == 0 else total_ref[plane]
+                if step < 3:
+                    total_ref[plane] = so_far + back_image
+                else:
+                    image_ref[plane] = (so_far + back_image).astype(bf16)
+        expand_ref[step // 2, :, step % 2 * 16 : step % 2 * 16 + 16] = jnp.concatenate(
+            [part_expand[:, :128].reshape(32, 8, 128), part_expand[:, 128:].reshape(32, 8, 128)],
+            axis=1,
+        ).astype(bf16)
 
 
 def pixel_step(*inputs):
-    def chunk(*lead):
-        return pl.BlockSpec(lead + (256,), lambda step: (0,) * len(lead) + (step,))
-
-    def whole(*shape):
-        return pl.BlockSpec(shape, lambda step: (0,) * len(shape))
-
     return call(
         pixel_kernel,
         "pixel",
@@ -569,16 +581,6 @@
         ],
         6_000_000_000,
         scratch=[pltpu.VMEM((4, 192, 256), f32)],
-        grid=(4,),
-        in_specs=[
-            chunk(192), chunk(1, 16), chunk(13, 1), chunk(2, 192), chunk(2, 208), chunk(4, 192),
-            whole(4, 192, 256), chunk(256), chunk(16), whole(192, 256),
-        ],
-        out_specs=[
-            whole(4, 192, 256),
-            pl.BlockSpec((1, 32, 16, 128), lambda step: (step // 2, 0, step % 2, 0)),
-            chunk(16),
-        ],
     )(*inputs)
 
 
@@ -642,9 +644,9 @@
     cotangent = slots16(cotangent[0])
     top, left, ring, other = first_transfers(images, w_proj, w_qkv, w_out)
     slots = slot_order()
-    taps16 = jnp.pad(w_depth.reshape(9, 1024), ((0, 7), (0, 0)))
+    taps = w_depth.reshape(9, 1024)
     even, odd, slopes, activated, conv_slope, cells, pooled = expand_step(
-        images, top, left, w_expand, taps16
+        images, top, left, w_expand, taps
     )
     cotangent = cotangent.reshape(192, 512)
     spot = jnp.stack([lax.axis_index("core"), lax.axis_index("ylo")]).astype(jnp.int32)
@@ -665,7 +667,7 @@
     )
     early = pair_sum(early)
     image, expand, depth = pixel_step(
-        d_conv, slots16(below), right, even, odd, slopes, cells, w_expand, taps16,
+        d_conv, slots16(below), right, even, odd, slopes, cells, w_expand, taps,
         d_pooled,
     )
     image = image.reshape(2, 2, 12, 16, 256)[:, :, :, :12]

time: 228 us -> 222 us (0.974)
  Pallas kernels: 25.1 us -> 21.7 us
    pallas_call x1, Pallas kernels: 5.36 us -> 1.79 us  [pixel_step(): call(pixel_kernel, 'pixel', [jax.ShapeDtypeStruct((4, 192, 256), bf16), j...]
    ppermute x1, waiting for transfers between devices: 0.01 us -> 2.32 us  [first_transfers(): lax.ppermute(own[128:], RING, around(6))]
  transfers between devices with their start and end apart: 16 -> 16, of which waited for: 5 -> 5; matrix products, arithmetic and copies ran while one was open for 4% -> 3% of each run, Pallas kernels for 6% -> 4%
where the time goes in v5:
time: 222 us; the launch traced here: 221 us
  starting transfers between devices  77.3 us (35%)
  blocking collectives  59.9 us (27%)
  waiting for transfers between devices  47.8 us (22%)
  Pallas kernels  21.7 us (10%)
  local copies, waits for them, and re-layouts  10.5 us (5%)
  other arithmetic  2.25 us (1%)
    all_to_all x3, blocking collectives, exchange(): return lax.all_to_all(block, axes, 0, 0, tiled=True)  59.9 us
    all_to_all x3, waiting for transfers between devices, exchange(): return lax.all_to_all(block, axes, 0, 0, tiled=True)  44 us
    all_to_all x3, starting transfers between devices, exchange(): return lax.all_to_all(block, axes, 0, 0, tiled=True)  31.2 us
    ppermute x4, starting transfers between devices, swap_cores(): return lax.ppermute(block, 'core', [(0, 1), (1, 0)])  19.7 us
    pallas_call x1, Pallas kernels, attention(): pl.pallas_call(attention_kernel, out_shape=jax.ShapeDtypeStruct((8, 192,...  6.34 us
    ppermute x2, starting transfers between devices, col_rim(): return lax.ppermute(edge, COL, step_route(PARTS, distance))  5.42 us
    ppermute x2, starting transfers between devices, row_rim(): return lax.ppermute(edge, ROW, step_route(PARTS, distance))  5.23 us
    ppermute x1, starting transfers between devices, first_transfers(): above = lax.ppermute(own, RING, around(7))  5.1 us
  transfers between devices with their start and end apart: 16, of which 5 were waited for; matrix products, arithmetic and copies ran while one was open for 3% of the time, Pallas kernels for 4%

profile of v5, /device:TPU:1, one launch (start us, length us, event | category | flops | bytes accessed | tf_op | source)
XLA Modules:
  0.0 221.0 jit_solution(16093997937805130235)
XLA Ops:
  1.3 3.9 %collective-permute-start = (bf16[1,24,256]{2,1,0:T(8,128)(2,1)S(1)}, bf16[1,24,256]{2,1,0:T(8,128)(2,1)S(1)}, u32[]{:S(2)}, u32[]{:S(2)}) collective-permute-start(bf16[1,24,256]{2,1,0:T(8,128)(2,1)S(1)} %slice_bitcast_fusion.4), channel_id=1, source_target_pairs={{0,8},{8,16},{16,24},{24,32},{32,40},{40,48},{48,56},{1,9},{9,17},... | collective-permute-start | bytes 36872 | tf_op jit(solution)/shard_map/ppermute | solution.py:69
  5.3 1.0 shard.1
  6.3 5.1 %collective-permute-start.1 = (bf16[256,512]{1,0:T(8,128)(2,1)S(1)}, bf16[256,512]{1,0:T(8,128)(2,1)S(1)}, u32[]{:S(2)}, u32[]{:S(2)}) collective-permute-start(bf16[256,512]{1,0:T(8,128)(2,1)S(1)} %shard.1), channel_id=1, source_target_pairs={{0,416},{128,0},{256,128},{384,256},{32,384},{160,32},{288,160},{4... | collective-permute-start | bytes 786440 | tf_op jit(solution)/shard_map/ppermute | solution.py:148
  11.4 1.9 collective-permute-start.4
  13.4 2.6 %collective-permute-start.2 = (bf16[128,512]{1,0:T(8,128)(2,1)S(1)}, bf16[128,512]{1,0:T(8,128)(2,1)S(1)}, u32[]{:S(2)}, u32[]{:S(2)}) collective-permute-start(bf16[128,512]{1,0:T(8,128)(2,1)S(1)} %get-tuple-element.59), channel_id=1, source_target_pairs={{0,256},{128,384},{256,32},{384,160},{32,288},{160,416},{288,0},{4... | collective-permute-start | bytes 393224 | tf_op jit(solution)/shard_map/ppermute | solution.py:152
  16.0 4.9 %collective-permute-start.3 = (bf16[128,512]{1,0:T(8,128)(2,1)S(1)}, bf16[128,512]{1,0:T(8,128)(2,1)S(1)}, u32[]{:S(2)}, u32[]{:S(2)}) collective-permute-start(bf16[128,512]{1,0:T(8,128)(2,1)S(1)} %get-tuple-element.60), channel_id=1, source_target_pairs={{0,288},{128,416},{256,0},{384,128},{32,256},{160,384},{288,32},{4... | collective-permute-start | bytes 393224 | tf_op jit(solution)/shard_map/ppermute | solution.py:152
  21.9 4.1 %collective-permute-start.5 = (bf16[25,1,256]{2,1,0:T(2,128)(2,1)S(1)}, bf16[25,1,256]{2,1,0:T(2,128)(2,1)S(1)}, u32[]{:S(2)}, u32[]{:S(2)}) collective-permute-start(bf16[25,1,256]{2,1,0:T(2,128)(2,1)S(1)} %pad_maximum_fusion.5), channel_id=1, source_target_pairs={{0,1},{1,2},{2,3},{3,4},{4,5},{5,6},{6,7},{8,9},{9,10},{10,11},{11... | collective-permute-start | bytes 38408 | tf_op jit(solution)/shard_map/ppermute | solution.py:73
  26.0 2.3 %collective-permute-done.3 = bf16[128,512]{1,0:T(8,128)(2,1)S(1)} collective-permute-done((bf16[128,512]{1,0:T(8,128)(2,1)S(1)}, bf16[128,512]{1,0:T(8,128)(2,1)S(1)}, u32[]{:S(2)}, u32[]{:S(2)}) %collective-permute-start.3) | collective-permute-done | bytes 131104 | tf_op jit(solution)/shard_map/ppermute | solution.py:152
  28.6 3.4 %collective-permute-start.6 = (bf16[4,256,512]{2,1,0:T(8,128)(2,1)S(1)}, bf16[4,256,512]{2,1,0:T(8,128)(2,1)S(1)}, u32[]{:S(2)}, u32[]{:S(2)}) collective-permute-start(bf16[4,256,512]{2,1,0:T(8,128)(2,1)S(1)} %pad_maximum_fusion.1.ring_ref), channel_id=1, source_target_pairs={{0,64},{64,0},{1,65},{65,1},{2,66},{66,2},{3,67},{67,3},{4,68},{68... | collective-permute-start | bytes 3145736 | tf_op jit(solution)/shard_map/ppermute | solution.py:92
  32.9 4.6 %expand.1 = (bf16[2,192,1024]{2,1,0:T(8,128)(2,1)}, bf16[2,208,1024]{2,1,0:T(8,128)(2,1)}, bf16[4,192,1024]{2,1,0:T(8,128)(2,1)}, bf16[192,1024]{1,0:T(8,128)(2,...) custom-call(bf16[24,24,256]{2,1,0:T(8,128)(2,1)S(1)} %bitcast.96, ...), custom_call_target="tpu_custom_call" | custom-call | flops 6000000000 | bytes 8000000 | tf_op jit(solution)/shard_map/expand/pallas_call | solution.py:314
  37.5 3.8 %section.1 = (bf16[8,192,128]{2,1,0:T(8,128)(2,1)}, bf16[192,512]{1,0:T(8,128)(2,1)}, bf16[192,512]{1,0:T(8,128)(2,1)}, bf16[1024,512]{1,0:T(8,128)(2,1)}, bf16[...) custom-call(s32[2]{0:T(128)S(1)} %pad_add_fusion.spot_ref, bf16[4,256,512]{2,1,0:T(8,128)(2,1)S(1)} %pad_maximum_fusion.1.ring_ref, ...), custom_call_target="tpu_custom_call" | custom-call | flops 4000000000 | bytes 8000000 | tf_op jit(solution)/shard_map/section/pallas_call | solution.py:389
  41.3 17.7 %all-to-all-start = ((bf16[64,24,128]{2,1,0:T(8,128)(2,1)}), bf16[64,24,128]{2,1,0:T(8,128)(2,1)S(1)}, u32[]{:S(2)}, u32[]{:S(2)}) async-start(bf16[64,24,128]{2,1,0:T(8,128)(2,1)} %bitcast.106), calls=%async_computation | async-start | bytes 786432 | tf_op jit(solution)/shard_map/all_to_all | solution.py:96
  59.6 15.3 %all-to-all-done = bf16[64,24,128]{2,1,0:T(8,128)(2,1)S(1)} async-done(((bf16[64,24,128]{2,1,0:T(8,128)(2,1)}), bf16[64,24,128]{2,1,0:T(8,128)(2,1)S(1)}, u32[]{:S(2)}, u32[]{:S(2)}) %all-to-all-start) | async-done | bytes 393248 | tf_op jit(solution)/shard_map/all_to_all | solution.py:96
  75.6 6.3 %attention.1 = bf16[8,192,128]{2,1,0:T(8,128)(2,1)} custom-call(bf16[8,192,128]{2,1,0:T(8,128)(2,1)} %bitcast.107, bf16[192,192]{1,0:T(8,128)(2,1)} %constant.92.clone.order_ref, f32[1,192]{1,0:T(1,128)} %or_convert_fusion.valid_ref), custom_call_target="tpu_custom_call" | custom-call | flops 7000000000 | bytes 1000000 | tf_op jit(solution)/shard_map/attention/pallas_call | solution.py:212
  82.0 8.9 %all-to-all-start.1 = ((bf16[64,24,128]{2,1,0:T(8,128)(2,1)}), bf16[64,24,128]{2,1,0:T(8,128)(2,1)S(1)}, u32[]{:S(2)}, u32[]{:S(2)}) async-start(bf16[64,24,128]{2,1,0:T(8,128)(2,1)} %bitcast.105), calls=%async_computation.1 | async-start | bytes 786432 | tf_op jit(solution)/shard_map/all_to_all | solution.py:96
  90.9 15.2 %all-to-all-done.1 = bf16[64,24,128]{2,1,0:T(8,128)(2,1)S(1)} async-done(((bf16[64,24,128]{2,1,0:T(8,128)(2,1)}), bf16[64,24,128]{2,1,0:T(8,128)(2,1)S(1)}, u32[]{:S(2)}, u32[]{:S(2)}) %all-to-all-start.1) | async-done | bytes 393248 | tf_op jit(solution)/shard_map/all_to_all | solution.py:96
  106.1 2.3 %back.1 = (bf16[192,1024]{1,0:T(8,128)(2,1)S(1)}, bf16[192,512]{1,0:T(8,128)(2,1)S(1)}, bf16[192,1024]{1,0:T(8,128)(2,1)S(1)}) custom-call(bf16[8,192,128]{2,1,0:T(8,128)(2,1)S(1)} %bitcast.89, bf16[192,192]{1,0:T(8,128)(2,1)S(1)} %dynamic-slice_bitcast_fusion.3.slots_ref, bf16[192,512]{1,0:T(8,128)(2,1)S(1)} %copy-done.5, bf16[192,512]{1,0:T(8,128)(2,1)S(1)} %bitcast.92, ...), custom_call_target="tpu_custom_call" | custom-call | flops 1500000000 | bytes 8000000 | tf_op jit(solution)/shard_map/back/pallas_call | solution.py:443
  108.5 1.3 collective-permute-start.8
  109.8 1.3 collective-permute-start.9
  111.1 1.3 collective-permute-start.7
  112.4 2.0 parts.1
  114.5 4.6 %collective-permute-start.10 = (bf16[32,144,128]{2,1,0:T(8,128)(2,1)S(1)}, bf16[32,144,128]{2,1,0:T(8,128)(2,1)S(1)}, u32[]{:S(2)}, u32[]{:S(2)}) collective-permute-start(bf16[32,144,128]{2,1,0:T(8,128)(2,1)S(1)} %dynamic-slice_bitcast_fusion), channel_id=1, source_target_pairs={{0,64},{64,0},{1,65},{65,1},{2,66},{66,2},{3,67},{67,3},{4,68},{68... | collective-permute-start | bytes 3538952 | tf_op jit(solution)/shard_map/ppermute | solution.py:92
  119.3 1.8 pixel.1
  121.3 2.1 collective-permute-start.11
  123.3 1.4 collective-permute-done.11
  125.3 27.9 %all_to_all.30 = bf16[32,184,128]{2,1,0:T(8,128)(2,1)S(1)} all-to-all(bf16[32,184,128]{2,1,0:T(8,128)(2,1)S(1)} %pad_maximum_fusion), channel_id=1, replica_groups=mesh['ylo'=4,'core'=2,'yhi'=2,'x'=4,'z'=8] {'x'}, dimensions={0} | all-to-all | bytes 3014656 | tf_op jit(solution)/shard_map/all_to_all | solution.py:96
  153.5 19.0 %all_to_all.31 = bf16[8,184,128]{2,1,0:T(8,128)(2,1)S(1)} all-to-all(bf16[8,184,128]{2,1,0:T(8,128)(2,1)S(1)} %reduce_sum.33), channel_id=1, replica_groups=mesh['ylo'=4,'core'=2,'yhi'=2,'x'=4,'z'=8] {'z'}, dimensions={0} | all-to-all | bytes 753664 | tf_op jit(solution)/shard_map/all_to_all | solution.py:96
  172.7 13.1 %all_to_all.32 = bf16[8,88,128]{2,1,0:T(8,128)(2,1)S(1)} all-to-all(bf16[8,88,128]{2,1,0:T(8,128)(2,1)S(1)} %bitcast.101), channel_id=1, replica_groups=mesh['ylo'=4,'core'=2,'yhi'=2,'x'=4,'z'=8] {'ylo','yhi'}, dimensions={0} | all-to-all | bytes 360448 | tf_op jit(solution)/shard_map/all_to_all | solution.py:96
  186.7 4.5 %all-to-all-start.5 = ((bf16[32,88,128]{2,1,0:T(8,128)(2,1)}), bf16[32,88,128]{2,1,0:T(8,128)(2,1)S(1)}, u32[]{:S(2)}, u32[]{:S(2)}) async-start(bf16[32,88,128]{2,1,0:T(8,128)(2,1)} %broadcast_in_dim.26), calls=%async_computation.5 | async-start | bytes 1441792 | tf_op jit(solution)/shard_map/all_to_all | solution.py:96
  192.4 13.6 %all-to-all-done.5 = bf16[32,88,128]{2,1,0:T(8,128)(2,1)S(1)} async-done(((bf16[32,88,128]{2,1,0:T(8,128)(2,1)}), bf16[32,88,128]{2,1,0:T(8,128)(2,1)S(1)}, u32[]{:S(2)}, u32[]{:S(2)}) %all-to-all-start.5) | async-done | bytes 720928 | tf_op jit(solution)/shard_map/all_to_all | solution.py:96
  206.1 9.6 %collective-permute-start.12 = (bf16[32,56,128]{2,1,0:T(8,128)(2,1)S(1)}, bf16[32,56,128]{2,1,0:T(8,128)(2,1)S(1)}, u32[]{:S(2)}, u32[]{:S(2)}) collective-permute-start(bf16[32,56,128]{2,1,0:T(8,128)(2,1)S(1)} %get-tuple-element.56), channel_id=1, source_target_pairs={{0,64},{64,0},{1,65},{65,1},{2,66},{66,2},{3,67},{67,3},{4,68},{68... | collective-permute-start | bytes 1376264 | tf_op jit(solution)/shard_map/ppermute | solution.py:92
  218.4 1.1 copy.31
  (98 shorter events, 11.8 us)
Async XLA Ops:
  1.3 11.9 %collective-permute-start = (bf16[1,24,256]{2,1,0:T(8,128)(2,1)S(1)}, bf16[1,24,256]{2,1,0:T(8,128)(2,1)S(1)}, u32[]{:S(2)}, u32[]{:S(2)}) collective-permute-start(bf16[1,24,256]{2,1,0:T(8,128)(2,1)S(1)} %slice_bitcast_fusion.4), channel_id=1, source_target_pairs={{0,8},{8,16},{16,24},{24,32},{32,40},{40,48},{48,56},{1,9},{9,17},... | collective-permute-start | bytes 36872 | tf_op jit(solution)/shard_map/ppermute | solution.py:69
  6.3 22.2 %collective-permute-start.1 = (bf16[256,512]{1,0:T(8,128)(2,1)S(1)}, bf16[256,512]{1,0:T(8,128)(2,1)S(1)}, u32[]{:S(2)}, u32[]{:S(2)}) collective-permute-start(bf16[256,512]{1,0:T(8,128)(2,1)S(1)} %shard.1), channel_id=1, source_target_pairs={{0,416},{128,0},{256,128},{384,256},{32,384},{160,32},{288,160},{4... | collective-permute-start | bytes 786440 | tf_op jit(solution)/shard_map/ppermute | solution.py:148
  11.4 17.1 %collective-permute-start.4 = (bf16[256,512]{1,0:T(8,128)(2,1)S(1)}, bf16[256,512]{1,0:T(8,128)(2,1)S(1)}, u32[]{:S(2)}, u32[]{:S(2)}) collective-permute-start(bf16[256,512]{1,0:T(8,128)(2,1)S(1)} %shard.1), channel_id=1, source_target_pairs={{0,128},{128,256},{256,384},{384,32},{32,160},{160,288},{288,416},... | collective-permute-start | bytes 786440 | tf_op jit(solution)/shard_map/ppermute | solution.py:147
  13.3 18.7 %copy-start.13 = (bf16[3,3,1024]{2,1,0:T(4,128)(2,1)S(1)}, bf16[3,3,1024]{2,1,0:T(4,128)(2,1)}, u32[]{:S(2)}) copy-start(bf16[3,3,1024]{2,1,0:T(4,128)(2,1)} %param.12) | copy-start | bytes 55300
  13.3 18.7 %copy-start.11 = (bf16[1,12,12,512]{3,2,1,0:T(8,128)(2,1)S(1)}, bf16[1,12,12,512]{3,2,1,0:T(8,128)(2,1)}, u32[]{:S(2)}) copy-start(bf16[1,12,12,512]{3,2,1,0:T(8,128)(2,1)} %param.17) | copy-start | bytes 442372
  13.4 12.7 %collective-permute-start.2 = (bf16[128,512]{1,0:T(8,128)(2,1)S(1)}, bf16[128,512]{1,0:T(8,128)(2,1)S(1)}, u32[]{:S(2)}, u32[]{:S(2)}) collective-permute-start(bf16[128,512]{1,0:T(8,128)(2,1)S(1)} %get-tuple-element.59), channel_id=1, source_target_pairs={{0,256},{128,384},{256,32},{384,160},{32,288},{160,416},{288,0},{4... | collective-permute-start | bytes 393224 | tf_op jit(solution)/shard_map/ppermute | solution.py:152
  16.0 12.4 %collective-permute-start.3 = (bf16[128,512]{1,0:T(8,128)(2,1)S(1)}, bf16[128,512]{1,0:T(8,128)(2,1)S(1)}, u32[]{:S(2)}, u32[]{:S(2)}) collective-permute-start(bf16[128,512]{1,0:T(8,128)(2,1)S(1)} %get-tuple-element.60), channel_id=1, source_target_pairs={{0,288},{128,416},{256,0},{384,128},{32,256},{160,384},{288,32},{4... | collective-permute-start | bytes 393224 | tf_op jit(solution)/shard_map/ppermute | solution.py:152
  21.9 10.9 %copy-start.12 = (bf16[2,192,192]{2,1,0:T(8,128)(2,1)S(1)}, bf16[2,192,192]{2,1,0:T(8,128)(2,1)}, u32[]{:S(2)}) copy-start(bf16[2,192,192]{2,1,0:T(8,128)(2,1)} %constant.91.clone) | copy-start | bytes 442372
  21.9 6.7 %collective-permute-start.5 = (bf16[25,1,256]{2,1,0:T(2,128)(2,1)S(1)}, bf16[25,1,256]{2,1,0:T(2,128)(2,1)S(1)}, u32[]{:S(2)}, u32[]{:S(2)}) collective-permute-start(bf16[25,1,256]{2,1,0:T(2,128)(2,1)S(1)} %pad_maximum_fusion.5), channel_id=1, source_target_pairs={{0,1},{1,2},{2,3},{3,4},{4,5},{5,6},{6,7},{8,9},{9,10},{10,11},{11... | collective-permute-start | bytes 38408 | tf_op jit(solution)/shard_map/ppermute | solution.py:73
  28.4 4.5 %copy-start.1 = (bf16[1,24,24,256]{3,2,1,0:T(8,128)(2,1)S(1)}, bf16[1,24,24,256]{3,2,1,0:T(8,128)(2,1)}, u32[]{:S(2)}) copy-start(bf16[1,24,24,256]{3,2,1,0:T(8,128)(2,1)} %param.10) | copy-start | bytes 884740
  28.4 4.5 %copy-start.2 = (bf16[256,1024]{1,0:T(8,128)(2,1)S(1)}, bf16[256,1024]{1,0:T(8,128)(2,1)}, u32[]{:S(2)}) copy-start(bf16[256,1024]{1,0:T(8,128)(2,1)} %w_expand_ref.3) | copy-start | bytes 1572868
  28.6 8.9 %collective-permute-start.6 = (bf16[4,256,512]{2,1,0:T(8,128)(2,1)S(1)}, bf16[4,256,512]{2,1,0:T(8,128)(2,1)S(1)}, u32[]{:S(2)}, u32[]{:S(2)}) collective-permute-start(bf16[4,256,512]{2,1,0:T(8,128)(2,1)S(1)} %pad_maximum_fusion.1.ring_ref), channel_id=1, source_target_pairs={{0,64},{64,0},{1,65},{65,1},{2,66},{66,2},{3,67},{67,3},{4,68},{68... | collective-permute-start | bytes 3145736 | tf_op jit(solution)/shard_map/ppermute | solution.py:92
  32.9 4.7 %copy-start.3 = (bf16[256,512]{1,0:T(8,128)(2,1)S(1)}, bf16[256,512]{1,0:T(8,128)(2,1)}, u32[]{:S(2)}) copy-start(bf16[256,512]{1,0:T(8,128)(2,1)} %short_ref.3) | copy-start | bytes 786436
  41.3 33.6 %all-to-all-start = ((bf16[64,24,128]{2,1,0:T(8,128)(2,1)}), bf16[64,24,128]{2,1,0:T(8,128)(2,1)S(1)}, u32[]{:S(2)}, u32[]{:S(2)}) async-start(bf16[64,24,128]{2,1,0:T(8,128)(2,1)} %bitcast.106), calls=%async_computation | async-start | bytes 786432 | tf_op jit(solution)/shard_map/all_to_all | solution.py:96
  74.9 0.8 copy-start.10
  75.6 30.5 %copy-start = (bf16[12,16,512]{2,1,0:T(8,128)(2,1)S(1)}, bf16[12,16,512]{2,1,0:T(8,128)(2,1)}, u32[]{:S(2)}) copy-start(bf16[12,16,512]{2,1,0:T(8,128)(2,1)} %pad.12) | copy-start | bytes 589828
  75.6 30.5 %copy-start.5 = (bf16[192,512]{1,0:T(8,128)(2,1)S(1)}, bf16[192,512]{1,0:T(8,128)(2,1)}, u32[]{:S(2)}) copy-start(bf16[192,512]{1,0:T(8,128)(2,1)} %get-tuple-element.38.section_ref) | copy-start | bytes 589828
  82.0 24.2 %all-to-all-start.1 = ((bf16[64,24,128]{2,1,0:T(8,128)(2,1)}), bf16[64,24,128]{2,1,0:T(8,128)(2,1)S(1)}, u32[]{:S(2)}, u32[]{:S(2)}) async-start(bf16[64,24,128]{2,1,0:T(8,128)(2,1)} %bitcast.105), calls=%async_computation.1 | async-start | bytes 786432 | tf_op jit(solution)/shard_map/all_to_all | solution.py:96
  106.1 6.2 %copy-start.4 = (bf16[192,512]{1,0:T(8,128)(2,1)S(1)}, bf16[192,512]{1,0:T(8,128)(2,1)}, u32[]{:S(2)}) copy-start(bf16[192,512]{1,0:T(8,128)(2,1)} %get-tuple-element.49.normed_ref) | copy-start | bytes 589828
  108.5 10.7 %collective-permute-start.8 = (bf16[12,1,1024]{2,1,0:T(2,128)(2,1)S(1)}, bf16[12,1,1024]{2,1,0:T(2,128)(2,1)S(1)}, u32[]{:S(2)}, u32[]{:S(2)}) collective-permute-start(bf16[12,1,1024]{2,1,0:T(2,128)(2,1)S(1)} %slice.90), channel_id=1, source_target_pairs={{1,0},{2,1},{3,2},{4,3},{5,4},{6,5},{7,6},{9,8},{10,9},{11,10},{12... | collective-permute-start | bytes 73736 | tf_op jit(solution)/shard_map/ppermute | solution.py:73
  109.8 9.4 %collective-permute-start.9 = (bf16[1,1,1024]{2,1,0:T(2,128)(2,1)S(1)}, bf16[1,1,1024]{2,1,0:T(2,128)(2,1)S(1)}, u32[]{:S(2)}, u32[]{:S(2)}) collective-permute-start(bf16[1,1,1024]{2,1,0:T(2,128)(2,1)S(1)} %slice.91), channel_id=1, source_target_pairs={{9,0},{10,1},{11,2},{12,3},{13,4},{14,5},{15,6},{17,8},{18,9},{19,... | collective-permute-start | bytes 6152 | tf_op jit(solution)/shard_map/ppermute | solution.py:83
  111.1 8.1 %collective-permute-start.7 = (bf16[1,12,1024]{2,1,0:T(8,128)(2,1)S(1)}, bf16[1,12,1024]{2,1,0:T(8,128)(2,1)S(1)}, u32[]{:S(2)}, u32[]{:S(2)}) collective-permute-start(bf16[1,12,1024]{2,1,0:T(8,128)(2,1)S(1)} %slice_bitcast_fusion.3), channel_id=1, source_target_pairs={{8,0},{16,8},{24,16},{32,24},{40,32},{48,40},{56,48},{9,1},{17,9},... | collective-permute-start | bytes 73736 | tf_op jit(solution)/shard_map/ppermute | solution.py:69
  112.4 6.9 %copy-start.8 = (bf16[2,192,1024]{2,1,0:T(8,128)(2,1)S(1)}, bf16[2,192,1024]{2,1,0:T(8,128)(2,1)}, u32[]{:S(2)}) copy-start(bf16[2,192,1024]{2,1,0:T(8,128)(2,1)} %get-tuple-element.43.even_ref) | copy-start | bytes 2359300
  112.4 6.9 %copy-start.9 = (bf16[4,192,256]{2,1,0:T(8,128)(2,1)S(1)}, bf16[4,192,256]{2,1,0:T(8,128)(2,1)}, u32[]{:S(2)}) copy-start(bf16[4,192,256]{2,1,0:T(8,128)(2,1)} %get-tuple-element.46.cells_ref) | copy-start | bytes 1179652
  114.4 4.9 %copy-start.6 = (bf16[4,192,1024]{2,1,0:T(8,128)(2,1)S(1)}, bf16[4,192,1024]{2,1,0:T(8,128)(2,1)}, u32[]{:S(2)}) copy-start(bf16[4,192,1024]{2,1,0:T(8,128)(2,1)} %get-tuple-element.45.slopes_ref) | copy-start | bytes 4718596
  114.4 4.9 %copy-start.7 = (bf16[2,208,1024]{2,1,0:T(8,128)(2,1)S(1)}, bf16[2,208,1024]{2,1,0:T(8,128)(2,1)}, u32[]{:S(2)}) copy-start(bf16[2,208,1024]{2,1,0:T(8,128)(2,1)} %get-tuple-element.44.odd_ref) | copy-start | bytes 2555908
  114.5 10.4 %collective-permute-start.10 = (bf16[32,144,128]{2,1,0:T(8,128)(2,1)S(1)}, bf16[32,144,128]{2,1,0:T(8,128)(2,1)S(1)}, u32[]{:S(2)}, u32[]{:S(2)}) collective-permute-start(bf16[32,144,128]{2,1,0:T(8,128)(2,1)S(1)} %dynamic-slice_bitcast_fusion), channel_id=1, source_target_pairs={{0,64},{64,0},{1,65},{65,1},{2,66},{66,2},{3,67},{67,3},{4,68},{68... | collective-permute-start | bytes 3538952 | tf_op jit(solution)/shard_map/ppermute | solution.py:92
  121.3 3.5 %collective-permute-start.11 = (bf16[32,40,128]{2,1,0:T(8,128)(2,1)S(1)}, bf16[32,40,128]{2,1,0:T(8,128)(2,1)S(1)}, u32[]{:S(2)}, u32[]{:S(2)}) collective-permute-start(bf16[32,40,128]{2,1,0:T(8,128)(2,1)S(1)} %pad_maximum_fusion.2), channel_id=1, source_target_pairs={{0,64},{64,0},{1,65},{65,1},{2,66},{66,2},{3,67},{67,3},{4,68},{68... | collective-permute-start | bytes 983048 | tf_op jit(solution)/shard_map/ppermute | solution.py:92
  186.7 19.3 %all-to-all-start.5 = ((bf16[32,88,128]{2,1,0:T(8,128)(2,1)}), bf16[32,88,128]{2,1,0:T(8,128)(2,1)S(1)}, u32[]{:S(2)}, u32[]{:S(2)}) async-start(bf16[32,88,128]{2,1,0:T(8,128)(2,1)} %broadcast_in_dim.26), calls=%async_computation.5 | async-start | bytes 1441792 | tf_op jit(solution)/shard_map/all_to_all | solution.py:96
  206.1 12.0 %collective-permute-start.12 = (bf16[32,56,128]{2,1,0:T(8,128)(2,1)S(1)}, bf16[32,56,128]{2,1,0:T(8,128)(2,1)S(1)}, u32[]{:S(2)}, u32[]{:S(2)}) collective-permute-start(bf16[32,56,128]{2,1,0:T(8,128)(2,1)S(1)} %get-tuple-element.56), channel_id=1, source_target_pairs={{0,64},{64,0},{1,65},{65,1},{2,66},{66,2},{3,67},{67,3},{4,68},{68... | collective-permute-start | bytes 1376264 | tf_op jit(solution)/shard_map/ppermute | solution.py:92

commit v6 on v5

--- a/solution.py
+++ b/solution.py
@@ -157,37 +157,43 @@
 
 
 def slot_order():
-    target = np.arange(192)
-    both = []
-    for odd in range(2):
-        group = (target // 24 + odd * 4) % 8
-        wanted = target // 2 % 12 * 16 + target % 2 * 8 + group
-        both.append(target[None, :] == wanted[:, None])
-    both = jnp.asarray(np.stack(both), bf16)
-    return lax.dynamic_index_in_dim(both, lax.axis_index("z") % 2, 0, keepdims=False)
-
-
-def row_order():
-    target = np.arange(192)
-    wanted = target // 2 % 8 * 24 + target // 16 * 2 + target % 2
-    return jnp.asarray(target[None, :] == wanted[:, None], bf16)
+    order = np.zeros((144, 192), np.float32)
+    for row in range(12):
+        for col in range(12):
+            piece = row % 4 * 2 + col % 4 // 2
+            place = row // 4 * 6 + col // 4 * 2 + col % 2
+            order[piece * 18 + place, row * 16 + col] = 1.0
+    return jnp.asarray(order, bf16)
+
+
+def unit_order():
+    order = np.zeros((576, 576), np.float32)
+    filled = [0] * 8
+    for source in range(576):
+        part_row, part_col, place = source // 144, source % 144 // 18, source % 18
+        high_row = (part_row + place // 6) % 2
+        high_col = (part_col + place % 6 // 2) % 2
+        unit = high_row * 4 + high_col * 2 + place % 2
+        order[unit * 72 + filled[unit], source] = 1.0
+        filled[unit] += 1
+    return jnp.asarray(order, bf16)
 
 
 def dot_kt(left, right):
     return lax.dot_general(left, right, (((1,), (1,)), ((), ())), preferred_element_type=f32)
 
 
-def attention_kernel(slots_ref, order_ref, valid_ref, out_ref, sorted_ref, result_ref):
+def attention_kernel(tokens_ref, order_ref, out_ref, sorted_ref, result_ref):
     scale = 1.0 / math.sqrt(32)
     order = order_ref[...]
-    valid = valid_ref[...] > 0.0
-    for part in range(8):
-        sorted_ref[part * 192 : part * 192 + 192] = dot(order, slots_ref[part]).astype(bf16)
-    for group in range(8):
-        blocks = [row * 16 for row in range(96) if row % 8 == group]
-        unit = jnp.concatenate([sorted_ref[at : at + 16] for at in blocks], axis=0)
-        query, key, value, d_mix = (unit[:, 32 * i : 32 * i + 32] for i in range(4))
-        raised = jnp.where(valid, jnp.exp(dot_kt(query, key) * scale), 0.0)
+    for half in range(2):
+        tokens = tokens_ref[4 * half : 4 * half + 4].reshape(576, 128)
+        sorted_ref[half] = dot(order, tokens)
+    for unit in range(8):
+        at = slice(unit * 72, unit * 72 + 72)
+        tokens = jnp.concatenate([sorted_ref[0, at], sorted_ref[1, at]], axis=0).astype(bf16)
+        query, key, value, d_mix = (tokens[:, 32 * i : 32 * i + 32] for i in range(4))
+        raised = jnp.exp(dot_kt(query, key) * scale)
         weights32 = raised * (1.0 / jnp.sum(raised, axis=-1, keepdims=True))
         weights = weights32.astype(bf16)
         mixture = dot(weights, value)
@@ -198,26 +204,24 @@
         ).astype(bf16)
         d_query = dot(d_scores, key) * scale
         d_key = dot_tt(d_scores, query) * scale
-        result = jnp.concatenate([d_query, d_key, d_value, mixture], axis=-1).astype(bf16)
-        for index, at in enumerate(blocks):
-            result_ref[at : at + 16] = result[index * 16 : index * 16 + 16]
-    for part in range(8):
-        out_ref[part] = dot_tt(order, result_ref[part * 192 : part * 192 + 192]).astype(bf16)
-
-
-def attention(slots):
-    slot = lax.broadcasted_iota(jnp.int32, (1, 192), 1)
-    high = (lax.axis_index("z") >= 4).astype(jnp.int32)
-    valid = ((slot % 2 == 0) | (slot // 2 % 2 == high)).astype(f32)
+        result = jnp.concatenate([d_query, d_key, d_value, mixture], axis=-1)
+        result_ref[0, at] = result[:72]
+        result_ref[1, at] = result[72:]
+    for half in range(2):
+        back = dot_tt(order, result_ref[half].astype(bf16)).astype(bf16)
+        out_ref[4 * half : 4 * half + 4] = back.reshape(4, 144, 128)
+
+
+def attention(tokens):
     return pl.pallas_call(
         attention_kernel,
-        out_shape=jax.ShapeDtypeStruct((8, 192, 128), bf16),
-        scratch_shapes=[pltpu.VMEM((1536, 128), bf16), pltpu.VMEM((1536, 128), bf16)],
+        out_shape=jax.ShapeDtypeStruct((8, 144, 128), bf16),
+        scratch_shapes=[pltpu.VMEM((2, 576, 128), f32), pltpu.VMEM((2, 576, 128), f32)],
         cost_estimate=pl.CostEstimate(
-            flops=7_000_000_000, bytes_accessed=1_000_000, transcendentals=300_000
+            flops=6_000_000_000, bytes_accessed=1_000_000, transcendentals=300_000
         ),
         name="attention",
-    )(slots, row_order(), valid)
+    )(tokens, unit_order())
 
 
 def token_mask():
@@ -385,7 +389,7 @@
 
 def section_step(spot, ring, other, activated, pooled, w_short, cotangent, slots):
     inputs = (spot, ring, other, in_place(activated), in_place(pooled), w_short, in_place(cotangent), slots)
-    shapes = [(8, 192, 128), (192, 512), (192, 512), (1024, 512), (512, 768), (256, 512)]
+    shapes = [(8, 144, 128), (192, 512), (192, 512), (1024, 512), (512, 768), (256, 512)]
     return call(
         section_kernel,
         "section",
@@ -653,9 +657,9 @@
     pieces, section_out, normed, proj, qkv = section_step(
         spot, ring, other, activated, pooled, w_short, cotangent, slots
     )
-    got = exchange(pieces.reshape(64, 24, 128), GRID_AXES)
-    mixed = attention(got.reshape(8, 192, 128))
-    got = exchange(mixed.reshape(64, 24, 128), GRID_AXES).reshape(HEADS, 192, 128)
+    got = exchange(pieces.reshape(64, 9, 2, 128), GRID_AXES)
+    mixed = attention(got.reshape(8, 144, 128))
+    got = exchange(mixed.reshape(64, 9, 2, 128), GRID_AXES).reshape(HEADS, 144, 128)
     results, d_section, d_conv = back_step(
         got, slots, section_out, cotangent, proj, qkv, conv_slope
     )

time: 222 us -> 217 us (0.977)
  blocking collectives: 59.9 us -> 91.4 us
  starting transfers between devices: 77.3 us -> 58 us
  waiting for transfers between devices: 47.8 us -> 31.8 us
    all_to_all x3 -> x4, blocking collectives: 59.9 us -> 91.4 us  [exchange(): return lax.all_to_all(block, axes, 0, 0, tiled=True)]
    all_to_all x3 -> x2, starting transfers between devices: 31.2 us -> 12.3 us  [exchange(): return lax.all_to_all(block, axes, 0, 0, tiled=True)]
    all_to_all x3 -> x2, waiting for transfers between devices: 44 us -> 28.1 us  [exchange(): return lax.all_to_all(block, axes, 0, 0, tiled=True)]
  transfers between devices with their start and end apart: 16 -> 15, of which waited for: 5 -> 4; matrix products, arithmetic and copies ran while one was open for 3% -> 3% of each run, Pallas kernels for 4% -> 4%
where the time goes in v6:
time: 217 us; the launch traced here: 216 us
  blocking collectives  91.4 us (42%)
  starting transfers between devices  58 us (27%)
  waiting for transfers between devices  31.8 us (15%)
  Pallas kernels  22.3 us (10%)
  local copies, waits for them, and re-layouts  9.77 us (5%)
    all_to_all x4, blocking collectives, exchange(): return lax.all_to_all(block, axes, 0, 0, tiled=True)  91.4 us
    all_to_all x2, waiting for transfers between devices, exchange(): return lax.all_to_all(block, axes, 0, 0, tiled=True)  28.1 us
    ppermute x4, starting transfers between devices, swap_cores(): return lax.ppermute(block, 'core', [(0, 1), (1, 0)])  19.2 us
    all_to_all x2, starting transfers between devices, exchange(): return lax.all_to_all(block, axes, 0, 0, tiled=True)  12.3 us
    pallas_call x1, Pallas kernels, attention(): pl.pallas_call(attention_kernel, out_shape=jax.ShapeDtypeStruct((8, 144,...  6.82 us
    ppermute x2, starting transfers between devices, col_rim(): return lax.ppermute(edge, COL, step_route(PARTS, distance))  5.42 us
    ppermute x2, starting transfers between devices, row_rim(): return lax.ppermute(edge, ROW, step_route(PARTS, distance))  5.23 us
    ppermute x1, starting transfers between devices, first_transfers(): above = lax.ppermute(own, RING, around(7))  5.1 us
  transfers between devices with their start and end apart: 15, of which 4 were waited for; matrix products, arithmetic and copies ran while one was open for 3% of the time, Pallas kernels for 4%

profile of v6, /device:TPU:1, one launch (start us, length us, event | category | flops | bytes accessed | tf_op | source)
XLA Modules:
  0.0 216.3 jit_solution(274058181466033181)
XLA Ops:
  1.3 3.9 %collective-permute-start = (bf16[1,24,256]{2,1,0:T(8,128)(2,1)S(1)}, bf16[1,24,256]{2,1,0:T(8,128)(2,1)S(1)}, u32[]{:S(2)}, u32[]{:S(2)}) collective-permute-start(bf16[1,24,256]{2,1,0:T(8,128)(2,1)S(1)} %slice_bitcast_fusion.4), channel_id=1, source_target_pairs={{0,8},{8,16},{16,24},{24,32},{32,40},{40,48},{48,56},{1,9},{9,17},... | collective-permute-start | bytes 36872 | tf_op jit(solution)/shard_map/ppermute | solution.py:69
  5.3 1.0 shard.1
  6.3 5.1 %collective-permute-start.1 = (bf16[256,512]{1,0:T(8,128)(2,1)S(1)}, bf16[256,512]{1,0:T(8,128)(2,1)S(1)}, u32[]{:S(2)}, u32[]{:S(2)}) collective-permute-start(bf16[256,512]{1,0:T(8,128)(2,1)S(1)} %shard.1), channel_id=1, source_target_pairs={{0,416},{128,0},{256,128},{384,256},{32,384},{160,32},{288,160},{4... | collective-permute-start | bytes 786440 | tf_op jit(solution)/shard_map/ppermute | solution.py:148
  11.4 1.9 collective-permute-start.4
  13.4 2.6 %collective-permute-start.2 = (bf16[128,512]{1,0:T(8,128)(2,1)S(1)}, bf16[128,512]{1,0:T(8,128)(2,1)S(1)}, u32[]{:S(2)}, u32[]{:S(2)}) collective-permute-start(bf16[128,512]{1,0:T(8,128)(2,1)S(1)} %get-tuple-element.59), channel_id=1, source_target_pairs={{0,256},{128,384},{256,32},{384,160},{32,288},{160,416},{288,0},{4... | collective-permute-start | bytes 393224 | tf_op jit(solution)/shard_map/ppermute | solution.py:152
  16.0 4.9 %collective-permute-start.3 = (bf16[128,512]{1,0:T(8,128)(2,1)S(1)}, bf16[128,512]{1,0:T(8,128)(2,1)S(1)}, u32[]{:S(2)}, u32[]{:S(2)}) collective-permute-start(bf16[128,512]{1,0:T(8,128)(2,1)S(1)} %get-tuple-element.60), channel_id=1, source_target_pairs={{0,288},{128,416},{256,0},{384,128},{32,256},{160,384},{288,32},{4... | collective-permute-start | bytes 393224 | tf_op jit(solution)/shard_map/ppermute | solution.py:152
  21.9 4.1 %collective-permute-start.5 = (bf16[25,1,256]{2,1,0:T(2,128)(2,1)S(1)}, bf16[25,1,256]{2,1,0:T(2,128)(2,1)S(1)}, u32[]{:S(2)}, u32[]{:S(2)}) collective-permute-start(bf16[25,1,256]{2,1,0:T(2,128)(2,1)S(1)} %pad_maximum_fusion.5), channel_id=1, source_target_pairs={{0,1},{1,2},{2,3},{3,4},{4,5},{5,6},{6,7},{8,9},{9,10},{10,11},{11... | collective-permute-start | bytes 38408 | tf_op jit(solution)/shard_map/ppermute | solution.py:73
  26.0 2.3 %collective-permute-done.3 = bf16[128,512]{1,0:T(8,128)(2,1)S(1)} collective-permute-done((bf16[128,512]{1,0:T(8,128)(2,1)S(1)}, bf16[128,512]{1,0:T(8,128)(2,1)S(1)}, u32[]{:S(2)}, u32[]{:S(2)}) %collective-permute-start.3) | collective-permute-done | bytes 131104 | tf_op jit(solution)/shard_map/ppermute | solution.py:152
  28.5 3.3 %collective-permute-start.6 = (bf16[4,256,512]{2,1,0:T(8,128)(2,1)S(1)}, bf16[4,256,512]{2,1,0:T(8,128)(2,1)S(1)}, u32[]{:S(2)}, u32[]{:S(2)}) collective-permute-start(bf16[4,256,512]{2,1,0:T(8,128)(2,1)S(1)} %pad_maximum_fusion.1.ring_ref), channel_id=1, source_target_pairs={{0,64},{64,0},{1,65},{65,1},{2,66},{66,2},{3,67},{67,3},{4,68},{68... | collective-permute-start | bytes 3145736 | tf_op jit(solution)/shard_map/ppermute | solution.py:92
  32.7 4.7 %expand.1 = (bf16[2,192,1024]{2,1,0:T(8,128)(2,1)}, bf16[2,208,1024]{2,1,0:T(8,128)(2,1)}, bf16[4,192,1024]{2,1,0:T(8,128)(2,1)}, bf16[192,1024]{1,0:T(8,128)(2,...) custom-call(bf16[24,24,256]{2,1,0:T(8,128)(2,1)S(1)} %bitcast.94, ...), custom_call_target="tpu_custom_call" | custom-call | flops 6000000000 | bytes 8000000 | tf_op jit(solution)/shard_map/expand/pallas_call | solution.py:318
  37.3 3.6 %section.1 = (bf16[8,144,128]{2,1,0:T(8,128)(2,1)}, bf16[192,512]{1,0:T(8,128)(2,1)}, bf16[192,512]{1,0:T(8,128)(2,1)}, bf16[1024,512]{1,0:T(8,128)(2,1)}, bf16[...) custom-call(s32[2]{0:T(128)S(1)} %pad_add_fusion.spot_ref, bf16[4,256,512]{2,1,0:T(8,128)(2,1)S(1)} %pad_maximum_fusion.1.ring_ref, ...), custom_call_target="tpu_custom_call" | custom-call | flops 4000000000 | bytes 8000000 | tf_op jit(solution)/shard_map/section/pallas_call | solution.py:393
  41.0 32.9 %all_to_all.30 = bf16[64,9,2,128]{3,2,1,0:T(2,128)(2,1)} all-to-all(bf16[64,9,2,128]{3,2,1,0:T(2,128)(2,1)} %bitcast.105), channel_id=1, replica_groups=mesh['ylo'=4,'core'=2,'yhi'=2,'x'=4,'z'=8] {'yhi','x','z'}, dimensions={0} | all-to-all | bytes 589824 | tf_op jit(solution)/shard_map/all_to_all | solution.py:96
  73.9 6.8 %attention.1 = bf16[8,144,128]{2,1,0:T(8,128)(2,1)} custom-call(bf16[8,144,128]{2,1,0:T(8,128)(2,1)} %bitcast.106, bf16[576,576]{1,0:T(8,128)(2,1)} %constant.45.clone.order_ref), custom_call_target="tpu_custom_call" | custom-call | flops 6000000000 | bytes 1000000 | tf_op jit(solution)/shard_map/attention/pallas_call | solution.py:216
  80.7 7.8 %all-to-all-start.1 = ((bf16[64,9,2,128]{3,2,1,0:T(2,128)(2,1)}), bf16[64,9,2,128]{3,2,1,0:T(2,128)(2,1)S(1)}, u32[]{:S(2)}, u32[]{:S(2)}) async-start(bf16[64,9,2,128]{3,2,1,0:T(2,128)(2,1)} %bitcast.104), calls=%async_computation.1 | async-start | bytes 589824 | tf_op jit(solution)/shard_map/all_to_all | solution.py:96
  88.5 14.5 %all-to-all-done.1 = bf16[64,9,2,128]{3,2,1,0:T(2,128)(2,1)S(1)} async-done(((bf16[64,9,2,128]{3,2,1,0:T(2,128)(2,1)}), bf16[64,9,2,128]{3,2,1,0:T(2,128)(2,1)S(1)}, u32[]{:S(2)}, u32[]{:S(2)}) %all-to-all-start.1) | async-done | bytes 294944 | tf_op jit(solution)/shard_map/all_to_all | solution.py:96
  103.0 2.5 %back.1 = (bf16[192,1024]{1,0:T(8,128)(2,1)S(1)}, bf16[192,512]{1,0:T(8,128)(2,1)S(1)}, bf16[192,1024]{1,0:T(8,128)(2,1)S(1)}) custom-call(bf16[8,144,128]{2,1,0:T(8,128)(2,1)S(1)} %bitcast.87, bf16[144,192]{1,0:T(8,128)(2,1)S(1)} %copy-done.4, bf16[192,512]{1,0:T(8,128)(2,1)S(1)} %copy-done.6, bf16[192,512]{1,0:T(8,128)(2,1)S(1)} %bitcast.90, ...), custom_call_target="tpu_custom_call" | custom-call | flops 1500000000 | bytes 8000000 | tf_op jit(solution)/shard_map/back/pallas_call | solution.py:447
  105.6 1.3 collective-permute-start.8
  106.9 1.3 collective-permute-start.9
  108.2 1.3 collective-permute-start.7
  109.5 2.0 parts.1
  111.6 4.4 %collective-permute-start.10 = (bf16[32,144,128]{2,1,0:T(8,128)(2,1)S(1)}, bf16[32,144,128]{2,1,0:T(8,128)(2,1)S(1)}, u32[]{:S(2)}, u32[]{:S(2)}) collective-permute-start(bf16[32,144,128]{2,1,0:T(8,128)(2,1)S(1)} %dynamic-slice_bitcast_fusion), channel_id=1, source_target_pairs={{0,64},{64,0},{1,65},{65,1},{2,66},{66,2},{3,67},{67,3},{4,68},{68... | collective-permute-start | bytes 3538952 | tf_op jit(solution)/shard_map/ppermute | solution.py:92
  116.1 1.8 pixel.1
  118.1 2.1 collective-permute-start.11
  120.1 1.4 collective-permute-done.11
  122.2 27.8 %all_to_all.31 = bf16[32,184,128]{2,1,0:T(8,128)(2,1)S(1)} all-to-all(bf16[32,184,128]{2,1,0:T(8,128)(2,1)S(1)} %pad_maximum_fusion), channel_id=1, replica_groups=mesh['ylo'=4,'core'=2,'yhi'=2,'x'=4,'z'=8] {'x'}, dimensions={0} | all-to-all | bytes 3014656 | tf_op jit(solution)/shard_map/all_to_all | solution.py:96
  150.2 18.1 %all_to_all.32 = bf16[8,184,128]{2,1,0:T(8,128)(2,1)S(1)} all-to-all(bf16[8,184,128]{2,1,0:T(8,128)(2,1)S(1)} %reduce_sum.33), channel_id=1, replica_groups=mesh['ylo'=4,'core'=2,'yhi'=2,'x'=4,'z'=8] {'z'}, dimensions={0} | all-to-all | bytes 753664 | tf_op jit(solution)/shard_map/all_to_all | solution.py:96
  168.5 12.6 %all_to_all.33 = bf16[8,88,128]{2,1,0:T(8,128)(2,1)S(1)} all-to-all(bf16[8,88,128]{2,1,0:T(8,128)(2,1)S(1)} %bitcast.99), channel_id=1, replica_groups=mesh['ylo'=4,'core'=2,'yhi'=2,'x'=4,'z'=8] {'ylo','yhi'}, dimensions={0} | all-to-all | bytes 360448 | tf_op jit(solution)/shard_map/all_to_all | solution.py:96
  181.1 1.0 broadcast_in_dim.26
  182.1 4.5 %all-to-all-start.5 = ((bf16[32,88,128]{2,1,0:T(8,128)(2,1)}), bf16[32,88,128]{2,1,0:T(8,128)(2,1)S(1)}, u32[]{:S(2)}, u32[]{:S(2)}) async-start(bf16[32,88,128]{2,1,0:T(8,128)(2,1)} %broadcast_in_dim.26), calls=%async_computation.5 | async-start | bytes 1441792 | tf_op jit(solution)/shard_map/all_to_all | solution.py:96
  187.8 13.6 %all-to-all-done.5 = bf16[32,88,128]{2,1,0:T(8,128)(2,1)S(1)} async-done(((bf16[32,88,128]{2,1,0:T(8,128)(2,1)}), bf16[32,88,128]{2,1,0:T(8,128)(2,1)S(1)}, u32[]{:S(2)}, u32[]{:S(2)}) %all-to-all-start.5) | async-done | bytes 720928 | tf_op jit(solution)/shard_map/all_to_all | solution.py:96
  201.5 9.6 %collective-permute-start.12 = (bf16[32,56,128]{2,1,0:T(8,128)(2,1)S(1)}, bf16[32,56,128]{2,1,0:T(8,128)(2,1)S(1)}, u32[]{:S(2)}, u32[]{:S(2)}) collective-permute-start(bf16[32,56,128]{2,1,0:T(8,128)(2,1)S(1)} %get-tuple-element.56), channel_id=1, source_target_pairs={{0,64},{64,0},{1,65},{65,1},{2,66},{66,2},{3,67},{67,3},{4,68},{68... | collective-permute-start | bytes 1376264 | tf_op jit(solution)/shard_map/ppermute | solution.py:92
  213.8 1.1 copy.31
  (93 shorter events, 9.5 us)
Async XLA Ops:
  1.3 12.0 %collective-permute-start = (bf16[1,24,256]{2,1,0:T(8,128)(2,1)S(1)}, bf16[1,24,256]{2,1,0:T(8,128)(2,1)S(1)}, u32[]{:S(2)}, u32[]{:S(2)}) collective-permute-start(bf16[1,24,256]{2,1,0:T(8,128)(2,1)S(1)} %slice_bitcast_fusion.4), channel_id=1, source_target_pairs={{0,8},{8,16},{16,24},{24,32},{32,40},{40,48},{48,56},{1,9},{9,17},... | collective-permute-start | bytes 36872 | tf_op jit(solution)/shard_map/ppermute | solution.py:69
  6.3 25.6 %copy-start.12 = (bf16[3,3,1024]{2,1,0:T(4,128)(2,1)S(1)}, bf16[3,3,1024]{2,1,0:T(4,128)(2,1)}, u32[]{:S(2)}) copy-start(bf16[3,3,1024]{2,1,0:T(4,128)(2,1)} %param.12) | copy-start | bytes 55300
  6.3 22.1 %collective-permute-start.1 = (bf16[256,512]{1,0:T(8,128)(2,1)S(1)}, bf16[256,512]{1,0:T(8,128)(2,1)S(1)}, u32[]{:S(2)}, u32[]{:S(2)}) collective-permute-start(bf16[256,512]{1,0:T(8,128)(2,1)S(1)} %shard.1), channel_id=1, source_target_pairs={{0,416},{128,0},{256,128},{384,256},{32,384},{160,32},{288,160},{4... | collective-permute-start | bytes 786440 | tf_op jit(solution)/shard_map/ppermute | solution.py:148
  11.4 17.0 %collective-permute-start.4 = (bf16[256,512]{1,0:T(8,128)(2,1)S(1)}, bf16[256,512]{1,0:T(8,128)(2,1)S(1)}, u32[]{:S(2)}, u32[]{:S(2)}) collective-permute-start(bf16[256,512]{1,0:T(8,128)(2,1)S(1)} %shard.1), channel_id=1, source_target_pairs={{0,128},{128,256},{256,384},{384,32},{32,160},{160,288},{288,416},... | collective-permute-start | bytes 786440 | tf_op jit(solution)/shard_map/ppermute | solution.py:147
  13.3 18.5 %copy-start.11 = (bf16[1,12,12,512]{3,2,1,0:T(8,128)(2,1)S(1)}, bf16[1,12,12,512]{3,2,1,0:T(8,128)(2,1)}, u32[]{:S(2)}) copy-start(bf16[1,12,12,512]{3,2,1,0:T(8,128)(2,1)} %param.17) | copy-start | bytes 442372
  13.4 12.7 %collective-permute-start.2 = (bf16[128,512]{1,0:T(8,128)(2,1)S(1)}, bf16[128,512]{1,0:T(8,128)(2,1)S(1)}, u32[]{:S(2)}, u32[]{:S(2)}) collective-permute-start(bf16[128,512]{1,0:T(8,128)(2,1)S(1)} %get-tuple-element.59), channel_id=1, source_target_pairs={{0,256},{128,384},{256,32},{384,160},{32,288},{160,416},{288,0},{4... | collective-permute-start | bytes 393224 | tf_op jit(solution)/shard_map/ppermute | solution.py:152
  16.0 12.4 %collective-permute-start.3 = (bf16[128,512]{1,0:T(8,128)(2,1)S(1)}, bf16[128,512]{1,0:T(8,128)(2,1)S(1)}, u32[]{:S(2)}, u32[]{:S(2)}) collective-permute-start(bf16[128,512]{1,0:T(8,128)(2,1)S(1)} %get-tuple-element.60), channel_id=1, source_target_pairs={{0,288},{128,416},{256,0},{384,128},{32,256},{160,384},{288,32},{4... | collective-permute-start | bytes 393224 | tf_op jit(solution)/shard_map/ppermute | solution.py:152
  21.9 10.8 %copy-start.1 = (bf16[1,24,24,256]{3,2,1,0:T(8,128)(2,1)S(1)}, bf16[1,24,24,256]{3,2,1,0:T(8,128)(2,1)}, u32[]{:S(2)}) copy-start(bf16[1,24,24,256]{3,2,1,0:T(8,128)(2,1)} %param.10) | copy-start | bytes 884740
  21.9 10.8 %copy-start.2 = (bf16[256,1024]{1,0:T(8,128)(2,1)S(1)}, bf16[256,1024]{1,0:T(8,128)(2,1)}, u32[]{:S(2)}) copy-start(bf16[256,1024]{1,0:T(8,128)(2,1)} %w_expand_ref.3) | copy-start | bytes 1572868
  21.9 6.6 %collective-permute-start.5 = (bf16[25,1,256]{2,1,0:T(2,128)(2,1)S(1)}, bf16[25,1,256]{2,1,0:T(2,128)(2,1)S(1)}, u32[]{:S(2)}, u32[]{:S(2)}) collective-permute-start(bf16[25,1,256]{2,1,0:T(2,128)(2,1)S(1)} %pad_maximum_fusion.5), channel_id=1, source_target_pairs={{0,1},{1,2},{2,3},{3,4},{4,5},{5,6},{6,7},{8,9},{9,10},{10,11},{11... | collective-permute-start | bytes 38408 | tf_op jit(solution)/shard_map/ppermute | solution.py:73
  28.5 8.8 %collective-permute-start.6 = (bf16[4,256,512]{2,1,0:T(8,128)(2,1)S(1)}, bf16[4,256,512]{2,1,0:T(8,128)(2,1)S(1)}, u32[]{:S(2)}, u32[]{:S(2)}) collective-permute-start(bf16[4,256,512]{2,1,0:T(8,128)(2,1)S(1)} %pad_maximum_fusion.1.ring_ref), channel_id=1, source_target_pairs={{0,64},{64,0},{1,65},{65,1},{2,66},{66,2},{3,67},{67,3},{4,68},{68... | collective-permute-start | bytes 3145736 | tf_op jit(solution)/shard_map/ppermute | solution.py:92
  32.6 4.7 %copy-start.3 = (bf16[256,512]{1,0:T(8,128)(2,1)S(1)}, bf16[256,512]{1,0:T(8,128)(2,1)}, u32[]{:S(2)}) copy-start(bf16[256,512]{1,0:T(8,128)(2,1)} %short_ref.3) | copy-start | bytes 786436
  32.6 4.7 %copy-start.4 = (bf16[144,192]{1,0:T(8,128)(2,1)S(1)}, bf16[144,192]{1,0:T(8,128)(2,1)}, u32[]{:S(2)}) copy-start(bf16[144,192]{1,0:T(8,128)(2,1)} %constant.44.clone.slots_ref) | copy-start | bytes 165892
  73.9 29.1 %copy-start = (bf16[12,16,512]{2,1,0:T(8,128)(2,1)S(1)}, bf16[12,16,512]{2,1,0:T(8,128)(2,1)}, u32[]{:S(2)}) copy-start(bf16[12,16,512]{2,1,0:T(8,128)(2,1)} %pad.12) | copy-start | bytes 589828
  73.9 29.1 %copy-start.6 = (bf16[192,512]{1,0:T(8,128)(2,1)S(1)}, bf16[192,512]{1,0:T(8,128)(2,1)}, u32[]{:S(2)}) copy-start(bf16[192,512]{1,0:T(8,128)(2,1)} %get-tuple-element.38.section_ref) | copy-start | bytes 589828
  80.7 22.3 %all-to-all-start.1 = ((bf16[64,9,2,128]{3,2,1,0:T(2,128)(2,1)}), bf16[64,9,2,128]{3,2,1,0:T(2,128)(2,1)S(1)}, u32[]{:S(2)}, u32[]{:S(2)}) async-start(bf16[64,9,2,128]{3,2,1,0:T(2,128)(2,1)} %bitcast.104), calls=%async_computation.1 | async-start | bytes 589824 | tf_op jit(solution)/shard_map/all_to_all | solution.py:96
  103.0 6.5 %copy-start.5 = (bf16[192,512]{1,0:T(8,128)(2,1)S(1)}, bf16[192,512]{1,0:T(8,128)(2,1)}, u32[]{:S(2)}) copy-start(bf16[192,512]{1,0:T(8,128)(2,1)} %get-tuple-element.49.normed_ref) | copy-start | bytes 589828
  105.6 10.4 %collective-permute-start.8 = (bf16[12,1,1024]{2,1,0:T(2,128)(2,1)S(1)}, bf16[12,1,1024]{2,1,0:T(2,128)(2,1)S(1)}, u32[]{:S(2)}, u32[]{:S(2)}) collective-permute-start(bf16[12,1,1024]{2,1,0:T(2,128)(2,1)S(1)} %slice.90), channel_id=1, source_target_pairs={{1,0},{2,1},{3,2},{4,3},{5,4},{6,5},{7,6},{9,8},{10,9},{11,10},{12... | collective-permute-start | bytes 73736 | tf_op jit(solution)/shard_map/ppermute | solution.py:73
  106.9 9.1 %collective-permute-start.9 = (bf16[1,1,1024]{2,1,0:T(2,128)(2,1)S(1)}, bf16[1,1,1024]{2,1,0:T(2,128)(2,1)S(1)}, u32[]{:S(2)}, u32[]{:S(2)}) collective-permute-start(bf16[1,1,1024]{2,1,0:T(2,128)(2,1)S(1)} %slice.91), channel_id=1, source_target_pairs={{9,0},{10,1},{11,2},{12,3},{13,4},{14,5},{15,6},{17,8},{18,9},{19,... | collective-permute-start | bytes 6152 | tf_op jit(solution)/shard_map/ppermute | solution.py:83
  108.2 7.8 %collective-permute-start.7 = (bf16[1,12,1024]{2,1,0:T(8,128)(2,1)S(1)}, bf16[1,12,1024]{2,1,0:T(8,128)(2,1)S(1)}, u32[]{:S(2)}, u32[]{:S(2)}) collective-permute-start(bf16[1,12,1024]{2,1,0:T(8,128)(2,1)S(1)} %slice_bitcast_fusion.3), channel_id=1, source_target_pairs={{8,0},{16,8},{24,16},{32,24},{40,32},{48,40},{56,48},{9,1},{17,9},... | collective-permute-start | bytes 73736 | tf_op jit(solution)/shard_map/ppermute | solution.py:69
  109.5 6.6 %copy-start.9 = (bf16[2,192,1024]{2,1,0:T(8,128)(2,1)S(1)}, bf16[2,192,1024]{2,1,0:T(8,128)(2,1)}, u32[]{:S(2)}) copy-start(bf16[2,192,1024]{2,1,0:T(8,128)(2,1)} %get-tuple-element.43.even_ref) | copy-start | bytes 2359300
  109.5 6.6 %copy-start.10 = (bf16[4,192,256]{2,1,0:T(8,128)(2,1)S(1)}, bf16[4,192,256]{2,1,0:T(8,128)(2,1)}, u32[]{:S(2)}) copy-start(bf16[4,192,256]{2,1,0:T(8,128)(2,1)} %get-tuple-element.46.cells_ref) | copy-start | bytes 1179652
  111.5 4.6 %copy-start.7 = (bf16[4,192,1024]{2,1,0:T(8,128)(2,1)S(1)}, bf16[4,192,1024]{2,1,0:T(8,128)(2,1)}, u32[]{:S(2)}) copy-start(bf16[4,192,1024]{2,1,0:T(8,128)(2,1)} %get-tuple-element.45.slopes_ref) | copy-start | bytes 4718596
  111.5 4.6 %copy-start.8 = (bf16[2,208,1024]{2,1,0:T(8,128)(2,1)S(1)}, bf16[2,208,1024]{2,1,0:T(8,128)(2,1)}, u32[]{:S(2)}) copy-start(bf16[2,208,1024]{2,1,0:T(8,128)(2,1)} %get-tuple-element.44.odd_ref) | copy-start | bytes 2555908
  111.6 10.1 %collective-permute-start.10 = (bf16[32,144,128]{2,1,0:T(8,128)(2,1)S(1)}, bf16[32,144,128]{2,1,0:T(8,128)(2,1)S(1)}, u32[]{:S(2)}, u32[]{:S(2)}) collective-permute-start(bf16[32,144,128]{2,1,0:T(8,128)(2,1)S(1)} %dynamic-slice_bitcast_fusion), channel_id=1, source_target_pairs={{0,64},{64,0},{1,65},{65,1},{2,66},{66,2},{3,67},{67,3},{4,68},{68... | collective-permute-start | bytes 3538952 | tf_op jit(solution)/shard_map/ppermute | solution.py:92
  118.1 3.5 %collective-permute-start.11 = (bf16[32,40,128]{2,1,0:T(8,128)(2,1)S(1)}, bf16[32,40,128]{2,1,0:T(8,128)(2,1)S(1)}, u32[]{:S(2)}, u32[]{:S(2)}) collective-permute-start(bf16[32,40,128]{2,1,0:T(8,128)(2,1)S(1)} %pad_maximum_fusion.2), channel_id=1, source_target_pairs={{0,64},{64,0},{1,65},{65,1},{2,66},{66,2},{3,67},{67,3},{4,68},{68... | collective-permute-start | bytes 983048 | tf_op jit(solution)/shard_map/ppermute | solution.py:92
  182.1 19.3 %all-to-all-start.5 = ((bf16[32,88,128]{2,1,0:T(8,128)(2,1)}), bf16[32,88,128]{2,1,0:T(8,128)(2,1)S(1)}, u32[]{:S(2)}, u32[]{:S(2)}) async-start(bf16[32,88,128]{2,1,0:T(8,128)(2,1)} %broadcast_in_dim.26), calls=%async_computation.5 | async-start | bytes 1441792 | tf_op jit(solution)/shard_map/all_to_all | solution.py:96
  201.5 12.0 %collective-permute-start.12 = (bf16[32,56,128]{2,1,0:T(8,128)(2,1)S(1)}, bf16[32,56,128]{2,1,0:T(8,128)(2,1)S(1)}, u32[]{:S(2)}, u32[]{:S(2)}) collective-permute-start(bf16[32,56,128]{2,1,0:T(8,128)(2,1)S(1)} %get-tuple-element.56), channel_id=1, source_target_pairs={{0,64},{64,0},{1,65},{65,1},{2,66},{66,2},{3,67},{67,3},{4,68},{68... | collective-permute-start | bytes 1376264 | tf_op jit(solution)/shard_map/ppermute | solution.py:92

commit v7 on v6

--- a/solution.py
+++ b/solution.py
@@ -134,7 +134,7 @@
         copy.wait()
 
 
-def first_transfers(images, w_proj, w_qkv, w_out):
+def first_transfers(images, w_proj, w_qkv, w_out, cotangent):
     own = call(
         shard_kernel,
         "shard",
@@ -152,8 +152,8 @@
         [lax.ppermute(own[:128], RING, around(2)), lax.ppermute(own[128:], RING, around(6))]
     )
     ring = jnp.stack([own, above, far, below])
-    ring, left = lax.optimization_barrier((ring, left))
-    return top, left, ring, swap_cores(ring)
+    ring, left, cotangent = lax.optimization_barrier((ring, left, cotangent))
+    return top, left, ring, swap_cores(ring), cotangent
 
 
 def slot_order():
@@ -176,14 +176,14 @@
         unit = high_row * 4 + high_col * 2 + place % 2
         order[unit * 72 + filled[unit], source] = 1.0
         filled[unit] += 1
-    return jnp.asarray(order, bf16)
+    return jnp.asarray(order, bf16), jnp.asarray(order.T, bf16)
 
 
 def dot_kt(left, right):
     return lax.dot_general(left, right, (((1,), (1,)), ((), ())), preferred_element_type=f32)
 
 
-def attention_kernel(tokens_ref, order_ref, out_ref, sorted_ref, result_ref):
+def attention_kernel(tokens_ref, order_ref, home_ref, out_ref, sorted_ref, result_ref):
     scale = 1.0 / math.sqrt(32)
     order = order_ref[...]
     for half in range(2):
@@ -208,7 +208,7 @@
         result_ref[0, at] = result[:72]
         result_ref[1, at] = result[72:]
     for half in range(2):
-        back = dot_tt(order, result_ref[half].astype(bf16)).astype(bf16)
+        back = dot(home_ref[...], result_ref[half].astype(bf16)).astype(bf16)
         out_ref[4 * half : 4 * half + 4] = back.reshape(4, 144, 128)
 
 
@@ -221,7 +221,7 @@
             flops=6_000_000_000, bytes_accessed=1_000_000, transcendentals=300_000
         ),
         name="attention",
-    )(tokens, unit_order())
+    )(tokens, *unit_order())
 
 
 def token_mask():
@@ -646,7 +646,7 @@
 def on_device(images, w_expand, w_depth, w_short, w_proj, w_qkv, w_out, cotangent):
     images = images[0]
     cotangent = slots16(cotangent[0])
-    top, left, ring, other = first_transfers(images, w_proj, w_qkv, w_out)
+    top, left, ring, other, cotangent = first_transfers(images, w_proj, w_qkv, w_out, cotangent)
     slots = slot_order()
     taps = w_depth.reshape(9, 1024)
     even, odd, slopes, activated, conv_slope, cells, pooled = expand_step(

time: 217 us -> 217 us (level)
  no operation moved by 1% of the time
where the time goes in v7:
time: 217 us; the launch traced here: 216 us
  blocking collectives  91.1 us (42%)
  starting transfers between devices  58.7 us (27%)
  waiting for transfers between devices  30.5 us (14%)
  Pallas kernels  22.2 us (10%)
  local copies, waits for them, and re-layouts  10.8 us (5%)
    all_to_all x4, blocking collectives, exchange(): return lax.all_to_all(block, axes, 0, 0, tiled=True)  91.1 us
    all_to_all x2, waiting for transfers between devices, exchange(): return lax.all_to_all(block, axes, 0, 0, tiled=True)  28.2 us
    ppermute x4, starting transfers between devices, swap_cores(): return lax.ppermute(block, 'core', [(0, 1), (1, 0)])  20.4 us
    all_to_all x2, starting transfers between devices, exchange(): return lax.all_to_all(block, axes, 0, 0, tiled=True)  12.1 us
    pallas_call x1, Pallas kernels, attention(): pl.pallas_call(attention_kernel, out_shape=jax.ShapeDtypeStruct((8, 144,...  6.69 us
    ppermute x2, starting transfers between devices, col_rim(): return lax.ppermute(edge, COL, step_route(PARTS, distance))  5.29 us
    ppermute x2, starting transfers between devices, row_rim(): return lax.ppermute(edge, ROW, step_route(PARTS, distance))  5.23 us
    ppermute x1, starting transfers between devices, first_transfers(): above = lax.ppermute(own, RING, around(7))  5.1 us
  transfers between devices with their start and end apart: 15, of which 4 were waited for; matrix products, arithmetic and copies ran while one was open for 3% of the time, Pallas kernels for 4%

profile of v7, /device:TPU:1, one launch (start us, length us, event | category | flops | bytes accessed | tf_op | source)
XLA Modules:
  0.0 216.2 jit_solution(12722760591805989647)
XLA Ops:
  1.3 3.9 %collective-permute-start = (bf16[1,24,256]{2,1,0:T(8,128)(2,1)S(1)}, bf16[1,24,256]{2,1,0:T(8,128)(2,1)S(1)}, u32[]{:S(2)}, u32[]{:S(2)}) collective-permute-start(bf16[1,24,256]{2,1,0:T(8,128)(2,1)S(1)} %slice_bitcast_fusion.4), channel_id=1, source_target_pairs={{0,8},{8,16},{16,24},{24,32},{32,40},{40,48},{48,56},{1,9},{9,17},... | collective-permute-start | bytes 36872 | tf_op jit(solution)/shard_map/ppermute | solution.py:69
  5.3 1.0 shard.1
  6.3 5.1 %collective-permute-start.1 = (bf16[256,512]{1,0:T(8,128)(2,1)S(1)}, bf16[256,512]{1,0:T(8,128)(2,1)S(1)}, u32[]{:S(2)}, u32[]{:S(2)}) collective-permute-start(bf16[256,512]{1,0:T(8,128)(2,1)S(1)} %shard.1), channel_id=1, source_target_pairs={{0,416},{128,0},{256,128},{384,256},{32,384},{160,32},{288,160},{4... | collective-permute-start | bytes 786440 | tf_op jit(solution)/shard_map/ppermute | solution.py:148
  11.4 1.9 collective-permute-start.4
  13.3 2.5 %collective-permute-start.2 = (bf16[128,512]{1,0:T(8,128)(2,1)S(1)}, bf16[128,512]{1,0:T(8,128)(2,1)S(1)}, u32[]{:S(2)}, u32[]{:S(2)}) collective-permute-start(bf16[128,512]{1,0:T(8,128)(2,1)S(1)} %get-tuple-element.61), channel_id=1, source_target_pairs={{0,256},{128,384},{256,32},{384,160},{32,288},{160,416},{288,0},{4... | collective-permute-start | bytes 393224 | tf_op jit(solution)/shard_map/ppermute | solution.py:152
  15.8 4.9 %collective-permute-start.3 = (bf16[128,512]{1,0:T(8,128)(2,1)S(1)}, bf16[128,512]{1,0:T(8,128)(2,1)S(1)}, u32[]{:S(2)}, u32[]{:S(2)}) collective-permute-start(bf16[128,512]{1,0:T(8,128)(2,1)S(1)} %get-tuple-element.62), channel_id=1, source_target_pairs={{0,288},{128,416},{256,0},{384,128},{32,256},{160,384},{288,32},{4... | collective-permute-start | bytes 393224 | tf_op jit(solution)/shard_map/ppermute | solution.py:152
  21.7 1.7 pad.12
  23.5 4.0 %collective-permute-start.5 = (bf16[25,1,256]{2,1,0:T(2,128)(2,1)S(1)}, bf16[25,1,256]{2,1,0:T(2,128)(2,1)S(1)}, u32[]{:S(2)}, u32[]{:S(2)}) collective-permute-start(bf16[25,1,256]{2,1,0:T(2,128)(2,1)S(1)} %pad_maximum_fusion.5), channel_id=1, source_target_pairs={{0,1},{1,2},{2,3},{3,4},{4,5},{5,6},{6,7},{8,9},{9,10},{10,11},{11... | collective-permute-start | bytes 38408 | tf_op jit(solution)/shard_map/ppermute | solution.py:73
  28.4 4.6 %collective-permute-start.6 = (bf16[4,256,512]{2,1,0:T(8,128)(2,1)S(1)}, bf16[4,256,512]{2,1,0:T(8,128)(2,1)S(1)}, u32[]{:S(2)}, u32[]{:S(2)}) collective-permute-start(bf16[4,256,512]{2,1,0:T(8,128)(2,1)S(1)} %pad_maximum_fusion.1.ring_ref), channel_id=1, source_target_pairs={{0,64},{64,0},{1,65},{65,1},{2,66},{66,2},{3,67},{67,3},{4,68},{68... | collective-permute-start | bytes 3145736 | tf_op jit(solution)/shard_map/ppermute | solution.py:92
  33.1 4.7 %expand.1 = (bf16[2,192,1024]{2,1,0:T(8,128)(2,1)}, bf16[2,208,1024]{2,1,0:T(8,128)(2,1)}, bf16[4,192,1024]{2,1,0:T(8,128)(2,1)}, bf16[192,1024]{1,0:T(8,128)(2,...) custom-call(bf16[24,24,256]{2,1,0:T(8,128)(2,1)S(1)} %bitcast.94, ...), custom_call_target="tpu_custom_call" | custom-call | flops 6000000000 | bytes 8000000 | tf_op jit(solution)/shard_map/expand/pallas_call | solution.py:318
  37.8 3.6 %section.1 = (bf16[8,144,128]{2,1,0:T(8,128)(2,1)}, bf16[192,512]{1,0:T(8,128)(2,1)}, bf16[192,512]{1,0:T(8,128)(2,1)}, bf16[1024,512]{1,0:T(8,128)(2,1)}, bf16[...) custom-call(s32[2]{0:T(128)S(1)} %pad_add_fusion.spot_ref, bf16[4,256,512]{2,1,0:T(8,128)(2,1)S(1)} %pad_maximum_fusion.1.ring_ref, ...), custom_call_target="tpu_custom_call" | custom-call | flops 4000000000 | bytes 8000000 | tf_op jit(solution)/shard_map/section/pallas_call | solution.py:393
  41.4 33.2 %all_to_all.30 = bf16[64,9,2,128]{3,2,1,0:T(2,128)(2,1)} all-to-all(bf16[64,9,2,128]{3,2,1,0:T(2,128)(2,1)} %bitcast.105), channel_id=1, replica_groups=mesh['ylo'=4,'core'=2,'yhi'=2,'x'=4,'z'=8] {'yhi','x','z'}, dimensions={0} | all-to-all | bytes 589824 | tf_op jit(solution)/shard_map/all_to_all | solution.py:96
  74.6 6.7 %attention.1 = bf16[8,144,128]{2,1,0:T(8,128)(2,1)} custom-call(bf16[8,144,128]{2,1,0:T(8,128)(2,1)} %bitcast.106, bf16[576,576]{1,0:T(8,128)(2,1)} %constant.47.clone.order_ref, bf16[576,576]{1,0:T(8,128)(2,1)} %constant.48.clone.home_ref), custom_call_target="tpu_custom_call" | custom-call | flops 6000000000 | bytes 1000000 | tf_op jit(solution)/shard_map/attention/pallas_call | solution.py:216
  81.3 7.8 %all-to-all-start.1 = ((bf16[64,9,2,128]{3,2,1,0:T(2,128)(2,1)}), bf16[64,9,2,128]{3,2,1,0:T(2,128)(2,1)S(1)}, u32[]{:S(2)}, u32[]{:S(2)}) async-start(bf16[64,9,2,128]{3,2,1,0:T(2,128)(2,1)} %bitcast.104), calls=%async_computation.1 | async-start | bytes 589824 | tf_op jit(solution)/shard_map/all_to_all | solution.py:96
  89.1 14.4 %all-to-all-done.1 = bf16[64,9,2,128]{3,2,1,0:T(2,128)(2,1)S(1)} async-done(((bf16[64,9,2,128]{3,2,1,0:T(2,128)(2,1)}), bf16[64,9,2,128]{3,2,1,0:T(2,128)(2,1)S(1)}, u32[]{:S(2)}, u32[]{:S(2)}) %all-to-all-start.1) | async-done | bytes 294944 | tf_op jit(solution)/shard_map/all_to_all | solution.py:96
  103.5 2.5 %back.1 = (bf16[192,1024]{1,0:T(8,128)(2,1)S(1)}, bf16[192,512]{1,0:T(8,128)(2,1)S(1)}, bf16[192,1024]{1,0:T(8,128)(2,1)S(1)}) custom-call(bf16[8,144,128]{2,1,0:T(8,128)(2,1)S(1)} %bitcast.87, bf16[144,192]{1,0:T(8,128)(2,1)S(1)} %copy-done.4, bf16[192,512]{1,0:T(8,128)(2,1)S(1)} %copy-done.6, bf16[192,512]{1,0:T(8,128)(2,1)S(1)} %bitcast.90, ...), custom_call_target="tpu_custom_call" | custom-call | flops 1500000000 | bytes 8000000 | tf_op jit(solution)/shard_map/back/pallas_call | solution.py:447
  106.1 1.3 collective-permute-start.8
  107.4 1.3 collective-permute-start.9
  108.7 1.3 collective-permute-start.7
  110.0 2.0 parts.1
  112.1 4.4 %collective-permute-start.10 = (bf16[32,144,128]{2,1,0:T(8,128)(2,1)S(1)}, bf16[32,144,128]{2,1,0:T(8,128)(2,1)S(1)}, u32[]{:S(2)}, u32[]{:S(2)}) collective-permute-start(bf16[32,144,128]{2,1,0:T(8,128)(2,1)S(1)} %dynamic-slice_bitcast_fusion), channel_id=1, source_target_pairs={{0,64},{64,0},{1,65},{65,1},{2,66},{66,2},{3,67},{67,3},{4,68},{68... | collective-permute-start | bytes 3538952 | tf_op jit(solution)/shard_map/ppermute | solution.py:92
  116.7 1.8 pixel.1
  118.6 2.1 collective-permute-start.11
  120.7 1.4 collective-permute-done.11
  122.7 29.1 %all_to_all.31 = bf16[32,184,128]{2,1,0:T(8,128)(2,1)S(1)} all-to-all(bf16[32,184,128]{2,1,0:T(8,128)(2,1)S(1)} %pad_maximum_fusion), channel_id=1, replica_groups=mesh['ylo'=4,'core'=2,'yhi'=2,'x'=4,'z'=8] {'x'}, dimensions={0} | all-to-all | bytes 3014656 | tf_op jit(solution)/shard_map/all_to_all | solution.py:96
  152.1 18.0 %all_to_all.32 = bf16[8,184,128]{2,1,0:T(8,128)(2,1)S(1)} all-to-all(bf16[8,184,128]{2,1,0:T(8,128)(2,1)S(1)} %reduce_sum.33), channel_id=1, replica_groups=mesh['ylo'=4,'core'=2,'yhi'=2,'x'=4,'z'=8] {'z'}, dimensions={0} | all-to-all | bytes 753664 | tf_op jit(solution)/shard_map/all_to_all | solution.py:96
  170.2 10.9 %all_to_all.33 = bf16[8,88,128]{2,1,0:T(8,128)(2,1)S(1)} all-to-all(bf16[8,88,128]{2,1,0:T(8,128)(2,1)S(1)} %bitcast.99), channel_id=1, replica_groups=mesh['ylo'=4,'core'=2,'yhi'=2,'x'=4,'z'=8] {'ylo','yhi'}, dimensions={0} | all-to-all | bytes 360448 | tf_op jit(solution)/shard_map/all_to_all | solution.py:96
  181.2 1.0 broadcast_in_dim.26
  182.1 4.3 %all-to-all-start.5 = ((bf16[32,88,128]{2,1,0:T(8,128)(2,1)}), bf16[32,88,128]{2,1,0:T(8,128)(2,1)S(1)}, u32[]{:S(2)}, u32[]{:S(2)}) async-start(bf16[32,88,128]{2,1,0:T(8,128)(2,1)} %broadcast_in_dim.26), calls=%async_computation.5 | async-start | bytes 1441792 | tf_op jit(solution)/shard_map/all_to_all | solution.py:96
  187.6 13.8 %all-to-all-done.5 = bf16[32,88,128]{2,1,0:T(8,128)(2,1)S(1)} async-done(((bf16[32,88,128]{2,1,0:T(8,128)(2,1)}), bf16[32,88,128]{2,1,0:T(8,128)(2,1)S(1)}, u32[]{:S(2)}, u32[]{:S(2)}) %all-to-all-start.5) | async-done | bytes 720928 | tf_op jit(solution)/shard_map/all_to_all | solution.py:96
  201.5 9.3 %collective-permute-start.12 = (bf16[32,56,128]{2,1,0:T(8,128)(2,1)S(1)}, bf16[32,56,128]{2,1,0:T(8,128)(2,1)S(1)}, u32[]{:S(2)}, u32[]{:S(2)}) collective-permute-start(bf16[32,56,128]{2,1,0:T(8,128)(2,1)S(1)} %get-tuple-element.58), channel_id=1, source_target_pairs={{0,64},{64,0},{1,65},{65,1},{2,66},{66,2},{3,67},{67,3},{4,68},{68... | collective-permute-start | bytes 1376264 | tf_op jit(solution)/shard_map/ppermute | solution.py:92
  213.6 1.1 copy.32
  (91 shorter events, 9.5 us)
Async XLA Ops:
  1.3 11.9 %collective-permute-start = (bf16[1,24,256]{2,1,0:T(8,128)(2,1)S(1)}, bf16[1,24,256]{2,1,0:T(8,128)(2,1)S(1)}, u32[]{:S(2)}, u32[]{:S(2)}) collective-permute-start(bf16[1,24,256]{2,1,0:T(8,128)(2,1)S(1)} %slice_bitcast_fusion.4), channel_id=1, source_target_pairs={{0,8},{8,16},{16,24},{24,32},{32,40},{40,48},{48,56},{1,9},{9,17},... | collective-permute-start | bytes 36872 | tf_op jit(solution)/shard_map/ppermute | solution.py:69
  6.3 22.0 %collective-permute-start.1 = (bf16[256,512]{1,0:T(8,128)(2,1)S(1)}, bf16[256,512]{1,0:T(8,128)(2,1)S(1)}, u32[]{:S(2)}, u32[]{:S(2)}) collective-permute-start(bf16[256,512]{1,0:T(8,128)(2,1)S(1)} %shard.1), channel_id=1, source_target_pairs={{0,416},{128,0},{256,128},{384,256},{32,384},{160,32},{288,160},{4... | collective-permute-start | bytes 786440 | tf_op jit(solution)/shard_map/ppermute | solution.py:148
  11.4 16.9 %collective-permute-start.4 = (bf16[256,512]{1,0:T(8,128)(2,1)S(1)}, bf16[256,512]{1,0:T(8,128)(2,1)S(1)}, u32[]{:S(2)}, u32[]{:S(2)}) collective-permute-start(bf16[256,512]{1,0:T(8,128)(2,1)S(1)} %shard.1), channel_id=1, source_target_pairs={{0,128},{128,256},{256,384},{384,32},{32,160},{160,288},{288,416},... | collective-permute-start | bytes 786440 | tf_op jit(solution)/shard_map/ppermute | solution.py:147
  13.3 14.1 %collective-permute-start.2 = (bf16[128,512]{1,0:T(8,128)(2,1)S(1)}, bf16[128,512]{1,0:T(8,128)(2,1)S(1)}, u32[]{:S(2)}, u32[]{:S(2)}) collective-permute-start(bf16[128,512]{1,0:T(8,128)(2,1)S(1)} %get-tuple-element.61), channel_id=1, source_target_pairs={{0,256},{128,384},{256,32},{384,160},{32,288},{160,416},{288,0},{4... | collective-permute-start | bytes 393224 | tf_op jit(solution)/shard_map/ppermute | solution.py:152
  15.8 12.4 %collective-permute-start.3 = (bf16[128,512]{1,0:T(8,128)(2,1)S(1)}, bf16[128,512]{1,0:T(8,128)(2,1)S(1)}, u32[]{:S(2)}, u32[]{:S(2)}) collective-permute-start(bf16[128,512]{1,0:T(8,128)(2,1)S(1)} %get-tuple-element.62), channel_id=1, source_target_pairs={{0,288},{128,416},{256,0},{384,128},{32,256},{160,384},{288,32},{4... | collective-permute-start | bytes 393224 | tf_op jit(solution)/shard_map/ppermute | solution.py:152
  21.7 11.3 %copy-start.11 = (bf16[3,3,1024]{2,1,0:T(4,128)(2,1)S(1)}, bf16[3,3,1024]{2,1,0:T(4,128)(2,1)}, u32[]{:S(2)}) copy-start(bf16[3,3,1024]{2,1,0:T(4,128)(2,1)} %param.13) | copy-start | bytes 55300
  21.7 11.4 %copy-start.1 = (bf16[1,24,24,256]{3,2,1,0:T(8,128)(2,1)S(1)}, bf16[1,24,24,256]{3,2,1,0:T(8,128)(2,1)}, u32[]{:S(2)}) copy-start(bf16[1,24,24,256]{3,2,1,0:T(8,128)(2,1)} %param.11) | copy-start | bytes 884740
  21.7 11.4 %copy-start.2 = (bf16[256,1024]{1,0:T(8,128)(2,1)S(1)}, bf16[256,1024]{1,0:T(8,128)(2,1)}, u32[]{:S(2)}) copy-start(bf16[256,1024]{1,0:T(8,128)(2,1)} %w_expand_ref.3) | copy-start | bytes 1572868
  23.5 4.9 %collective-permute-start.5 = (bf16[25,1,256]{2,1,0:T(2,128)(2,1)S(1)}, bf16[25,1,256]{2,1,0:T(2,128)(2,1)S(1)}, u32[]{:S(2)}, u32[]{:S(2)}) collective-permute-start(bf16[25,1,256]{2,1,0:T(2,128)(2,1)S(1)} %pad_maximum_fusion.5), channel_id=1, source_target_pairs={{0,1},{1,2},{2,3},{3,4},{4,5},{5,6},{6,7},{8,9},{9,10},{10,11},{11... | collective-permute-start | bytes 38408 | tf_op jit(solution)/shard_map/ppermute | solution.py:73
  28.4 9.4 %collective-permute-start.6 = (bf16[4,256,512]{2,1,0:T(8,128)(2,1)S(1)}, bf16[4,256,512]{2,1,0:T(8,128)(2,1)S(1)}, u32[]{:S(2)}, u32[]{:S(2)}) collective-permute-start(bf16[4,256,512]{2,1,0:T(8,128)(2,1)S(1)} %pad_maximum_fusion.1.ring_ref), channel_id=1, source_target_pairs={{0,64},{64,0},{1,65},{65,1},{2,66},{66,2},{3,67},{67,3},{4,68},{68... | collective-permute-start | bytes 3145736 | tf_op jit(solution)/shard_map/ppermute | solution.py:92
  33.1 4.7 %copy-start.3 = (bf16[256,512]{1,0:T(8,128)(2,1)S(1)}, bf16[256,512]{1,0:T(8,128)(2,1)}, u32[]{:S(2)}) copy-start(bf16[256,512]{1,0:T(8,128)(2,1)} %short_ref.3) | copy-start | bytes 786436
  33.1 4.7 %copy-start.4 = (bf16[144,192]{1,0:T(8,128)(2,1)S(1)}, bf16[144,192]{1,0:T(8,128)(2,1)}, u32[]{:S(2)}) copy-start(bf16[144,192]{1,0:T(8,128)(2,1)} %constant.46.clone.slots_ref) | copy-start | bytes 165892
  74.6 28.9 %copy-start = (bf16[12,16,512]{2,1,0:T(8,128)(2,1)S(1)}, bf16[12,16,512]{2,1,0:T(8,128)(2,1)}, u32[]{:S(2)}) copy-start(bf16[12,16,512]{2,1,0:T(8,128)(2,1)} %pad.12) | copy-start | bytes 589828
  74.6 28.9 %copy-start.6 = (bf16[192,512]{1,0:T(8,128)(2,1)S(1)}, bf16[192,512]{1,0:T(8,128)(2,1)}, u32[]{:S(2)}) copy-start(bf16[192,512]{1,0:T(8,128)(2,1)} %get-tuple-element.40.section_ref) | copy-start | bytes 589828
  81.3 22.2 %all-to-all-start.1 = ((bf16[64,9,2,128]{3,2,1,0:T(2,128)(2,1)}), bf16[64,9,2,128]{3,2,1,0:T(2,128)(2,1)S(1)}, u32[]{:S(2)}, u32[]{:S(2)}) async-start(bf16[64,9,2,128]{3,2,1,0:T(2,128)(2,1)} %bitcast.104), calls=%async_computation.1 | async-start | bytes 589824 | tf_op jit(solution)/shard_map/all_to_all | solution.py:96
  103.5 6.5 %copy-start.5 = (bf16[192,512]{1,0:T(8,128)(2,1)S(1)}, bf16[192,512]{1,0:T(8,128)(2,1)}, u32[]{:S(2)}) copy-start(bf16[192,512]{1,0:T(8,128)(2,1)} %get-tuple-element.51.normed_ref) | copy-start | bytes 589828
  106.1 10.5 %collective-permute-start.8 = (bf16[12,1,1024]{2,1,0:T(2,128)(2,1)S(1)}, bf16[12,1,1024]{2,1,0:T(2,128)(2,1)S(1)}, u32[]{:S(2)}, u32[]{:S(2)}) collective-permute-start(bf16[12,1,1024]{2,1,0:T(2,128)(2,1)S(1)} %slice.90), channel_id=1, source_target_pairs={{1,0},{2,1},{3,2},{4,3},{5,4},{6,5},{7,6},{9,8},{10,9},{11,10},{12... | collective-permute-start | bytes 73736 | tf_op jit(solution)/shard_map/ppermute | solution.py:73
  107.4 9.2 %collective-permute-start.9 = (bf16[1,1,1024]{2,1,0:T(2,128)(2,1)S(1)}, bf16[1,1,1024]{2,1,0:T(2,128)(2,1)S(1)}, u32[]{:S(2)}, u32[]{:S(2)}) collective-permute-start(bf16[1,1,1024]{2,1,0:T(2,128)(2,1)S(1)} %slice.91), channel_id=1, source_target_pairs={{9,0},{10,1},{11,2},{12,3},{13,4},{14,5},{15,6},{17,8},{18,9},{19,... | collective-permute-start | bytes 6152 | tf_op jit(solution)/shard_map/ppermute | solution.py:83
  108.7 7.8 %collective-permute-start.7 = (bf16[1,12,1024]{2,1,0:T(8,128)(2,1)S(1)}, bf16[1,12,1024]{2,1,0:T(8,128)(2,1)S(1)}, u32[]{:S(2)}, u32[]{:S(2)}) collective-permute-start(bf16[1,12,1024]{2,1,0:T(8,128)(2,1)S(1)} %slice_bitcast_fusion.3), channel_id=1, source_target_pairs={{8,0},{16,8},{24,16},{32,24},{40,32},{48,40},{56,48},{9,1},{17,9},... | collective-permute-start | bytes 73736 | tf_op jit(solution)/shard_map/ppermute | solution.py:69
  110.0 6.6 %copy-start.9 = (bf16[2,192,1024]{2,1,0:T(8,128)(2,1)S(1)}, bf16[2,192,1024]{2,1,0:T(8,128)(2,1)}, u32[]{:S(2)}) copy-start(bf16[2,192,1024]{2,1,0:T(8,128)(2,1)} %get-tuple-element.45.even_ref) | copy-start | bytes 2359300
  110.0 6.6 %copy-start.10 = (bf16[4,192,256]{2,1,0:T(8,128)(2,1)S(1)}, bf16[4,192,256]{2,1,0:T(8,128)(2,1)}, u32[]{:S(2)}) copy-start(bf16[4,192,256]{2,1,0:T(8,128)(2,1)} %get-tuple-element.48.cells_ref) | copy-start | bytes 1179652
  112.0 4.7 %copy-start.7 = (bf16[4,192,1024]{2,1,0:T(8,128)(2,1)S(1)}, bf16[4,192,1024]{2,1,0:T(8,128)(2,1)}, u32[]{:S(2)}) copy-start(bf16[4,192,1024]{2,1,0:T(8,128)(2,1)} %get-tuple-element.47.slopes_ref) | copy-start | bytes 4718596
  112.0 4.7 %copy-start.8 = (bf16[2,208,1024]{2,1,0:T(8,128)(2,1)S(1)}, bf16[2,208,1024]{2,1,0:T(8,128)(2,1)}, u32[]{:S(2)}) copy-start(bf16[2,208,1024]{2,1,0:T(8,128)(2,1)} %get-tuple-element.46.odd_ref) | copy-start | bytes 2555908
  112.1 10.2 %collective-permute-start.10 = (bf16[32,144,128]{2,1,0:T(8,128)(2,1)S(1)}, bf16[32,144,128]{2,1,0:T(8,128)(2,1)S(1)}, u32[]{:S(2)}, u32[]{:S(2)}) collective-permute-start(bf16[32,144,128]{2,1,0:T(8,128)(2,1)S(1)} %dynamic-slice_bitcast_fusion), channel_id=1, source_target_pairs={{0,64},{64,0},{1,65},{65,1},{2,66},{66,2},{3,67},{67,3},{4,68},{68... | collective-permute-start | bytes 3538952 | tf_op jit(solution)/shard_map/ppermute | solution.py:92
  118.6 3.5 %collective-permute-start.11 = (bf16[32,40,128]{2,1,0:T(8,128)(2,1)S(1)}, bf16[32,40,128]{2,1,0:T(8,128)(2,1)S(1)}, u32[]{:S(2)}, u32[]{:S(2)}) collective-permute-start(bf16[32,40,128]{2,1,0:T(8,128)(2,1)S(1)} %pad_maximum_fusion.2), channel_id=1, source_target_pairs={{0,64},{64,0},{1,65},{65,1},{2,66},{66,2},{3,67},{67,3},{4,68},{68... | collective-permute-start | bytes 983048 | tf_op jit(solution)/shard_map/ppermute | solution.py:92
  182.1 19.3 %all-to-all-start.5 = ((bf16[32,88,128]{2,1,0:T(8,128)(2,1)}), bf16[32,88,128]{2,1,0:T(8,128)(2,1)S(1)}, u32[]{:S(2)}, u32[]{:S(2)}) async-start(bf16[32,88,128]{2,1,0:T(8,128)(2,1)} %broadcast_in_dim.26), calls=%async_computation.5 | async-start | bytes 1441792 | tf_op jit(solution)/shard_map/all_to_all | solution.py:96
  201.5 11.7 %collective-permute-start.12 = (bf16[32,56,128]{2,1,0:T(8,128)(2,1)S(1)}, bf16[32,56,128]{2,1,0:T(8,128)(2,1)S(1)}, u32[]{:S(2)}, u32[]{:S(2)}) collective-permute-start(bf16[32,56,128]{2,1,0:T(8,128)(2,1)S(1)} %get-tuple-element.58), channel_id=1, source_target_pairs={{0,64},{64,0},{1,65},{65,1},{2,66},{66,2},{3,67},{67,3},{4,68},{68... | collective-permute-start | bytes 1376264 | tf_op jit(solution)/shard_map/ppermute | solution.py:92

commit v8 on v6

--- a/solution.py
+++ b/solution.py
@@ -189,24 +189,37 @@
     for half in range(2):
         tokens = tokens_ref[4 * half : 4 * half + 4].reshape(576, 128)
         sorted_ref[half] = dot(order, tokens)
-    for unit in range(8):
-        at = slice(unit * 72, unit * 72 + 72)
-        tokens = jnp.concatenate([sorted_ref[0, at], sorted_ref[1, at]], axis=0).astype(bf16)
-        query, key, value, d_mix = (tokens[:, 32 * i : 32 * i + 32] for i in range(4))
-        raised = jnp.exp(dot_kt(query, key) * scale)
-        weights32 = raised * (1.0 / jnp.sum(raised, axis=-1, keepdims=True))
-        weights = weights32.astype(bf16)
-        mixture = dot(weights, value)
-        d_weights = dot_kt(d_mix, value)
-        d_value = dot_tt(weights, d_mix)
-        d_scores = (
-            weights32 * (d_weights - jnp.sum(weights32 * d_weights, axis=-1, keepdims=True))
-        ).astype(bf16)
-        d_query = dot(d_scores, key) * scale
-        d_key = dot_tt(d_scores, query) * scale
-        result = jnp.concatenate([d_query, d_key, d_value, mixture], axis=-1)
-        result_ref[0, at] = result[:72]
-        result_ref[1, at] = result[72:]
+    for first in (0, 4):
+        spots = [slice(unit * 72, unit * 72 + 72) for unit in range(first, first + 4)]
+        units = [
+            jnp.concatenate([sorted_ref[0, at], sorted_ref[1, at]], axis=0).astype(bf16)
+            for at in spots
+        ]
+        cut = [[unit[:, 32 * i : 32 * i + 32] for i in range(4)] for unit in units]
+        scores = [dot_kt(query, key) for query, key, _, _ in cut]
+        d_weights = [dot_kt(d_mix, value) for _, _, value, d_mix in cut]
+        raised = [jnp.exp(score * scale) for score in scores]
+        totals = [1.0 / jnp.sum(part, axis=-1, keepdims=True) for part in raised]
+        weights32 = [part * total for part, total in zip(raised, totals)]
+        weights = [part.astype(bf16) for part in weights32]
+        mixture = [dot(part, heads[2]) for part, heads in zip(weights, cut)]
+        d_value = [dot_tt(part, heads[3]) for part, heads in zip(weights, cut)]
+        inner = [
+            jnp.sum(part * back, axis=-1, keepdims=True)
+            for part, back in zip(weights32, d_weights)
+        ]
+        d_scores = [
+            (part * (back - total)).astype(bf16)
+            for part, back, total in zip(weights32, d_weights, inner)
+        ]
+        d_query = [dot(part, heads[1]) * scale for part, heads in zip(d_scores, cut)]
+        d_key = [dot_tt(part, heads[0]) * scale for part, heads in zip(d_scores, cut)]
+        for index, at in enumerate(spots):
+            result = jnp.concatenate(
+                [d_query[index], d_key[index], d_value[index], mixture[index]], axis=-1
+            )
+            result_ref[0, at] = result[:72]
+            result_ref[1, at] = result[72:]
     for half in range(2):
         back = dot_tt(order, result_ref[half].astype(bf16)).astype(bf16)
         out_ref[4 * half : 4 * half + 4] = back.reshape(4, 144, 128)

time: 217 us -> 216 us (level)
  no operation moved by 1% of the time
where the time goes in v8:
time: 216 us; the launch traced here: 215 us
  blocking collectives  91.4 us (42%)
  starting transfers between devices  58 us (27%)
  waiting for transfers between devices  31.8 us (15%)
  Pallas kernels  20.5 us (9%)
  local copies, waits for them, and re-layouts  9.77 us (5%)
    all_to_all x4, blocking collectives, exchange(): return lax.all_to_all(block, axes, 0, 0, tiled=True)  91.4 us
    all_to_all x2, waiting for transfers between devices, exchange(): return lax.all_to_all(block, axes, 0, 0, tiled=True)  28.1 us
    ppermute x4, starting transfers between devices, swap_cores(): return lax.ppermute(block, 'core', [(0, 1), (1, 0)])  19.2 us
    all_to_all x2, starting transfers between devices, exchange(): return lax.all_to_all(block, axes, 0, 0, tiled=True)  12.3 us
    ppermute x2, starting transfers between devices, col_rim(): return lax.ppermute(edge, COL, step_route(PARTS, distance))  5.42 us
    ppermute x2, starting transfers between devices, row_rim(): return lax.ppermute(edge, ROW, step_route(PARTS, distance))  5.23 us
    ppermute x1, starting transfers between devices, first_transfers(): above = lax.ppermute(own, RING, around(7))  5.1 us
    pallas_call x1, Pallas kernels, attention(): pl.pallas_call(attention_kernel, out_shape=jax.ShapeDtypeStruct((8, 144,...  5 us
  transfers between devices with their start and end apart: 15, of which 4 were waited for; matrix products, arithmetic and copies ran while one was open for 3% of the time, Pallas kernels for 4%

profile of v8, /device:TPU:1, one launch (start us, length us, event | category | flops | bytes accessed | tf_op | source)
XLA Modules:
  0.0 214.5 jit_solution(14099336956850147607)
XLA Ops:
  1.3 3.9 %collective-permute-start = (bf16[1,24,256]{2,1,0:T(8,128)(2,1)S(1)}, bf16[1,24,256]{2,1,0:T(8,128)(2,1)S(1)}, u32[]{:S(2)}, u32[]{:S(2)}) collective-permute-start(bf16[1,24,256]{2,1,0:T(8,128)(2,1)S(1)} %slice_bitcast_fusion.4), channel_id=1, source_target_pairs={{0,8},{8,16},{16,24},{24,32},{32,40},{40,48},{48,56},{1,9},{9,17},... | collective-permute-start | bytes 36872 | tf_op jit(solution)/shard_map/ppermute | solution.py:69
  5.3 1.0 shard.1
  6.3 5.1 %collective-permute-start.1 = (bf16[256,512]{1,0:T(8,128)(2,1)S(1)}, bf16[256,512]{1,0:T(8,128)(2,1)S(1)}, u32[]{:S(2)}, u32[]{:S(2)}) collective-permute-start(bf16[256,512]{1,0:T(8,128)(2,1)S(1)} %shard.1), channel_id=1, source_target_pairs={{0,416},{128,0},{256,128},{384,256},{32,384},{160,32},{288,160},{4... | collective-permute-start | bytes 786440 | tf_op jit(solution)/shard_map/ppermute | solution.py:148
  11.4 1.9 collective-permute-start.4
  13.4 2.6 %collective-permute-start.2 = (bf16[128,512]{1,0:T(8,128)(2,1)S(1)}, bf16[128,512]{1,0:T(8,128)(2,1)S(1)}, u32[]{:S(2)}, u32[]{:S(2)}) collective-permute-start(bf16[128,512]{1,0:T(8,128)(2,1)S(1)} %get-tuple-element.59), channel_id=1, source_target_pairs={{0,256},{128,384},{256,32},{384,160},{32,288},{160,416},{288,0},{4... | collective-permute-start | bytes 393224 | tf_op jit(solution)/shard_map/ppermute | solution.py:152
  16.0 4.9 %collective-permute-start.3 = (bf16[128,512]{1,0:T(8,128)(2,1)S(1)}, bf16[128,512]{1,0:T(8,128)(2,1)S(1)}, u32[]{:S(2)}, u32[]{:S(2)}) collective-permute-start(bf16[128,512]{1,0:T(8,128)(2,1)S(1)} %get-tuple-element.60), channel_id=1, source_target_pairs={{0,288},{128,416},{256,0},{384,128},{32,256},{160,384},{288,32},{4... | collective-permute-start | bytes 393224 | tf_op jit(solution)/shard_map/ppermute | solution.py:152
  21.9 4.1 %collective-permute-start.5 = (bf16[25,1,256]{2,1,0:T(2,128)(2,1)S(1)}, bf16[25,1,256]{2,1,0:T(2,128)(2,1)S(1)}, u32[]{:S(2)}, u32[]{:S(2)}) collective-permute-start(bf16[25,1,256]{2,1,0:T(2,128)(2,1)S(1)} %pad_maximum_fusion.5), channel_id=1, source_target_pairs={{0,1},{1,2},{2,3},{3,4},{4,5},{5,6},{6,7},{8,9},{9,10},{10,11},{11... | collective-permute-start | bytes 38408 | tf_op jit(solution)/shard_map/ppermute | solution.py:73
  26.0 2.3 %collective-permute-done.3 = bf16[128,512]{1,0:T(8,128)(2,1)S(1)} collective-permute-done((bf16[128,512]{1,0:T(8,128)(2,1)S(1)}, bf16[128,512]{1,0:T(8,128)(2,1)S(1)}, u32[]{:S(2)}, u32[]{:S(2)}) %collective-permute-start.3) | collective-permute-done | bytes 131104 | tf_op jit(solution)/shard_map/ppermute | solution.py:152
  28.5 3.3 %collective-permute-start.6 = (bf16[4,256,512]{2,1,0:T(8,128)(2,1)S(1)}, bf16[4,256,512]{2,1,0:T(8,128)(2,1)S(1)}, u32[]{:S(2)}, u32[]{:S(2)}) collective-permute-start(bf16[4,256,512]{2,1,0:T(8,128)(2,1)S(1)} %pad_maximum_fusion.1.ring_ref), channel_id=1, source_target_pairs={{0,64},{64,0},{1,65},{65,1},{2,66},{66,2},{3,67},{67,3},{4,68},{68... | collective-permute-start | bytes 3145736 | tf_op jit(solution)/shard_map/ppermute | solution.py:92
  32.7 4.7 %expand.1 = (bf16[2,192,1024]{2,1,0:T(8,128)(2,1)}, bf16[2,208,1024]{2,1,0:T(8,128)(2,1)}, bf16[4,192,1024]{2,1,0:T(8,128)(2,1)}, bf16[192,1024]{1,0:T(8,128)(2,...) custom-call(bf16[24,24,256]{2,1,0:T(8,128)(2,1)S(1)} %bitcast.94, ...), custom_call_target="tpu_custom_call" | custom-call | flops 6000000000 | bytes 8000000 | tf_op jit(solution)/shard_map/expand/pallas_call | solution.py:331
  37.3 3.6 %section.1 = (bf16[8,144,128]{2,1,0:T(8,128)(2,1)}, bf16[192,512]{1,0:T(8,128)(2,1)}, bf16[192,512]{1,0:T(8,128)(2,1)}, bf16[1024,512]{1,0:T(8,128)(2,1)}, bf16[...) custom-call(s32[2]{0:T(128)S(1)} %pad_add_fusion.spot_ref, bf16[4,256,512]{2,1,0:T(8,128)(2,1)S(1)} %pad_maximum_fusion.1.ring_ref, ...), custom_call_target="tpu_custom_call" | custom-call | flops 4000000000 | bytes 8000000 | tf_op jit(solution)/shard_map/section/pallas_call | solution.py:406
  41.0 32.9 %all_to_all.30 = bf16[64,9,2,128]{3,2,1,0:T(2,128)(2,1)} all-to-all(bf16[64,9,2,128]{3,2,1,0:T(2,128)(2,1)} %bitcast.105), channel_id=1, replica_groups=mesh['ylo'=4,'core'=2,'yhi'=2,'x'=4,'z'=8] {'yhi','x','z'}, dimensions={0} | all-to-all | bytes 589824 | tf_op jit(solution)/shard_map/all_to_all | solution.py:96
  73.9 5.0 %attention.1 = bf16[8,144,128]{2,1,0:T(8,128)(2,1)} custom-call(bf16[8,144,128]{2,1,0:T(8,128)(2,1)} %bitcast.106, bf16[576,576]{1,0:T(8,128)(2,1)} %constant.45.clone.order_ref), custom_call_target="tpu_custom_call" | custom-call | flops 6000000000 | bytes 1000000 | tf_op jit(solution)/shard_map/attention/pallas_call | solution.py:229
  78.9 7.8 %all-to-all-start.1 = ((bf16[64,9,2,128]{3,2,1,0:T(2,128)(2,1)}), bf16[64,9,2,128]{3,2,1,0:T(2,128)(2,1)S(1)}, u32[]{:S(2)}, u32[]{:S(2)}) async-start(bf16[64,9,2,128]{3,2,1,0:T(2,128)(2,1)} %bitcast.104), calls=%async_computation.1 | async-start | bytes 589824 | tf_op jit(solution)/shard_map/all_to_all | solution.py:96
  86.7 14.5 %all-to-all-done.1 = bf16[64,9,2,128]{3,2,1,0:T(2,128)(2,1)S(1)} async-done(((bf16[64,9,2,128]{3,2,1,0:T(2,128)(2,1)}), bf16[64,9,2,128]{3,2,1,0:T(2,128)(2,1)S(1)}, u32[]{:S(2)}, u32[]{:S(2)}) %all-to-all-start.1) | async-done | bytes 294944 | tf_op jit(solution)/shard_map/all_to_all | solution.py:96
  101.2 2.5 %back.1 = (bf16[192,1024]{1,0:T(8,128)(2,1)S(1)}, bf16[192,512]{1,0:T(8,128)(2,1)S(1)}, bf16[192,1024]{1,0:T(8,128)(2,1)S(1)}) custom-call(bf16[8,144,128]{2,1,0:T(8,128)(2,1)S(1)} %bitcast.87, bf16[144,192]{1,0:T(8,128)(2,1)S(1)} %copy-done.4, bf16[192,512]{1,0:T(8,128)(2,1)S(1)} %copy-done.6, bf16[192,512]{1,0:T(8,128)(2,1)S(1)} %bitcast.90, ...), custom_call_target="tpu_custom_call" | custom-call | flops 1500000000 | bytes 8000000 | tf_op jit(solution)/shard_map/back/pallas_call | solution.py:460
  103.8 1.3 collective-permute-start.8
  105.1 1.3 collective-permute-start.9
  106.4 1.3 collective-permute-start.7
  107.7 2.0 parts.1
  109.8 4.4 %collective-permute-start.10 = (bf16[32,144,128]{2,1,0:T(8,128)(2,1)S(1)}, bf16[32,144,128]{2,1,0:T(8,128)(2,1)S(1)}, u32[]{:S(2)}, u32[]{:S(2)}) collective-permute-start(bf16[32,144,128]{2,1,0:T(8,128)(2,1)S(1)} %dynamic-slice_bitcast_fusion), channel_id=1, source_target_pairs={{0,64},{64,0},{1,65},{65,1},{2,66},{66,2},{3,67},{67,3},{4,68},{68... | collective-permute-start | bytes 3538952 | tf_op jit(solution)/shard_map/ppermute | solution.py:92
  114.3 1.8 pixel.1
  116.3 2.1 collective-permute-start.11
  118.3 1.5 collective-permute-done.11
  120.3 27.8 %all_to_all.31 = bf16[32,184,128]{2,1,0:T(8,128)(2,1)S(1)} all-to-all(bf16[32,184,128]{2,1,0:T(8,128)(2,1)S(1)} %pad_maximum_fusion), channel_id=1, replica_groups=mesh['ylo'=4,'core'=2,'yhi'=2,'x'=4,'z'=8] {'x'}, dimensions={0} | all-to-all | bytes 3014656 | tf_op jit(solution)/shard_map/all_to_all | solution.py:96
  148.4 18.1 %all_to_all.32 = bf16[8,184,128]{2,1,0:T(8,128)(2,1)S(1)} all-to-all(bf16[8,184,128]{2,1,0:T(8,128)(2,1)S(1)} %reduce_sum.33), channel_id=1, replica_groups=mesh['ylo'=4,'core'=2,'yhi'=2,'x'=4,'z'=8] {'z'}, dimensions={0} | all-to-all | bytes 753664 | tf_op jit(solution)/shard_map/all_to_all | solution.py:96
  166.6 12.6 %all_to_all.33 = bf16[8,88,128]{2,1,0:T(8,128)(2,1)S(1)} all-to-all(bf16[8,88,128]{2,1,0:T(8,128)(2,1)S(1)} %bitcast.99), channel_id=1, replica_groups=mesh['ylo'=4,'core'=2,'yhi'=2,'x'=4,'z'=8] {'ylo','yhi'}, dimensions={0} | all-to-all | bytes 360448 | tf_op jit(solution)/shard_map/all_to_all | solution.py:96
  179.3 1.0 broadcast_in_dim.26
  180.3 4.5 %all-to-all-start.5 = ((bf16[32,88,128]{2,1,0:T(8,128)(2,1)}), bf16[32,88,128]{2,1,0:T(8,128)(2,1)S(1)}, u32[]{:S(2)}, u32[]{:S(2)}) async-start(bf16[32,88,128]{2,1,0:T(8,128)(2,1)} %broadcast_in_dim.26), calls=%async_computation.5 | async-start | bytes 1441792 | tf_op jit(solution)/shard_map/all_to_all | solution.py:96
  185.9 13.6 %all-to-all-done.5 = bf16[32,88,128]{2,1,0:T(8,128)(2,1)S(1)} async-done(((bf16[32,88,128]{2,1,0:T(8,128)(2,1)}), bf16[32,88,128]{2,1,0:T(8,128)(2,1)S(1)}, u32[]{:S(2)}, u32[]{:S(2)}) %all-to-all-start.5) | async-done | bytes 720928 | tf_op jit(solution)/shard_map/all_to_all | solution.py:96
  199.6 9.6 %collective-permute-start.12 = (bf16[32,56,128]{2,1,0:T(8,128)(2,1)S(1)}, bf16[32,56,128]{2,1,0:T(8,128)(2,1)S(1)}, u32[]{:S(2)}, u32[]{:S(2)}) collective-permute-start(bf16[32,56,128]{2,1,0:T(8,128)(2,1)S(1)} %get-tuple-element.56), channel_id=1, source_target_pairs={{0,64},{64,0},{1,65},{65,1},{2,66},{66,2},{3,67},{67,3},{4,68},{68... | collective-permute-start | bytes 1376264 | tf_op jit(solution)/shard_map/ppermute | solution.py:92
  211.9 1.1 copy.31
  (93 shorter events, 9.5 us)
Async XLA Ops:
  1.3 12.0 %collective-permute-start = (bf16[1,24,256]{2,1,0:T(8,128)(2,1)S(1)}, bf16[1,24,256]{2,1,0:T(8,128)(2,1)S(1)}, u32[]{:S(2)}, u32[]{:S(2)}) collective-permute-start(bf16[1,24,256]{2,1,0:T(8,128)(2,1)S(1)} %slice_bitcast_fusion.4), channel_id=1, source_target_pairs={{0,8},{8,16},{16,24},{24,32},{32,40},{40,48},{48,56},{1,9},{9,17},... | collective-permute-start | bytes 36872 | tf_op jit(solution)/shard_map/ppermute | solution.py:69
  6.3 25.6 %copy-start.12 = (bf16[3,3,1024]{2,1,0:T(4,128)(2,1)S(1)}, bf16[3,3,1024]{2,1,0:T(4,128)(2,1)}, u32[]{:S(2)}) copy-start(bf16[3,3,1024]{2,1,0:T(4,128)(2,1)} %param.12) | copy-start | bytes 55300
  6.3 22.1 %collective-permute-start.1 = (bf16[256,512]{1,0:T(8,128)(2,1)S(1)}, bf16[256,512]{1,0:T(8,128)(2,1)S(1)}, u32[]{:S(2)}, u32[]{:S(2)}) collective-permute-start(bf16[256,512]{1,0:T(8,128)(2,1)S(1)} %shard.1), channel_id=1, source_target_pairs={{0,416},{128,0},{256,128},{384,256},{32,384},{160,32},{288,160},{4... | collective-permute-start | bytes 786440 | tf_op jit(solution)/shard_map/ppermute | solution.py:148
  11.4 17.0 %collective-permute-start.4 = (bf16[256,512]{1,0:T(8,128)(2,1)S(1)}, bf16[256,512]{1,0:T(8,128)(2,1)S(1)}, u32[]{:S(2)}, u32[]{:S(2)}) collective-permute-start(bf16[256,512]{1,0:T(8,128)(2,1)S(1)} %shard.1), channel_id=1, source_target_pairs={{0,128},{128,256},{256,384},{384,32},{32,160},{160,288},{288,416},... | collective-permute-start | bytes 786440 | tf_op jit(solution)/shard_map/ppermute | solution.py:147
  13.3 18.5 %copy-start.11 = (bf16[1,12,12,512]{3,2,1,0:T(8,128)(2,1)S(1)}, bf16[1,12,12,512]{3,2,1,0:T(8,128)(2,1)}, u32[]{:S(2)}) copy-start(bf16[1,12,12,512]{3,2,1,0:T(8,128)(2,1)} %param.17) | copy-start | bytes 442372
  13.4 12.7 %collective-permute-start.2 = (bf16[128,512]{1,0:T(8,128)(2,1)S(1)}, bf16[128,512]{1,0:T(8,128)(2,1)S(1)}, u32[]{:S(2)}, u32[]{:S(2)}) collective-permute-start(bf16[128,512]{1,0:T(8,128)(2,1)S(1)} %get-tuple-element.59), channel_id=1, source_target_pairs={{0,256},{128,384},{256,32},{384,160},{32,288},{160,416},{288,0},{4... | collective-permute-start | bytes 393224 | tf_op jit(solution)/shard_map/ppermute | solution.py:152
  16.0 12.4 %collective-permute-start.3 = (bf16[128,512]{1,0:T(8,128)(2,1)S(1)}, bf16[128,512]{1,0:T(8,128)(2,1)S(1)}, u32[]{:S(2)}, u32[]{:S(2)}) collective-permute-start(bf16[128,512]{1,0:T(8,128)(2,1)S(1)} %get-tuple-element.60), channel_id=1, source_target_pairs={{0,288},{128,416},{256,0},{384,128},{32,256},{160,384},{288,32},{4... | collective-permute-start | bytes 393224 | tf_op jit(solution)/shard_map/ppermute | solution.py:152
  21.9 10.8 %copy-start.1 = (bf16[1,24,24,256]{3,2,1,0:T(8,128)(2,1)S(1)}, bf16[1,24,24,256]{3,2,1,0:T(8,128)(2,1)}, u32[]{:S(2)}) copy-start(bf16[1,24,24,256]{3,2,1,0:T(8,128)(2,1)} %param.10) | copy-start | bytes 884740
  21.9 10.8 %copy-start.2 = (bf16[256,1024]{1,0:T(8,128)(2,1)S(1)}, bf16[256,1024]{1,0:T(8,128)(2,1)}, u32[]{:S(2)}) copy-start(bf16[256,1024]{1,0:T(8,128)(2,1)} %w_expand_ref.3) | copy-start | bytes 1572868
  21.9 6.6 %collective-permute-start.5 = (bf16[25,1,256]{2,1,0:T(2,128)(2,1)S(1)}, bf16[25,1,256]{2,1,0:T(2,128)(2,1)S(1)}, u32[]{:S(2)}, u32[]{:S(2)}) collective-permute-start(bf16[25,1,256]{2,1,0:T(2,128)(2,1)S(1)} %pad_maximum_fusion.5), channel_id=1, source_target_pairs={{0,1},{1,2},{2,3},{3,4},{4,5},{5,6},{6,7},{8,9},{9,10},{10,11},{11... | collective-permute-start | bytes 38408 | tf_op jit(solution)/shard_map/ppermute | solution.py:73
  28.5 8.8 %collective-permute-start.6 = (bf16[4,256,512]{2,1,0:T(8,128)(2,1)S(1)}, bf16[4,256,512]{2,1,0:T(8,128)(2,1)S(1)}, u32[]{:S(2)}, u32[]{:S(2)}) collective-permute-start(bf16[4,256,512]{2,1,0:T(8,128)(2,1)S(1)} %pad_maximum_fusion.1.ring_ref), channel_id=1, source_target_pairs={{0,64},{64,0},{1,65},{65,1},{2,66},{66,2},{3,67},{67,3},{4,68},{68... | collective-permute-start | bytes 3145736 | tf_op jit(solution)/shard_map/ppermute | solution.py:92
  32.6 4.7 %copy-start.3 = (bf16[256,512]{1,0:T(8,128)(2,1)S(1)}, bf16[256,512]{1,0:T(8,128)(2,1)}, u32[]{:S(2)}) copy-start(bf16[256,512]{1,0:T(8,128)(2,1)} %short_ref.3) | copy-start | bytes 786436
  32.6 4.7 %copy-start.4 = (bf16[144,192]{1,0:T(8,128)(2,1)S(1)}, bf16[144,192]{1,0:T(8,128)(2,1)}, u32[]{:S(2)}) copy-start(bf16[144,192]{1,0:T(8,128)(2,1)} %constant.44.clone.slots_ref) | copy-start | bytes 165892
  73.9 27.3 %copy-start = (bf16[12,16,512]{2,1,0:T(8,128)(2,1)S(1)}, bf16[12,16,512]{2,1,0:T(8,128)(2,1)}, u32[]{:S(2)}) copy-start(bf16[12,16,512]{2,1,0:T(8,128)(2,1)} %pad.12) | copy-start | bytes 589828
  73.9 27.3 %copy-start.6 = (bf16[192,512]{1,0:T(8,128)(2,1)S(1)}, bf16[192,512]{1,0:T(8,128)(2,1)}, u32[]{:S(2)}) copy-start(bf16[192,512]{1,0:T(8,128)(2,1)} %get-tuple-element.38.section_ref) | copy-start | bytes 589828
  78.9 22.3 %all-to-all-start.1 = ((bf16[64,9,2,128]{3,2,1,0:T(2,128)(2,1)}), bf16[64,9,2,128]{3,2,1,0:T(2,128)(2,1)S(1)}, u32[]{:S(2)}, u32[]{:S(2)}) async-start(bf16[64,9,2,128]{3,2,1,0:T(2,128)(2,1)} %bitcast.104), calls=%async_computation.1 | async-start | bytes 589824 | tf_op jit(solution)/shard_map/all_to_all | solution.py:96
  101.2 6.5 %copy-start.5 = (bf16[192,512]{1,0:T(8,128)(2,1)S(1)}, bf16[192,512]{1,0:T(8,128)(2,1)}, u32[]{:S(2)}) copy-start(bf16[192,512]{1,0:T(8,128)(2,1)} %get-tuple-element.49.normed_ref) | copy-start | bytes 589828
  103.8 10.4 %collective-permute-start.8 = (bf16[12,1,1024]{2,1,0:T(2,128)(2,1)S(1)}, bf16[12,1,1024]{2,1,0:T(2,128)(2,1)S(1)}, u32[]{:S(2)}, u32[]{:S(2)}) collective-permute-start(bf16[12,1,1024]{2,1,0:T(2,128)(2,1)S(1)} %slice.90), channel_id=1, source_target_pairs={{1,0},{2,1},{3,2},{4,3},{5,4},{6,5},{7,6},{9,8},{10,9},{11,10},{12... | collective-permute-start | bytes 73736 | tf_op jit(solution)/shard_map/ppermute | solution.py:73
  105.1 9.1 %collective-permute-start.9 = (bf16[1,1,1024]{2,1,0:T(2,128)(2,1)S(1)}, bf16[1,1,1024]{2,1,0:T(2,128)(2,1)S(1)}, u32[]{:S(2)}, u32[]{:S(2)}) collective-permute-start(bf16[1,1,1024]{2,1,0:T(2,128)(2,1)S(1)} %slice.91), channel_id=1, source_target_pairs={{9,0},{10,1},{11,2},{12,3},{13,4},{14,5},{15,6},{17,8},{18,9},{19,... | collective-permute-start | bytes 6152 | tf_op jit(solution)/shard_map/ppermute | solution.py:83
  106.4 7.8 %collective-permute-start.7 = (bf16[1,12,1024]{2,1,0:T(8,128)(2,1)S(1)}, bf16[1,12,1024]{2,1,0:T(8,128)(2,1)S(1)}, u32[]{:S(2)}, u32[]{:S(2)}) collective-permute-start(bf16[1,12,1024]{2,1,0:T(8,128)(2,1)S(1)} %slice_bitcast_fusion.3), channel_id=1, source_target_pairs={{8,0},{16,8},{24,16},{32,24},{40,32},{48,40},{56,48},{9,1},{17,9},... | collective-permute-start | bytes 73736 | tf_op jit(solution)/shard_map/ppermute | solution.py:69
  107.7 6.6 %copy-start.9 = (bf16[2,192,1024]{2,1,0:T(8,128)(2,1)S(1)}, bf16[2,192,1024]{2,1,0:T(8,128)(2,1)}, u32[]{:S(2)}) copy-start(bf16[2,192,1024]{2,1,0:T(8,128)(2,1)} %get-tuple-element.43.even_ref) | copy-start | bytes 2359300
  107.7 6.6 %copy-start.10 = (bf16[4,192,256]{2,1,0:T(8,128)(2,1)S(1)}, bf16[4,192,256]{2,1,0:T(8,128)(2,1)}, u32[]{:S(2)}) copy-start(bf16[4,192,256]{2,1,0:T(8,128)(2,1)} %get-tuple-element.46.cells_ref) | copy-start | bytes 1179652
  109.6 4.6 %copy-start.7 = (bf16[4,192,1024]{2,1,0:T(8,128)(2,1)S(1)}, bf16[4,192,1024]{2,1,0:T(8,128)(2,1)}, u32[]{:S(2)}) copy-start(bf16[4,192,1024]{2,1,0:T(8,128)(2,1)} %get-tuple-element.45.slopes_ref) | copy-start | bytes 4718596
  109.7 4.6 %copy-start.8 = (bf16[2,208,1024]{2,1,0:T(8,128)(2,1)S(1)}, bf16[2,208,1024]{2,1,0:T(8,128)(2,1)}, u32[]{:S(2)}) copy-start(bf16[2,208,1024]{2,1,0:T(8,128)(2,1)} %get-tuple-element.44.odd_ref) | copy-start | bytes 2555908
  109.8 10.1 %collective-permute-start.10 = (bf16[32,144,128]{2,1,0:T(8,128)(2,1)S(1)}, bf16[32,144,128]{2,1,0:T(8,128)(2,1)S(1)}, u32[]{:S(2)}, u32[]{:S(2)}) collective-permute-start(bf16[32,144,128]{2,1,0:T(8,128)(2,1)S(1)} %dynamic-slice_bitcast_fusion), channel_id=1, source_target_pairs={{0,64},{64,0},{1,65},{65,1},{2,66},{66,2},{3,67},{67,3},{4,68},{68... | collective-permute-start | bytes 3538952 | tf_op jit(solution)/shard_map/ppermute | solution.py:92
  116.3 3.5 %collective-permute-start.11 = (bf16[32,40,128]{2,1,0:T(8,128)(2,1)S(1)}, bf16[32,40,128]{2,1,0:T(8,128)(2,1)S(1)}, u32[]{:S(2)}, u32[]{:S(2)}) collective-permute-start(bf16[32,40,128]{2,1,0:T(8,128)(2,1)S(1)} %pad_maximum_fusion.2), channel_id=1, source_target_pairs={{0,64},{64,0},{1,65},{65,1},{2,66},{66,2},{3,67},{67,3},{4,68},{68... | collective-permute-start | bytes 983048 | tf_op jit(solution)/shard_map/ppermute | solution.py:92
  180.3 19.3 %all-to-all-start.5 = ((bf16[32,88,128]{2,1,0:T(8,128)(2,1)}), bf16[32,88,128]{2,1,0:T(8,128)(2,1)S(1)}, u32[]{:S(2)}, u32[]{:S(2)}) async-start(bf16[32,88,128]{2,1,0:T(8,128)(2,1)} %broadcast_in_dim.26), calls=%async_computation.5 | async-start | bytes 1441792 | tf_op jit(solution)/shard_map/all_to_all | solution.py:96
  199.6 12.0 %collective-permute-start.12 = (bf16[32,56,128]{2,1,0:T(8,128)(2,1)S(1)}, bf16[32,56,128]{2,1,0:T(8,128)(2,1)S(1)}, u32[]{:S(2)}, u32[]{:S(2)}) collective-permute-start(bf16[32,56,128]{2,1,0:T(8,128)(2,1)S(1)} %get-tuple-element.56), channel_id=1, source_target_pairs={{0,64},{64,0},{1,65},{65,1},{2,66},{66,2},{3,67},{67,3},{4,68},{68... | collective-permute-start | bytes 1376264 | tf_op jit(solution)/shard_map/ppermute | solution.py:92
